TPU v7x, 32 devices: a whole 2x2x4 slice. The times are simulated.
32 devices in a mesh: row: 4 (over y, core), col: 8 (over z, x).
Axes of the slice: x: 2, y: 2, z: 4, core: 2. Of those that a mesh axis runs over, the one named last changes fastest.
Arguments:
- prompt_token_states: bfloat16 [896, 5120], P('col', 'row'), may hold values from -960 to 960
- gain: bfloat16 [5120], P('row'), may hold values from 0.25 to 1.75
- projection_weight: bfloat16 [5120, 2, 5120], P('col', None, 'row'), may hold values from -0.078125 to 0.078125
- adapter_down_maps: bfloat16 [8, 5120, 256], P('col', 'row'), may hold values from -0.078125 to 0.078125
- adapter_up_maps: bfloat16 [8, 2, 128, 5120], P('col', None, None, 'row'), may hold values from -0.5 to 0.5
- prompt_token_length: int32 [12], replicated, may hold values from 1 to 134, 896 in all
- prompt_of_request: int32 [144], replicated, may hold values from 0 to 11, never falling along the last dimension, each value on 1 to 16 neighbouring positions
- adapter_of_request: int32 [144], replicated, may hold values from 0 to 31, as said below
- adapter_slot_index: int32 [32], replicated, may hold values from -1 to 7, as said below
Outputs:
- query_rows: bfloat16 [896, 16, 5120], P('col', None, 'row')
- value_rows: bfloat16 [896, 16, 5120], P('col', None, 'row')
Inputs may be any that keep to these rules, and one draw needn't show every extreme that they name: `adapter_of_request`: every request names a loaded adapter (adapter_slot_index not -1), and every slot 0 to 7 is named by some request. `adapter_slot_index`: the values other than -1 are 0 to 7, each once; the others are -1. `prompt_of_request`: requests of one prompt stand together, prompts in rising order; each prompt has 1 to 16 requests.
All inputs are finite; a program needn't handle non-finite values.
Results may differ from a plain program's by a relative error of at most 0.0057.
Values may be sent and summed in bfloat16 or wider, within the bound.
No kernel may reach another device: no remote copies, remote signals or barrier semaphores. Data moves between devices by JAX's collectives and lax.ppermute only.
A program may use at most 128 MiB of HBM per device.

v0:
```python
import jax
import jax.numpy as jnp
from jax import lax
from jax.sharding import PartitionSpec as P

SLOTS = 16


def request_table(
    prompt_of_request, adapter_of_request, adapter_slot_index, prompts, slots, loaded_adapters
):
    n_req = prompt_of_request.shape[0]
    before = jnp.sum(
        (prompt_of_request[None, :] < prompt_of_request[:, None]).astype(jnp.int32), axis=1
    )
    position = jnp.arange(n_req, dtype=jnp.int32) - before
    adapter_hot = (
        adapter_of_request[:, None]
        == jnp.arange(adapter_slot_index.shape[0], dtype=jnp.int32)[None, :]
    )
    slot_index = jnp.sum(jnp.where(adapter_hot, adapter_slot_index[None, :], 0), axis=1)
    prompt_hot = (
        prompt_of_request[:, None] == jnp.arange(prompts, dtype=jnp.int32)[None, :]
    ).astype(jnp.float32)
    place_hot = (position[:, None] == jnp.arange(slots, dtype=jnp.int32)[None, :]).astype(
        jnp.float32
    )
    slot_hot = (
        slot_index[:, None] == jnp.arange(loaded_adapters, dtype=jnp.int32)[None, :]
    ).astype(jnp.float32)
    paired = (place_hot[:, :, None] * slot_hot[:, None, :]).reshape(n_req, slots * loaded_adapters)
    return jnp.dot(prompt_hot.T, paired, precision=lax.Precision.HIGHEST)


def body(
    prompt_token_states,
    gain,
    projection_weight,
    adapter_down_maps,
    adapter_up_maps,
    prompt_token_length,
    prompt_of_request,
    adapter_of_request,
    adapter_slot_index,
):
    column_count = lax.axis_size("col")
    col_place = lax.axis_index("col")
    tok_rows = prompt_token_states.shape[0]
    hidden_width = prompt_token_states.shape[1]
    low_rank_width = adapter_down_maps.shape[2] // 2
    loaded_adapters = adapter_down_maps.shape[0] * column_count
    prompts = prompt_token_length.shape[0]
    states = prompt_token_states.astype(jnp.float32)
    square_sum = lax.psum(jnp.sum(states * states, axis=1), "row")
    scale_rows = lax.rsqrt(square_sum / (hidden_width * lax.axis_size("row")) + 1e-05)
    normalized_states = (states * scale_rows[:, None] * gain.astype(jnp.float32)[None, :]).astype(
        jnp.bfloat16
    )
    full_rows = lax.all_gather(normalized_states, "row", axis=1, tiled=True)
    weight_flat = projection_weight.reshape(projection_weight.shape[0], 2 * hidden_width)
    column_block = lax.all_to_all(full_rows, "col", split_axis=1, concat_axis=0, tiled=True)
    base = lax.psum_scatter(
        jnp.dot(column_block, weight_flat, preferred_element_type=jnp.float32),
        "col",
        scatter_dimension=0,
        tiled=True,
    )
    partial_rank = jnp.einsum(
        "bf,lfm->blm",
        lax.all_gather(normalized_states, "col", axis=0, tiled=True),
        adapter_down_maps,
        preferred_element_type=jnp.float32,
    )
    low_rank_rows = lax.psum(partial_rank, "row").astype(jnp.bfloat16)
    every_token_row = low_rank_rows.shape[0]
    rank_split_parts = low_rank_rows.reshape(
        every_token_row, adapter_down_maps.shape[0], 2, low_rank_width
    )
    adapter_correction = jnp.einsum(
        "pqsm,qsmn->pqsn", rank_split_parts, adapter_up_maps, preferred_element_type=jnp.float32
    )
    adapter_correction = adapter_correction.reshape(
        every_token_row, adapter_down_maps.shape[0], 2 * hidden_width
    ).astype(jnp.bfloat16)
    delta = lax.all_to_all(adapter_correction, "col", split_axis=0, concat_axis=1, tiled=True)
    table = request_table(
        prompt_of_request, adapter_of_request, adapter_slot_index, prompts, SLOTS, loaded_adapters
    )
    ends = jnp.cumsum(prompt_token_length)
    token_index = col_place * tok_rows + jnp.arange(tok_rows, dtype=jnp.int32)
    prompt_of = jnp.sum((token_index[:, None] >= ends[None, :]).astype(jnp.int32), axis=1)
    prompt_hot = (prompt_of[:, None] == jnp.arange(prompts, dtype=jnp.int32)[None, :]).astype(
        jnp.bfloat16
    )
    pick = jnp.dot(prompt_hot, table.astype(jnp.bfloat16), preferred_element_type=jnp.float32)
    pick = pick.reshape(tok_rows, SLOTS, loaded_adapters)
    live = jnp.sum(pick, axis=2)
    chosen = jnp.einsum(
        "tka,taf->tkf", pick.astype(jnp.bfloat16), delta, preferred_element_type=jnp.float32
    )
    mixed = (live[:, :, None] * base[:, None, :] + chosen).astype(jnp.bfloat16)
    return (mixed[:, :, :hidden_width], mixed[:, :, hidden_width:])


def solution(mesh):
    placed = (
        P("col", "row"),
        P("row"),
        P("col", None, "row"),
        P("col", "row", None),
        P("col", None, None, "row"),
        P(),
        P(),
        P(),
        P(),
    )
    return jax.shard_map(
        body,
        mesh=mesh,
        in_specs=placed,
        out_specs=(P("col", None, "row"), P("col", None, "row")),
        check_vma=False,
    )
```

profile of v0, /device:TPU:0, one launch (start us, length us, event | category | flops | bytes accessed | tf_op | source)
XLA Modules:
  0.0 359.1 jit_solution(8952035884761519594)
XLA Ops:
  7.2 0.0 copy-start
  7.2 0.0 all-gather.3.cloned.1.call-start
  7.2 0.7 convert_element_type.72
  8.0 1.1 fusion.5
  9.1 8.4 %psum.14 = f32[112]{0:T(128)S(1)} all-reduce(f32[112]{0:T(128)S(1)} %fusion.5), channel_id=1, replica_groups=mesh['row'=4,'col'=8] {'row'}, use_global_device_ids=true, to_apply=%region_6.7 | all-reduce | flops 112 | bytes 896 | tf_op jit(solution)/shard_map/psum | solution.py:54
  17.5 1.8 fusion.7
  19.3 0.0 all-gather.3.cloned.1.call-update
  19.3 0.0 all-gather.5.cloned.1.call-start
  19.3 0.7 all-gather.5.cloned.1.call-update
  20.0 17.0 %all-gather.3.cloned.1.call-done = bf16[112,5120]{1,0:T(8,128)(2,1)} async-done(((bf16[112,1280]{1,0:T(8,128)(2,1)}), bf16[112,5120]{1,0:T(8,128)(2,1)}) %all-gather.3.cloned.1.call-update) | async-done | bytes 1146896 | tf_op jit(solution)/shard_map/all_gather | solution.py:59
  37.0 2.4 copy.53
  39.4 5.5 %all-to-all-start = ((bf16[112,8,640]{2,0,1:T(8,128)(2,1)}), bf16[112,8,640]{2,0,1:T(8,128)(2,1)S(1)}, u32[]{:S(2)}, u32[]{:S(2)}) async-start(bf16[112,8,640]{2,0,1:T(8,128)(2,1)} %bitcast.43), calls=%async_computation | async-start | bytes 2293760 | tf_op jit(solution)/shard_map/all_to_all | solution.py:61
  44.9 0.0 reduce-scatter.2.cloned.1.call-start
  44.9 4.3 %copy.45 = bf16[80,8,2,1280]{3,1,2,0:T(8,128)(2,1)} copy(bf16[80,8,2,1280]{3,2,1,0:T(2,128)(2,1)} %bitcast.46) | data formatting | bytes 6553600
  49.2 33.2 %all-to-all-done = bf16[112,8,640]{2,0,1:T(8,128)(2,1)S(1)} async-done(((bf16[112,8,640]{2,0,1:T(8,128)(2,1)}), bf16[112,8,640]{2,0,1:T(8,128)(2,1)S(1)}, u32[]{:S(2)}, u32[]{:S(2)}) %all-to-all-start) | async-done | bytes 1146912 | tf_op jit(solution)/shard_map/all_to_all | solution.py:61
  82.4 8.0 %fusion.21 = f32[896,2560]{1,0:T(8,128)} fusion(bf16[896,640]{1,0:T(8,128)(2,1)S(1)} %bitcast.49, bf16[640,2560]{1,0:T(8,128)(2,1)} %bitcast.47), kind=kOutput, calls=%fused_computation.39 | convolution fusion | flops 2936012800 | bytes 13598720 | tf_op jit(solution)/shard_map/dot_general | solution.py:63
  90.4 0.0 reduce-scatter.2.cloned.1.call-update
  90.4 13.9 %all-gather.5.cloned.1.call-done = bf16[896,1280]{1,0:T(8,128)(2,1)} async-done(((bf16[112,1280]{1,0:T(8,128)(2,1)}), bf16[896,1280]{1,0:T(8,128)(2,1)}) %all-gather.5.cloned.1.call-update) | async-done | bytes 2293776 | tf_op jit(solution)/shard_map/all_gather | solution.py:70
  104.3 0.0 copy-done.5
  104.3 2.4 convolution_bitcast_fusion
  106.7 20.7 %all-reduce.1 = bf16[896,1,256]{2,0,1:T(8,128)(2,1)S(1)} all-reduce(f32[896,1,256]{2,0,1:T(8,128)S(1)} %convolution_bitcast_fusion), channel_id=1, replica_groups=mesh['row'=4,'col'=8] {'row'}, use_global_device_ids=true, to_apply=%region_8.9 | all-reduce | flops 229376 | bytes 1376256 | tf_op jit(solution)/shard_map/psum | solution.py:74
  127.4 0.1 reshape.132
  127.5 0.0 copy-done
  127.6 3.5 fusion.2
  131.0 7.2 %copy.38 = bf16[896,1,2,1280]{0,3,2,1:T(8,128)(2,1)} copy(bf16[896,1,2,1280]{3,0,2,1:T(8,128)(2,1)} %fusion.2) | data formatting | bytes 9175040 | tf_op jit(solution)/shard_map/convert_element_type | solution.py:84
  138.3 0.5 broadcast.38
  138.8 7.1 %reduce = bf16[896,2560]{0,1:T(8,128)(2,1)} reduce(bf16[896,1,2560]{0,2,1:T(8,128)(2,1)} %bitcast.44, bf16[]{:T(256)} %broadcast.38), dimensions={1}, to_apply=%copy.39.reduce_sub_computation | reduce | bytes 9175042 | tf_op jit(solution)/shard_map/convert_element_type | solution.py:84
  145.9 7.8 %copy.54 = bf16[896,2560]{1,0:T(8,128)(2,1)} copy(bf16[896,2560]{0,1:T(8,128)(2,1)} %reduce) | data formatting | bytes 9175040
  153.6 8.1 %reshape.134 = bf16[8,2,143360]{2,1,0:T(2,128)(2,1)} reshape(bf16[896,2560]{1,0:T(8,128)(2,1)} %copy.54) | data formatting | bytes 9175040
  161.7 4.9 %all-to-all-start.1 = ((bf16[8,2,143360]{2,1,0:T(2,128)(2,1)}), bf16[8,2,143360]{2,1,0:T(2,128)(2,1)}, u32[]{:S(2)}, u32[]{:S(2)}) async-start(bf16[8,2,143360]{2,1,0:T(2,128)(2,1)} %reshape.134), calls=%async_computation.2 | async-start | bytes 9175040 | tf_op jit(solution)/shard_map/all_to_all | solution.py:85
  166.7 0.0 copy-done.6
  166.7 0.2 reduce-window.8
  166.9 0.1 convert_reduce_fusion.1
  167.0 0.0 copy-done.3
  167.0 0.0 copy-done.4
  167.0 0.1 select_reduce_fusion
  167.1 0.2 convert_reduce_fusion
  167.3 0.2 convolution_convert_fusion.1
  167.5 0.3 fusion.20
  167.9 0.2 copy.41
  168.0 0.1 copy.35
  168.1 121.4 %all-to-all-done.1 = bf16[8,2,143360]{2,1,0:T(2,128)(2,1)} async-done(((bf16[8,2,143360]{2,1,0:T(2,128)(2,1)}), bf16[8,2,143360]{2,1,0:T(2,128)(2,1)}, u32[]{:S(2)}, u32[]{:S(2)}) %all-to-all-start.1) | async-done | bytes 4587552 | tf_op jit(solution)/shard_map/all_to_all | solution.py:85
  289.5 9.1 %reshape.135 = bf16[896,1,2560]{2,1,0:T(2,128)(2,1)} reshape(bf16[8,2,143360]{2,1,0:T(2,128)(2,1)} %all-to-all-done.1) | data formatting | bytes 9175040
  298.6 7.6 %copy.43 = bf16[896,1,2560]{2,0,1:T(8,128)(2,1)} copy(bf16[896,1,2560]{2,1,0:T(2,128)(2,1)} %reshape.135) | data formatting | bytes 9175040
  306.2 34.8 %reduce-scatter.2.cloned.1.call-done = f32[112,2560]{1,0:T(8,128)} async-done(((f32[896,2560]{1,0:T(8,128)}), f32[112,2560]{1,0:T(8,128)}) %reduce-scatter.2.cloned.1.call-update) | async-done | bytes 1146896 | tf_op jit(solution)/shard_map/reduce_scatter | solution.py:62
  341.0 7.2 %add_convert_fusion = bf16[112,16,2560]{2,1,0:T(8,128)(2,1)S(1)} fusion(bf16[112,16,8]{1,2,0:T(8,128)(2,1)S(1)} %copy.41, f32[112,2560]{1,0:T(8,128)} %reduce-scatter.2.cloned.1.call-done, f32[112,16]{1,0:T(8,128)S(1)} %copy.35, bf16[8,112,1,2560]{3,1,0,2:T(8,128)(2,1)} %bitcast.45), kind=kOutput, calls=%fused_computation | convolution fusion | flops 87162880 | bytes 14945280 | tf_op jit(solution)/shard_map/tka,taf->tkf/dot_general | solution.py:98
  348.2 0.0 copy-start.1
  348.2 4.4 %fusion.19 = (bf16[112,16,1280]{2,1,0:T(8,128)(2,1)}, bf16[112,16,1280]{2,1,0:T(8,128)(2,1)}) fusion(bf16[112,16,2560]{2,1,0:T(8,128)(2,1)S(1)} %add_convert_fusion), kind=kLoop, calls=%fused_computation.37 | loop fusion | bytes 18350080 | tf_op jit(solution)/shard_map/slice | solution.py:102
  (12 shorter events, 0.0 us)
Async XLA Ops:
  7.2 120.4 %copy-start = (bf16[1,2,128,1280]{3,2,1,0:T(8,128)(2,1)S(1)}, bf16[1,2,128,1280]{3,2,1,0:T(8,128)(2,1)}, u32[]{:S(2)}) copy-start(bf16[1,2,128,1280]{3,2,1,0:T(8,128)(2,1)} %param.13) | copy-start | bytes 1966084
  7.2 29.8 %all-gather.3.cloned.1.call-start = ((), (), s32[]{:S(2)}) async-start(), calls=%async_computation.3 | async-start | bytes 1433600 | tf_op jit(solution)/shard_map/all_gather | solution.py:59
  19.3 85.0 %all-gather.5.cloned.1.call-start = ((), (), s32[]{:S(2)}) async-start(), calls=%async_computation.5 | async-start | bytes 2580480 | tf_op jit(solution)/shard_map/all_gather | solution.py:70
  39.4 43.0 %all-to-all-start = ((bf16[112,8,640]{2,0,1:T(8,128)(2,1)}), bf16[112,8,640]{2,0,1:T(8,128)(2,1)S(1)}, u32[]{:S(2)}, u32[]{:S(2)}) async-start(bf16[112,8,640]{2,0,1:T(8,128)(2,1)} %bitcast.43), calls=%async_computation | async-start | bytes 2293760 | tf_op jit(solution)/shard_map/all_to_all | solution.py:61
  44.9 296.1 %reduce-scatter.2.cloned.1.call-start = ((), (), s32[]{:S(2)}) async-start(), calls=%async_computation.4 | async-start | bytes 10321920 | tf_op jit(solution)/shard_map/reduce_scatter | solution.py:62
  90.4 13.9 %copy-start.5 = (bf16[1,1280,256]{2,1,0:T(8,128)(2,1)S(1)}, bf16[1,1280,256]{2,1,0:T(8,128)(2,1)}, u32[]{:S(2)}) copy-start(bf16[1,1280,256]{2,1,0:T(8,128)(2,1)} %param.12) | copy-start | bytes 1966084
  161.7 4.9 %copy-start.6 = (s32[12]{0:T(128)S(1)}, s32[12]{0:T(128)}, u32[]{:S(2)}) copy-start(s32[12]{0:T(128)} %param.14) | copy-start | bytes 148
  161.7 5.2 %copy-start.3 = (s32[144]{0:T(256)S(1)}, s32[144]{0:T(256)}, u32[]{:S(2)}) copy-start(s32[144]{0:T(256)} %param.16) | copy-start | bytes 1732
  161.7 5.2 %copy-start.4 = (s32[32]{0:T(128)S(1)}, s32[32]{0:T(128)}, u32[]{:S(2)}) copy-start(s32[32]{0:T(128)} %param.17) | copy-start | bytes 388
  161.7 5.3 %copy-start.2 = (s32[144]{0:T(256)S(1)}, s32[144]{0:T(256)}, u32[]{:S(2)}) copy-start(s32[144]{0:T(256)} %param.15) | copy-start | bytes 1732
  161.7 127.8 %all-to-all-start.1 = ((bf16[8,2,143360]{2,1,0:T(2,128)(2,1)}), bf16[8,2,143360]{2,1,0:T(2,128)(2,1)}, u32[]{:S(2)}, u32[]{:S(2)}) async-start(bf16[8,2,143360]{2,1,0:T(2,128)(2,1)} %reshape.134), calls=%async_computation.2 | async-start | bytes 9175040 | tf_op jit(solution)/shard_map/all_to_all | solution.py:85
  348.2 4.4 %copy-start.1 = (bf16[1,2,128,1280]{3,2,1,0:T(8,128)(2,1)S(1)}, bf16[1,2,128,1280]{3,2,1,0:T(8,128)(2,1)}, u32[]{:S(2)}) copy-start(bf16[1,2,128,1280]{3,2,1,0:T(8,128)(2,1)} %param.13) | copy-start | bytes 1966084
Sparse Core Ops, SparseCore 0:
  19.4 17.5 all-gather.2
  39.2 65.0 all-gather.4
  108.0 232.9 reduce-scatter.1
where the time goes:
time: 360 us; the launch traced here: 359 us
  waiting for transfers between devices  221 us (61%)
  local copies, waits for them, and re-layouts  51.8 us (14%)
  blocking collectives  29.1 us (8%)
  matrix products  21.6 us (6%)
  between operations  13.9 us (4%)
  other arithmetic  11.3 us (3%)
  starting transfers between devices  10.5 us (3%)
    all_to_all x1, waiting for transfers between devices, body(): lax.all_to_all(adapter_correction, 'col', split_axis=0, concat_axis=1, ti...  121 us
    unnamed x19, local copies, waits for them, and re-layouts  36.9 us
    reduce_scatter x1, waiting for transfers between devices, body(): lax.psum_scatter(jnp.dot(column_block, weight_flat, preferred_element_typ...  34.8 us
    all_to_all x1, waiting for transfers between devices, body(): lax.all_to_all(full_rows, 'col', split_axis=1, concat_axis=0, tiled=True)  33.2 us
    psum x1, blocking collectives, body(): low_rank_rows = lax.psum(partial_rank, 'row').astype(jnp.bfloat16)  20.7 us
    all_gather x1, waiting for transfers between devices, body(): full_rows = lax.all_gather(normalized_states, 'row', axis=1, tiled=True)  17 us
    all_gather x1, waiting for transfers between devices, body(): lax.all_gather(normalized_states, 'col', axis=0, tiled=True)  13.9 us
    psum x1, blocking collectives, body(): square_sum = lax.psum(jnp.sum(states * states, axis=1), 'row')  8.37 us
  transfers between devices with their start and end apart: 5, of which 5 were waited for; matrix products, arithmetic and copies ran while one was open for 19% of the time, Pallas kernels for 0%

commit v1 on v0

v1 whole, which is shorter than its diff:
```python
import functools

import jax
import jax.numpy as jnp
from jax import lax
from jax.experimental import pallas as pl
from jax.experimental.pallas import tpu as pltpu
from jax.sharding import PartitionSpec as P

SLOTS = 16
GROUP = 16


def mix_kernel(
    col_ref, rank_ref, up_ref, base_ref, scale_ref, pick_ref, out_ref, rows_ref, *, adapters, low_rank
):
    tokens = base_ref.shape[0]
    groups = tokens // GROUP
    used = adapters * GROUP
    col = col_ref[0]
    scale = scale_ref[...]

    @pl.when(pl.program_id(0) == 0)
    def _():
        rows_ref[:, used + 2 * GROUP :, :] = jnp.zeros_like(rows_ref[:, used + 2 * GROUP :, :])

    for a in range(adapters):
        delta = jnp.dot(
            rank_ref[lax.bitwise_xor(col, a), 0], up_ref[a, 0], preferred_element_type=jnp.float32
        )
        delta = (delta * scale).astype(jnp.bfloat16)
        for g in range(groups):
            rows_ref[g, a * GROUP : (a + 1) * GROUP, :] = delta[g * GROUP : (g + 1) * GROUP, :]
    base = base_ref[...] * scale
    high = base.astype(jnp.bfloat16)
    low = (base - high.astype(jnp.float32)).astype(jnp.bfloat16)
    for g in range(groups):
        rows_ref[g, used : used + GROUP, :] = high[g * GROUP : (g + 1) * GROUP, :]
        rows_ref[g, used + GROUP : used + 2 * GROUP, :] = low[g * GROUP : (g + 1) * GROUP, :]
    for g in range(groups):
        mixed = jnp.dot(pick_ref[g], rows_ref[g], preferred_element_type=jnp.float32)
        out_ref[g] = mixed.astype(jnp.bfloat16)


def mix(col, rank, up, base, scale, pick, half):
    adapters, _, tokens, low_rank = rank.shape
    width = up.shape[3]
    groups, rows, depth = pick.shape
    block = 256 if width % 256 == 0 else 128
    steps = width // block
    out = pl.pallas_call(
        functools.partial(mix_kernel, adapters=adapters, low_rank=low_rank),
        grid_spec=pltpu.PrefetchScalarGridSpec(
            num_scalar_prefetch=1,
            grid=(steps,),
            in_specs=[
                pl.BlockSpec((adapters, 1, tokens, low_rank), lambda i, _: (0, half, 0, 0)),
                pl.BlockSpec((adapters, 1, low_rank, block), lambda i, _: (0, half, 0, i)),
                pl.BlockSpec((tokens, block), lambda i, _: (0, half * steps + i)),
                pl.BlockSpec((tokens, 1), lambda i, _: (0, 0)),
                pl.BlockSpec((groups, rows, depth), lambda i, _: (0, 0, 0)),
            ],
            out_specs=pl.BlockSpec((groups, rows, block), lambda i, _: (0, 0, i)),
            scratch_shapes=[pltpu.VMEM((groups, depth, block), jnp.bfloat16)],
        ),
        out_shape=jax.ShapeDtypeStruct((groups, rows, width), jnp.bfloat16),
        compiler_params=pltpu.CompilerParams(vmem_limit_bytes=40 * 1024 * 1024),
        cost_estimate=pl.CostEstimate(
            flops=2 * groups * rows * depth * width,
            bytes_accessed=2 * groups * rows * width + 2 * adapters * low_rank * width,
            transcendentals=0,
        ),
    )(col, rank, up, base, scale, pick)
    return out.reshape(tokens, SLOTS, width)


def pick_matrix(
    token_index,
    prompt_token_length,
    prompt_of_request,
    adapter_of_request,
    adapter_slot_index,
    adapters,
    depth,
):
    tokens = token_index.shape[0]
    ends = jnp.cumsum(prompt_token_length)
    prompt_of = jnp.sum((token_index[:, None] >= ends[None, :]).astype(jnp.int32), axis=1)
    first = jnp.sum((prompt_of_request[None, :] < prompt_of[:, None]).astype(jnp.int32), axis=1)
    after = jnp.sum((prompt_of_request[None, :] <= prompt_of[:, None]).astype(jnp.int32), axis=1)
    hot = adapter_of_request[:, None] == jnp.arange(adapter_slot_index.shape[0], dtype=jnp.int32)[None, :]
    slot_of = jnp.sum(jnp.where(hot, adapter_slot_index[None, :], 0), axis=1)
    request = first[:, None] + jnp.arange(SLOTS, dtype=jnp.int32)[None, :]
    live = request < after[:, None]
    requests = jnp.arange(prompt_of_request.shape[0], dtype=jnp.int32)
    slot = jnp.sum(
        jnp.where(request[:, :, None] == requests[None, None, :], slot_of[None, None, :], 0), axis=2
    )
    place = (jnp.arange(tokens, dtype=jnp.int32) % GROUP)[:, None]
    column = jnp.where(live, slot * GROUP + place, -1)
    columns = jnp.arange(depth, dtype=jnp.int32)[None, None, :]
    used = adapters * GROUP
    of_base = (columns >= used) & (columns < used + 2 * GROUP) & (columns % GROUP == place[:, :, None])
    pick = (columns == column[:, :, None]) | (of_base & live[:, :, None])
    return pick.astype(jnp.bfloat16).reshape(tokens // GROUP, GROUP * SLOTS, depth)


def body(
    prompt_token_states,
    gain,
    projection_weight,
    adapter_down_maps,
    adapter_up_maps,
    prompt_token_length,
    prompt_of_request,
    adapter_of_request,
    adapter_slot_index,
):
    rows, cols = lax.axis_size("row"), lax.axis_size("col")
    row, col = lax.axis_index("row"), lax.axis_index("col")
    lines = cols // 2
    line, side = col // 2, col % 2
    tokens, width = prompt_token_states.shape
    depth_in = projection_weight.shape[0]
    low_rank = adapter_down_maps.shape[2] // 2
    adapters = cols

    def send(value, pairs):
        flat = [(a * cols + b, c * cols + d) for (a, b), (c, d) in pairs]
        return lax.ppermute(value, ("row", "col"), flat)

    every = [(r, c) for r in range(rows) for c in range(cols)]

    def to_side(value):
        return send(value, [((r, c), (r, c ^ 1)) for r, c in every])

    def to_line(value, k):
        return send(value, [((r, c), (r, c ^ (2 * k))) for r, c in every])

    def to_owner(value, k):
        return send(
            value, [((r, 2 * (r ^ k) + s), (r, 2 * r + s)) for r in range(rows) for s in range(2)]
        )

    def over_rows(value):
        bit = 2
        while bit < rows:
            got = send(
                value,
                [
                    ((c // 2 ^ e, c), (c // 2 ^ e ^ bit, c))
                    for c in range(cols)
                    for e in range(0, bit, 2)
                ],
            )
            value = jnp.where((row ^ line) & bit != 0, got, value)
            bit *= 2
        got = send(value, [((c // 2 ^ e, c), (c // 2 ^ e ^ 1, c)) for c in range(cols) for e in range(0, rows, 2)])
        return jnp.where((row ^ line) & 1 != 0, got, value)

    up = lax.all_gather(adapter_up_maps, "col", axis=0, tiled=True)

    states = prompt_token_states.astype(jnp.float32)
    gained = (states * gain.astype(jnp.float32)[None, :]).astype(jnp.bfloat16)
    mine = lax.dynamic_slice_in_dim(gained, side * depth_in, depth_in, 1)
    theirs = lax.dynamic_slice_in_dim(gained, (1 - side) * depth_in, depth_in, 1)
    block = jnp.stack([mine, to_side(theirs)])
    other_down = to_side(adapter_down_maps[0])
    blocks = [over_rows(block)] + [over_rows(to_owner(block, k)) for k in range(1, lines)]

    weight = projection_weight.reshape(depth_in, 2 * width)
    sums = []
    for k in range(lines):
        out = jnp.dot(blocks[k][1], weight, preferred_element_type=jnp.float32).astype(jnp.bfloat16)
        kept = jnp.dot(blocks[k][0], weight, preferred_element_type=jnp.float32)
        sums.append(kept + to_side(out).astype(jnp.float32))
    base = sums[0]
    for k in range(1, lines):
        base = base + to_line(sums[k].astype(jnp.bfloat16), k).astype(jnp.float32)

    gathered = jnp.concatenate([gained] + [to_line(gained, k) for k in range(1, lines)], axis=0)
    down = jnp.concatenate([adapter_down_maps[0], other_down], axis=1)
    partial = jnp.dot(gathered, down, preferred_element_type=jnp.float32)
    partial = partial.reshape(lines, tokens, 4 * low_rank)
    held = lax.dynamic_index_in_dim(partial, row ^ line, 0, keepdims=False)
    for j in range(1, rows):
        out = lax.dynamic_index_in_dim(partial, row ^ j ^ line, 0, keepdims=False)
        held = held + send(out, [((r, c), (r ^ j, c)) for r, c in every])
    held = held.astype(jnp.bfloat16)
    ranks = jnp.stack([held] + [to_owner(held, k) for k in range(1, lines)])
    ranks = over_rows(ranks)
    ranks = ranks.reshape(lines, tokens, 2, 2, low_rank).transpose(0, 2, 3, 1, 4)
    ranks = ranks.reshape(adapters, 2, tokens, low_rank)

    square_sum = lax.psum(jnp.sum(states * states, axis=1), "row")
    scale = lax.rsqrt(square_sum / (width * rows) + 1e-05)[:, None]
    depth = -(-(adapters * GROUP + 2 * GROUP) // 128) * 128
    token_index = col * tokens + jnp.arange(tokens, dtype=jnp.int32)
    pick = pick_matrix(
        token_index,
        prompt_token_length,
        prompt_of_request,
        adapter_of_request,
        adapter_slot_index,
        adapters,
        depth,
    )
    place = col.astype(jnp.int32).reshape(1)
    return tuple(mix(place, ranks, up, base, scale, pick, half) for half in range(2))


def solution(mesh):
    placed = (
        P("col", "row"),
        P("row"),
        P("col", None, "row"),
        P("col", "row", None),
        P("col", None, None, "row"),
        P(),
        P(),
        P(),
        P(),
    )
    return jax.shard_map(
        body,
        mesh=mesh,
        in_specs=placed,
        out_specs=(P("col", None, "row"), P("col", None, "row")),
        check_vma=False,
    )
```

time: 360 us -> 236 us (0.66)
  the two profiles are of different devices: /device:TPU:0 before, /device:TPU:21 now
where the time goes in v1:
time: 236 us; the launch traced here: 235 us
  starting transfers between devices  88.4 us (37%)
  waiting for transfers between devices  82.6 us (35%)
  between operations  14.6 us (6%)
  matrix products  13.7 us (6%)
  other arithmetic  11.8 us (5%)
  Pallas kernels  9.83 us (4%)
  local copies, waits for them, and re-layouts  8.97 us (4%)
  blocking collectives  5.52 us (2%)
    ppermute x31, starting transfers between devices, send(): return lax.ppermute(value, ('row', 'col'), flat)  88.3 us
    ppermute x31, waiting for transfers between devices, send(): return lax.ppermute(value, ('row', 'col'), flat)  81.9 us
    pallas_call x2, Pallas kernels, mix(): pl.pallas_call(functools.partial(mix_kernel, adapters=adapters, low_rank=...  9.83 us
    dot_general x4, matrix products, body(): kept = jnp.dot(blocks[k][0], weight, preferred_element_type=jnp.float32)  7.84 us
    unnamed x37, local copies, waits for them, and re-layouts  5.79 us
    psum x1, blocking collectives, body(): square_sum = lax.psum(jnp.sum(states * states, axis=1), 'row')  5.52 us
    select_n x5, other arithmetic, over_rows(): value = jnp.where((row ^ line) & bit != 0, got, value)  4.84 us
  transfers between devices with their start and end apart: 32, of which 9 were waited for; matrix products, arithmetic and copies ran while one was open for 13% of the time, Pallas kernels for 0%

profile of v1, /device:TPU:21, one launch (start us, length us, event | category | flops | bytes accessed | tf_op | source)
XLA Modules:
  0.0 235.4 jit_solution(1503631364755614777)
XLA Ops:
  8.6 1.8 fusion.20
  10.7 3.2 %collective-permute-start.1 = (bf16[112,1280]{1,0:T(8,128)(2,1)}, bf16[112,1280]{1,0:T(8,128)(2,1)S(1)}, u32[]{:S(2)}, u32[]{:S(2)}) collective-permute-start(bf16[112,1280]{1,0:T(8,128)(2,1)} %get-tuple-element.10), channel_id=1, source_target_pairs={{0,4},{1,5},{2,6},{3,7},{4,0},{5,1},{6,2},{7,3},{8,12},{9,13},{10,... | collective-permute-start | bytes 860168 | tf_op jit(solution)/shard_map/ppermute | solution.py:130
  13.9 1.0 dynamic-slice_bitcast_fusion.3
  15.0 1.3 collective-permute-start.12
  18.3 1.0 collective-permute-done.12
  19.3 0.8 pad_maximum_fusion.1
  20.1 1.4 collective-permute-start.13
  21.4 16.6 %collective-permute-done.2 = bf16[112,1280]{1,0:T(8,128)(2,1)S(1)} collective-permute-done((bf16[112,1280]{1,0:T(8,128)(2,1)}, bf16[112,1280]{1,0:T(8,128)(2,1)S(1)}, u32[]{:S(2)}, u32[]{:S(2)}) %collective-permute-start.2) | collective-permute-done | bytes 286752 | tf_op jit(solution)/shard_map/ppermute | solution.py:130
  38.1 1.4 collective-permute-start.21
  39.4 16.6 %collective-permute-done.1 = bf16[112,1280]{1,0:T(8,128)(2,1)S(1)} collective-permute-done((bf16[112,1280]{1,0:T(8,128)(2,1)}, bf16[112,1280]{1,0:T(8,128)(2,1)S(1)}, u32[]{:S(2)}, u32[]{:S(2)}) %collective-permute-start.1) | collective-permute-done | bytes 286752 | tf_op jit(solution)/shard_map/ppermute | solution.py:130
  56.0 7.3 %collective-permute-start.16 = (bf16[2,112,640]{2,1,0:T(8,128)(2,1)}, bf16[2,112,640]{2,1,0:T(8,128)(2,1)}, u32[]{:S(2)}, u32[]{:S(2)}) collective-permute-start(bf16[2,112,640]{2,1,0:T(8,128)(2,1)} %pad_maximum_fusion.1), channel_id=1, source_target_pairs={{2,0},{3,1},{8,10},{9,11},{22,20},{23,21},{28,30},{29,31}} | collective-permute-start | bytes 860168 | tf_op jit(solution)/shard_map/ppermute | solution.py:130
  63.4 1.4 collective-permute-start.26
  65.4 2.5 %copy.23 = bf16[80,8,2,1280]{3,1,2,0:T(8,128)(2,1)S(1)} copy(bf16[80,8,2,1280]{3,2,1,0:T(2,128)(2,1)} %bitcast.83) | data formatting | bytes 6553600
  68.0 5.5 %psum.7 = f32[112]{0:T(128)S(1)} all-reduce(f32[112]{0:T(128)S(1)} %get-tuple-element.9), channel_id=1, replica_groups=mesh['row'=4,'col'=8] {'row'}, use_global_device_ids=true, to_apply=%region_1.2 | all-reduce | flops 112 | bytes 896 | tf_op jit(solution)/shard_map/psum | solution.py:195
  73.5 1.0 broadcast_select_fusion.5
  74.5 1.3 collective-permute-start.14
  77.9 2.4 %fusion.8 = f32[448,512]{1,0:T(8,128)S(1)} fusion(bf16[1280,256]{1,0:T(8,128)(2,1)} %collective-permute-done.3, bf16[1280,256]{1,0:T(8,128)(2,1)} %bitcast.1, bf16[112,1280]{1,0:T(8,128)(2,1)} %copy-done.15, bf16[112,1280]{1,0:T(8,128)(2,1)} %copy-done.16, bf16[112,1280]{1,0:T(8,128)(2,1)} %collective-permute-done, bf16[112,1280]{1,0:T(8,128)(2,1)} %get-tuple-element.10), kind=kOutput, calls=%fused_computation.18 | convolution fusion | flops 594411520 | bytes 3375104 | tf_op jit(solution)/shard_map/dot_general | solution.py:183
  80.3 12.0 %collective-permute-start.4 = (f32[112,512]{1,0:T(8,128)S(1)}, f32[112,512]{1,0:T(8,128)S(1)}, u32[]{:S(2)}, u32[]{:S(2)}) collective-permute-start(f32[112,512]{1,0:T(8,128)S(1)} %get-tuple-element.6), channel_id=1, source_target_pairs={{0,8},{1,9},{2,10},{3,11},{4,12},{5,13},{6,14},{7,15},{8,0},{9,1},... | collective-permute-start | bytes 688136 | tf_op jit(solution)/shard_map/ppermute | solution.py:130
  92.4 1.0 broadcast_select_fusion.3
  94.0 1.5 convolution_convert_fusion.3
  95.5 1.3 collective-permute-start.23
  96.8 1.0 broadcast_select_fusion.4
  97.8 1.3 collective-permute-start.18
  99.1 1.1 collective-permute-done.6
  100.2 4.1 %collective-permute-done.5 = f32[112,512]{1,0:T(8,128)S(1)} collective-permute-done((f32[112,512]{1,0:T(8,128)S(1)}, f32[112,512]{1,0:T(8,128)S(1)}, u32[]{:S(2)}, u32[]{:S(2)}) %collective-permute-start.5) | collective-permute-done | bytes 229408 | tf_op jit(solution)/shard_map/ppermute | solution.py:130
  105.8 2.3 collective-permute-start.7
  108.1 1.0 broadcast_select_fusion.2
  109.1 1.3 collective-permute-start.28
  110.4 1.3 collective-permute-start.15
  111.7 2.4 %collective-permute-done.7 = bf16[112,512]{1,0:T(8,128)(2,1)S(1)} collective-permute-done((bf16[112,512]{1,0:T(8,128)(2,1)S(1)}, bf16[112,512]{1,0:T(8,128)(2,1)S(1)}, u32[]{:S(2)}, u32[]{:S(2)}) %collective-permute-start.7) | collective-permute-done | bytes 114720 | tf_op jit(solution)/shard_map/ppermute | solution.py:130
  115.6 1.0 collective-permute-start.19
  117.9 4.1 %collective-permute-done.28 = bf16[2,112,640]{2,1,0:T(8,128)(2,1)S(1)} collective-permute-done((bf16[2,112,640]{2,1,0:T(8,128)(2,1)S(1)}, bf16[2,112,640]{2,1,0:T(8,128)(2,1)S(1)}, u32[]{:S(2)}, u32[]{:S(2)}) %collective-permute-start.28) | collective-permute-done | bytes 286752 | tf_op jit(solution)/shard_map/ppermute | solution.py:130
  122.6 0.8 collective-permute-start.29
  124.2 0.9 broadcast_select_fusion
  125.1 1.3 collective-permute-start.11
  127.0 1.5 fusion.3
  128.6 20.8 %collective-permute-start.20 = (bf16[112,2560]{1,0:T(8,128)(2,1)}, bf16[112,2560]{1,0:T(8,128)(2,1)}, u32[]{:S(2)}, u32[]{:S(2)}) collective-permute-start(bf16[112,2560]{1,0:T(8,128)(2,1)} %fusion.3), channel_id=1, source_target_pairs={{0,2},{1,3},{2,0},{3,1},{4,6},{5,7},{6,4},{7,5},{8,10},{9,11},{10,... | collective-permute-start | bytes 1720328 | tf_op jit(solution)/shard_map/ppermute | solution.py:130
  149.4 1.5 fusion.4
  150.9 1.7 collective-permute-start.25
  152.6 1.5 fusion.5
  154.1 20.3 %collective-permute-start.30 = (bf16[112,2560]{1,0:T(8,128)(2,1)}, bf16[112,2560]{1,0:T(8,128)(2,1)}, u32[]{:S(2)}, u32[]{:S(2)}) collective-permute-start(bf16[112,2560]{1,0:T(8,128)(2,1)} %fusion.5), channel_id=1, source_target_pairs={{0,6},{1,7},{2,4},{3,5},{4,2},{5,3},{6,0},{7,1},{8,14},{9,15},{10,... | collective-permute-start | bytes 1720328 | tf_op jit(solution)/shard_map/ppermute | solution.py:130
  174.5 0.9 and.110
  176.1 1.2 broadcast_select_fusion.1
  177.5 35.4 %collective-permute-done.30 = bf16[112,2560]{1,0:T(8,128)(2,1)} collective-permute-done((bf16[112,2560]{1,0:T(8,128)(2,1)}, bf16[112,2560]{1,0:T(8,128)(2,1)}, u32[]{:S(2)}, u32[]{:S(2)}) %collective-permute-start.30) | collective-permute-done | bytes 573472 | tf_op jit(solution)/shard_map/ppermute | solution.py:130
  212.8 3.4 %fusion.2.base_ref = f32[112,2560]{1,0:T(8,128)S(1)} fusion(bf16[640,2560]{1,0:T(8,128)(2,1)} %bitcast.80, bf16[112,2560]{1,0:T(8,128)(2,1)} %collective-permute-done.30, bf16[112,2560]{1,0:T(8,128)(2,1)} %collective-permute-done.25, bf16[112,2560]{1,0:T(8,128)(2,1)} %collective-permute-done.20, bf16[112,2560]{1,0:T(8,128)(2,1)} %collective-permute-done.15, ...), kind=kOutput, calls=%fused_computation.6 | convolution fusion | flops 369295360 | bytes 6860800 | tf_op jit(solution)/shard_map/dot_general | solution.py:175
  216.2 2.5 %copy-done = bf16[8,2,128,1280]{3,2,1,0:T(8,128)(2,1)S(1)} copy-done((bf16[8,2,128,1280]{3,2,1,0:T(8,128)(2,1)S(1)}, bf16[8,2,128,1280]{3,2,1,0:T(8,128)(2,1)}, u32[]{:S(2)}) %copy-start) | copy-done | bytes 5242904
  218.7 4.9 %shard_map.105 = bf16[7,256,1280]{2,1,0:T(8,128)(2,1)} custom-call(s32[1]{0:T(128)} %bitcast.col_ref, bf16[8,2,112,128]{3,2,1,0:T(8,128)(2,1)S(1)} %bitcast.71, bf16[8,2,128,1280]{3,2,1,0:T(8,128)(2,1)S(1)} %copy-done, f32[112,2560]{1,0:T(8,128)S(1)} %fusion.2.base_ref, f32[112,1]{1,0:T(8,128)S(1)} %copy.21.scale_ref, bf16[7,256,256]{2,1,0:T(8,128)(2,1)S(1)} %fusion.7.pick_ref), custom_call_target="tpu_custom_call" | custom-call | flops 1174405120 | bytes 7208960 | tf_op jit(solution)/shard_map/pallas_call | solution.py:51
  223.6 4.9 %shard_map.104 = bf16[7,256,1280]{2,1,0:T(8,128)(2,1)} custom-call(s32[1]{0:T(128)} %bitcast.col_ref, bf16[8,2,112,128]{3,2,1,0:T(8,128)(2,1)S(1)} %bitcast.72, bf16[8,2,128,1280]{3,2,1,0:T(8,128)(2,1)S(1)} %copy-done, f32[112,2560]{1,0:T(8,128)S(1)} %fusion.2.base_ref, f32[112,1]{1,0:T(8,128)S(1)} %copy.21.scale_ref, bf16[7,256,256]{2,1,0:T(8,128)(2,1)S(1)} %fusion.7.pick_ref), custom_call_target="tpu_custom_call" | custom-call | flops 1174405120 | bytes 7208960 | tf_op jit(solution)/shard_map/pallas_call | solution.py:51
  (115 shorter events, 14.3 us)
Async XLA Ops:
  7.2 9.3 %copy-start.17 = (s32[12]{0:T(128)S(1)}, s32[12]{0:T(128)}, u32[]{:S(2)}) copy-start(s32[12]{0:T(128)} %param.14) | copy-start | bytes 148
  7.2 9.6 %copy-start.14 = (s32[32]{0:T(128)S(1)}, s32[32]{0:T(128)}, u32[]{:S(2)}) copy-start(s32[32]{0:T(128)} %param.17) | copy-start | bytes 388
  7.2 9.6 %copy-start.12 = (s32[144]{0:T(256)S(1)}, s32[144]{0:T(256)}, u32[]{:S(2)}) copy-start(s32[144]{0:T(256)} %param.16) | copy-start | bytes 1732
  7.2 9.7 %copy-start.13 = (s32[144]{0:T(256)S(1)}, s32[144]{0:T(256)}, u32[]{:S(2)}) copy-start(s32[144]{0:T(256)} %param.15) | copy-start | bytes 1732
  7.2 209.0 %all-gather.2.cloned.1.call-start = ((), (), s32[]{:S(2)}) async-start(), calls=%async_computation | async-start | bytes 5898240 | tf_op jit(solution)/shard_map/all_gather | solution.py:161
  10.5 27.6 %collective-permute-start.2 = (bf16[112,1280]{1,0:T(8,128)(2,1)}, bf16[112,1280]{1,0:T(8,128)(2,1)S(1)}, u32[]{:S(2)}, u32[]{:S(2)}) collective-permute-start(bf16[112,1280]{1,0:T(8,128)(2,1)} %get-tuple-element.10), channel_id=1, source_target_pairs={{0,6},{1,7},{2,4},{3,5},{4,2},{5,3},{6,0},{7,1},{8,14},{9,15},{10,... | collective-permute-start | bytes 860168 | tf_op jit(solution)/shard_map/ppermute | solution.py:130
  10.7 45.3 %collective-permute-start.1 = (bf16[112,1280]{1,0:T(8,128)(2,1)}, bf16[112,1280]{1,0:T(8,128)(2,1)S(1)}, u32[]{:S(2)}, u32[]{:S(2)}) collective-permute-start(bf16[112,1280]{1,0:T(8,128)(2,1)} %get-tuple-element.10), channel_id=1, source_target_pairs={{0,4},{1,5},{2,6},{3,7},{4,0},{5,1},{6,2},{7,3},{8,12},{9,13},{10,... | collective-permute-start | bytes 860168 | tf_op jit(solution)/shard_map/ppermute | solution.py:130
  13.9 60.5 %collective-permute-start = (bf16[112,1280]{1,0:T(8,128)(2,1)}, bf16[112,1280]{1,0:T(8,128)(2,1)}, u32[]{:S(2)}, u32[]{:S(2)}) collective-permute-start(bf16[112,1280]{1,0:T(8,128)(2,1)} %get-tuple-element.10), channel_id=1, source_target_pairs={{0,2},{1,3},{2,0},{3,1},{4,6},{5,7},{6,4},{7,5},{8,10},{9,11},{10,... | collective-permute-start | bytes 860168 | tf_op jit(solution)/shard_map/ppermute | solution.py:130
  15.0 4.3 %collective-permute-start.12 = (bf16[112,640]{1,0:T(8,128)(2,1)S(1)}, bf16[112,640]{1,0:T(8,128)(2,1)S(1)}, u32[]{:S(2)}, u32[]{:S(2)}) collective-permute-start(bf16[112,640]{1,0:T(8,128)(2,1)S(1)} %get-tuple-element.12), channel_id=1, source_target_pairs={{0,1},{1,0},{2,3},{3,2},{4,5},{5,4},{6,7},{7,6},{8,9},{9,8},{10,11... | collective-permute-start | bytes 430088 | tf_op jit(solution)/shard_map/ppermute | solution.py:130
  16.2 61.6 %collective-permute-start.3 = (bf16[1280,256]{1,0:T(8,128)(2,1)}, bf16[1280,256]{1,0:T(8,128)(2,1)}, u32[]{:S(2)}, u32[]{:S(2)}) collective-permute-start(bf16[1280,256]{1,0:T(8,128)(2,1)} %bitcast.1), channel_id=1, source_target_pairs={{0,1},{1,0},{2,3},{3,2},{4,5},{5,4},{6,7},{7,6},{8,9},{9,8},{10,11... | collective-permute-start | bytes 1966088 | tf_op jit(solution)/shard_map/ppermute | solution.py:130
  19.3 46.2 %copy-start.6 = (bf16[112,640]{1,0:T(8,128)(2,1)}, bf16[112,640]{1,0:T(8,128)(2,1)S(1)}, u32[]{:S(2)}) copy-start(bf16[112,640]{1,0:T(8,128)(2,1)S(1)} %collective-permute-done.12) | copy-start | bytes 430084
  20.1 43.3 %collective-permute-start.13 = (bf16[2,112,640]{2,1,0:T(8,128)(2,1)}, bf16[2,112,640]{2,1,0:T(8,128)(2,1)}, u32[]{:S(2)}, u32[]{:S(2)}) collective-permute-start(bf16[2,112,640]{2,1,0:T(8,128)(2,1)} %pad_maximum_fusion.1), channel_id=1, source_target_pairs={{0,16},{1,17},{10,26},{11,27},{20,4},{21,5},{30,14},{31,15}} | collective-permute-start | bytes 860168 | tf_op jit(solution)/shard_map/ppermute | solution.py:130
  38.1 27.4 %copy-start.15 = (bf16[112,1280]{1,0:T(8,128)(2,1)}, bf16[112,1280]{1,0:T(8,128)(2,1)S(1)}, u32[]{:S(2)}) copy-start(bf16[112,1280]{1,0:T(8,128)(2,1)S(1)} %collective-permute-done.2) | copy-start | bytes 860164
  38.1 37.7 %collective-permute-start.21 = (bf16[2,112,640]{2,1,0:T(8,128)(2,1)}, bf16[2,112,640]{2,1,0:T(8,128)(2,1)}, u32[]{:S(2)}, u32[]{:S(2)}) collective-permute-start(bf16[2,112,640]{2,1,0:T(8,128)(2,1)} %pad_maximum_fusion.1), channel_id=1, source_target_pairs={{4,0},{5,1},{14,10},{15,11},{16,20},{17,21},{26,30},{27,31}} | collective-permute-start | bytes 860168 | tf_op jit(solution)/shard_map/ppermute | solution.py:130
  56.0 9.4 %copy-start.16 = (bf16[112,1280]{1,0:T(8,128)(2,1)}, bf16[112,1280]{1,0:T(8,128)(2,1)S(1)}, u32[]{:S(2)}) copy-start(bf16[112,1280]{1,0:T(8,128)(2,1)S(1)} %collective-permute-done.1) | copy-start | bytes 860164
  56.0 20.4 %collective-permute-start.16 = (bf16[2,112,640]{2,1,0:T(8,128)(2,1)}, bf16[2,112,640]{2,1,0:T(8,128)(2,1)}, u32[]{:S(2)}, u32[]{:S(2)}) collective-permute-start(bf16[2,112,640]{2,1,0:T(8,128)(2,1)} %pad_maximum_fusion.1), channel_id=1, source_target_pairs={{2,0},{3,1},{8,10},{9,11},{22,20},{23,21},{28,30},{29,31}} | collective-permute-start | bytes 860168 | tf_op jit(solution)/shard_map/ppermute | solution.py:130
  63.4 13.8 %collective-permute-start.26 = (bf16[2,112,640]{2,1,0:T(8,128)(2,1)}, bf16[2,112,640]{2,1,0:T(8,128)(2,1)}, u32[]{:S(2)}, u32[]{:S(2)}) collective-permute-start(bf16[2,112,640]{2,1,0:T(8,128)(2,1)} %pad_maximum_fusion.1), channel_id=1, source_target_pairs={{6,0},{7,1},{12,10},{13,11},{18,20},{19,21},{24,30},{25,31}} | collective-permute-start | bytes 860168 | tf_op jit(solution)/shard_map/ppermute | solution.py:130
  67.9 84.7 %copy-start.1 = (bf16[80,8,2,1280]{3,1,2,0:T(8,128)(2,1)}, bf16[80,8,2,1280]{3,1,2,0:T(8,128)(2,1)S(1)}, u32[]{:S(2)}) copy-start(bf16[80,8,2,1280]{3,1,2,0:T(8,128)(2,1)S(1)} %copy.23) | copy-start | bytes 9830404
  74.5 18.9 %collective-permute-start.14 = (bf16[2,112,640]{2,1,0:T(8,128)(2,1)S(1)}, bf16[2,112,640]{2,1,0:T(8,128)(2,1)S(1)}, u32[]{:S(2)}, u32[]{:S(2)}) collective-permute-start(bf16[2,112,640]{2,1,0:T(8,128)(2,1)S(1)} %broadcast_select_fusion.5), channel_id=1, source_target_pairs={{0,8},{16,24},{1,9},{17,25},{10,2},{26,18},{11,3},{27,19},{20,28},... | collective-permute-start | bytes 860168 | tf_op jit(solution)/shard_map/ppermute | solution.py:130
  75.8 16.6 %collective-permute-start.22 = (bf16[2,112,640]{2,1,0:T(8,128)(2,1)}, bf16[2,112,640]{2,1,0:T(8,128)(2,1)S(1)}, u32[]{:S(2)}, u32[]{:S(2)}) collective-permute-start(bf16[2,112,640]{2,1,0:T(8,128)(2,1)} %collective-permute-done.21), channel_id=1, source_target_pairs={{0,16},{1,17},{10,26},{11,27},{20,4},{21,5},{30,14},{31,15}} | collective-permute-start | bytes 860168 | tf_op jit(solution)/shard_map/ppermute | solution.py:130
  76.5 19.0 %collective-permute-start.17 = (bf16[2,112,640]{2,1,0:T(8,128)(2,1)}, bf16[2,112,640]{2,1,0:T(8,128)(2,1)S(1)}, u32[]{:S(2)}, u32[]{:S(2)}) collective-permute-start(bf16[2,112,640]{2,1,0:T(8,128)(2,1)} %collective-permute-done.16), channel_id=1, source_target_pairs={{0,16},{1,17},{10,26},{11,27},{20,4},{21,5},{30,14},{31,15}} | collective-permute-start | bytes 860168 | tf_op jit(solution)/shard_map/ppermute | solution.py:130
  77.2 28.6 %collective-permute-start.27 = (bf16[2,112,640]{2,1,0:T(8,128)(2,1)}, bf16[2,112,640]{2,1,0:T(8,128)(2,1)S(1)}, u32[]{:S(2)}, u32[]{:S(2)}) collective-permute-start(bf16[2,112,640]{2,1,0:T(8,128)(2,1)} %collective-permute-done.26), channel_id=1, source_target_pairs={{0,16},{1,17},{10,26},{11,27},{20,4},{21,5},{30,14},{31,15}} | collective-permute-start | bytes 860168 | tf_op jit(solution)/shard_map/ppermute | solution.py:130
  80.3 13.7 %copy-start.7 = (bf16[112,640]{1,0:T(8,128)(2,1)S(1)}, bf16[112,640]{1,0:T(8,128)(2,1)}, u32[]{:S(2)}) copy-start(bf16[112,640]{1,0:T(8,128)(2,1)} %copy-done.6) | copy-start | bytes 430084
  80.3 17.5 %collective-permute-start.4 = (f32[112,512]{1,0:T(8,128)S(1)}, f32[112,512]{1,0:T(8,128)S(1)}, u32[]{:S(2)}, u32[]{:S(2)}) collective-permute-start(f32[112,512]{1,0:T(8,128)S(1)} %get-tuple-element.6), channel_id=1, source_target_pairs={{0,8},{1,9},{2,10},{3,11},{4,12},{5,13},{6,14},{7,15},{8,0},{9,1},... | collective-permute-start | bytes 688136 | tf_op jit(solution)/shard_map/ppermute | solution.py:130
  92.4 7.9 %collective-permute-start.6 = (f32[112,512]{1,0:T(8,128)S(1)}, f32[112,512]{1,0:T(8,128)S(1)}, u32[]{:S(2)}, u32[]{:S(2)}) collective-permute-start(f32[112,512]{1,0:T(8,128)S(1)} %get-tuple-element.7), channel_id=1, source_target_pairs={{0,24},{1,25},{2,26},{3,27},{4,28},{5,29},{6,30},{7,31},{8,16},{9,... | collective-permute-start | bytes 688136 | tf_op jit(solution)/shard_map/ppermute | solution.py:130
  93.4 10.9 %collective-permute-start.5 = (f32[112,512]{1,0:T(8,128)S(1)}, f32[112,512]{1,0:T(8,128)S(1)}, u32[]{:S(2)}, u32[]{:S(2)}) collective-permute-start(f32[112,512]{1,0:T(8,128)S(1)} %get-tuple-element.8), channel_id=1, source_target_pairs={{0,16},{1,17},{2,18},{3,19},{4,20},{5,21},{6,22},{7,23},{8,24},{9,... | collective-permute-start | bytes 688136 | tf_op jit(solution)/shard_map/ppermute | solution.py:130
  95.5 21.1 %collective-permute-start.23 = (bf16[2,112,640]{2,1,0:T(8,128)(2,1)S(1)}, bf16[2,112,640]{2,1,0:T(8,128)(2,1)S(1)}, u32[]{:S(2)}, u32[]{:S(2)}) collective-permute-start(bf16[2,112,640]{2,1,0:T(8,128)(2,1)S(1)} %broadcast_select_fusion.3), channel_id=1, source_target_pairs={{0,8},{16,24},{1,9},{17,25},{10,2},{26,18},{11,3},{27,19},{20,28},... | collective-permute-start | bytes 860168 | tf_op jit(solution)/shard_map/ppermute | solution.py:130
  97.8 17.1 %collective-permute-start.18 = (bf16[2,112,640]{2,1,0:T(8,128)(2,1)S(1)}, bf16[2,112,640]{2,1,0:T(8,128)(2,1)S(1)}, u32[]{:S(2)}, u32[]{:S(2)}) collective-permute-start(bf16[2,112,640]{2,1,0:T(8,128)(2,1)S(1)} %broadcast_select_fusion.4), channel_id=1, source_target_pairs={{0,8},{16,24},{1,9},{17,25},{10,2},{26,18},{11,3},{27,19},{20,28},... | collective-permute-start | bytes 860168 | tf_op jit(solution)/shard_map/ppermute | solution.py:130
  104.4 4.7 %collective-permute-start.9 = (bf16[112,512]{1,0:T(8,128)(2,1)S(1)}, bf16[112,512]{1,0:T(8,128)(2,1)S(1)}, u32[]{:S(2)}, u32[]{:S(2)}) collective-permute-start(bf16[112,512]{1,0:T(8,128)(2,1)S(1)} %fusion.23), channel_id=1, source_target_pairs={{6,0},{7,1},{12,10},{13,11},{18,20},{19,21},{24,30},{25,31}} | collective-permute-start | bytes 344072 | tf_op jit(solution)/shard_map/ppermute | solution.py:130
  105.1 5.3 %collective-permute-start.8 = (bf16[112,512]{1,0:T(8,128)(2,1)S(1)}, bf16[112,512]{1,0:T(8,128)(2,1)S(1)}, u32[]{:S(2)}, u32[]{:S(2)}) collective-permute-start(bf16[112,512]{1,0:T(8,128)(2,1)S(1)} %fusion.23), channel_id=1, source_target_pairs={{4,0},{5,1},{14,10},{15,11},{16,20},{17,21},{26,30},{27,31}} | collective-permute-start | bytes 344072 | tf_op jit(solution)/shard_map/ppermute | solution.py:130
  105.8 8.3 %collective-permute-start.7 = (bf16[112,512]{1,0:T(8,128)(2,1)S(1)}, bf16[112,512]{1,0:T(8,128)(2,1)S(1)}, u32[]{:S(2)}, u32[]{:S(2)}) collective-permute-start(bf16[112,512]{1,0:T(8,128)(2,1)S(1)} %fusion.23), channel_id=1, source_target_pairs={{2,0},{3,1},{8,10},{9,11},{22,20},{23,21},{28,30},{29,31}} | collective-permute-start | bytes 344072 | tf_op jit(solution)/shard_map/ppermute | solution.py:130
  109.1 12.8 %collective-permute-start.28 = (bf16[2,112,640]{2,1,0:T(8,128)(2,1)S(1)}, bf16[2,112,640]{2,1,0:T(8,128)(2,1)S(1)}, u32[]{:S(2)}, u32[]{:S(2)}) collective-permute-start(bf16[2,112,640]{2,1,0:T(8,128)(2,1)S(1)} %broadcast_select_fusion.2), channel_id=1, source_target_pairs={{0,8},{16,24},{1,9},{17,25},{10,2},{26,18},{11,3},{27,19},{20,28},... | collective-permute-start | bytes 860168 | tf_op jit(solution)/shard_map/ppermute | solution.py:130
  110.4 13.1 %copy-start.8 = (bf16[112,512]{1,0:T(8,128)(2,1)}, bf16[112,512]{1,0:T(8,128)(2,1)S(1)}, u32[]{:S(2)}) copy-start(bf16[112,512]{1,0:T(8,128)(2,1)S(1)} %collective-permute-done.8) | copy-start | bytes 344068
  110.4 67.0 %collective-permute-start.15 = (bf16[112,2560]{1,0:T(8,128)(2,1)}, bf16[112,2560]{1,0:T(8,128)(2,1)}, u32[]{:S(2)}, u32[]{:S(2)}) collective-permute-start(bf16[112,2560]{1,0:T(8,128)(2,1)} %convolution_convert_fusion.3), channel_id=1, source_target_pairs={{0,1},{1,0},{2,3},{3,2},{4,5},{5,4},{6,7},{7,6},{8,9},{9,8},{10,11... | collective-permute-start | bytes 1720328 | tf_op jit(solution)/shard_map/ppermute | solution.py:130
  114.1 9.4 %copy-start.10 = (bf16[112,512]{1,0:T(8,128)(2,1)}, bf16[112,512]{1,0:T(8,128)(2,1)S(1)}, u32[]{:S(2)}) copy-start(bf16[112,512]{1,0:T(8,128)(2,1)S(1)} %collective-permute-done.7) | copy-start | bytes 344068
  114.2 9.3 %collective-permute-start.10 = (bf16[4,112,512]{2,1,0:T(8,128)(2,1)S(1)}, bf16[4,112,512]{2,1,0:T(8,128)(2,1)S(1)}, u32[]{:S(2)}, u32[]{:S(2)}) collective-permute-start(bf16[4,112,512]{2,1,0:T(8,128)(2,1)S(1)} %pad_maximum_fusion), channel_id=1, source_target_pairs={{0,16},{1,17},{10,26},{11,27},{20,4},{21,5},{30,14},{31,15}} | collective-permute-start | bytes 1376264 | tf_op jit(solution)/shard_map/ppermute | solution.py:130
  115.6 11.5 %collective-permute-start.19 = (bf16[112,2560]{1,0:T(8,128)(2,1)S(1)}, bf16[112,2560]{1,0:T(8,128)(2,1)S(1)}, u32[]{:S(2)}, u32[]{:S(2)}) collective-permute-start(bf16[112,2560]{1,0:T(8,128)(2,1)S(1)} %convolution_convert_fusion.2), channel_id=1, source_target_pairs={{0,1},{1,0},{2,3},{3,2},{4,5},{5,4},{6,7},{7,6},{8,9},{9,8},{10,11... | collective-permute-start | bytes 1720328 | tf_op jit(solution)/shard_map/ppermute | solution.py:130
  117.3 32.0 %collective-permute-start.24 = (bf16[112,2560]{1,0:T(8,128)(2,1)S(1)}, bf16[112,2560]{1,0:T(8,128)(2,1)S(1)}, u32[]{:S(2)}, u32[]{:S(2)}) collective-permute-start(bf16[112,2560]{1,0:T(8,128)(2,1)S(1)} %convolution_convert_fusion.1), channel_id=1, source_target_pairs={{0,1},{1,0},{2,3},{3,2},{4,5},{5,4},{6,7},{7,6},{8,9},{9,8},{10,11... | collective-permute-start | bytes 1720328 | tf_op jit(solution)/shard_map/ppermute | solution.py:130
  122.6 29.9 %collective-permute-start.29 = (bf16[112,2560]{1,0:T(8,128)(2,1)S(1)}, bf16[112,2560]{1,0:T(8,128)(2,1)S(1)}, u32[]{:S(2)}, u32[]{:S(2)}) collective-permute-start(bf16[112,2560]{1,0:T(8,128)(2,1)S(1)} %convolution_convert_fusion), channel_id=1, source_target_pairs={{0,1},{1,0},{2,3},{3,2},{4,5},{5,4},{6,7},{7,6},{8,9},{9,8},{10,11... | collective-permute-start | bytes 1720328 | tf_op jit(solution)/shard_map/ppermute | solution.py:130
  125.1 50.9 %collective-permute-start.11 = (bf16[4,112,512]{2,1,0:T(8,128)(2,1)}, bf16[4,112,512]{2,1,0:T(8,128)(2,1)}, u32[]{:S(2)}, u32[]{:S(2)}) collective-permute-start(bf16[4,112,512]{2,1,0:T(8,128)(2,1)} %broadcast_select_fusion), channel_id=1, source_target_pairs={{0,8},{16,24},{1,9},{17,25},{10,2},{26,18},{11,3},{27,19},{20,28},... | collective-permute-start | bytes 1376264 | tf_op jit(solution)/shard_map/ppermute | solution.py:130
  128.6 48.9 %collective-permute-start.20 = (bf16[112,2560]{1,0:T(8,128)(2,1)}, bf16[112,2560]{1,0:T(8,128)(2,1)}, u32[]{:S(2)}, u32[]{:S(2)}) collective-permute-start(bf16[112,2560]{1,0:T(8,128)(2,1)} %fusion.3), channel_id=1, source_target_pairs={{0,2},{1,3},{2,0},{3,1},{4,6},{5,7},{6,4},{7,5},{8,10},{9,11},{10,... | collective-permute-start | bytes 1720328 | tf_op jit(solution)/shard_map/ppermute | solution.py:130
  150.9 26.6 %collective-permute-start.25 = (bf16[112,2560]{1,0:T(8,128)(2,1)}, bf16[112,2560]{1,0:T(8,128)(2,1)}, u32[]{:S(2)}, u32[]{:S(2)}) collective-permute-start(bf16[112,2560]{1,0:T(8,128)(2,1)} %fusion.4), channel_id=1, source_target_pairs={{0,4},{1,5},{2,6},{3,7},{4,0},{5,1},{6,2},{7,3},{8,12},{9,13},{10,... | collective-permute-start | bytes 1720328 | tf_op jit(solution)/shard_map/ppermute | solution.py:130
  154.0 22.0 %copy-start.3 = (bf16[4,112,512]{2,1,0:T(8,128)(2,1)S(1)}, bf16[4,112,512]{2,1,0:T(8,128)(2,1)}, u32[]{:S(2)}) copy-start(bf16[4,112,512]{2,1,0:T(8,128)(2,1)} %copy-done.2) | copy-start | bytes 1376260
  154.1 22.0 %copy-start.9 = (bf16[112,512]{1,0:T(8,128)(2,1)S(1)}, bf16[112,512]{1,0:T(8,128)(2,1)}, u32[]{:S(2)}) copy-start(bf16[112,512]{1,0:T(8,128)(2,1)} %copy-done.8) | copy-start | bytes 344068
  154.1 22.0 %copy-start.11 = (bf16[112,512]{1,0:T(8,128)(2,1)S(1)}, bf16[112,512]{1,0:T(8,128)(2,1)}, u32[]{:S(2)}) copy-start(bf16[112,512]{1,0:T(8,128)(2,1)} %copy-done.10) | copy-start | bytes 344068
  154.1 58.8 %collective-permute-start.30 = (bf16[112,2560]{1,0:T(8,128)(2,1)}, bf16[112,2560]{1,0:T(8,128)(2,1)}, u32[]{:S(2)}, u32[]{:S(2)}) collective-permute-start(bf16[112,2560]{1,0:T(8,128)(2,1)} %fusion.5), channel_id=1, source_target_pairs={{0,6},{1,7},{2,4},{3,5},{4,2},{5,3},{6,0},{7,1},{8,14},{9,15},{10,... | collective-permute-start | bytes 1720328 | tf_op jit(solution)/shard_map/ppermute | solution.py:130
  176.0 36.8 %copy-start.5 = (bf16[2,112,640]{2,1,0:T(8,128)(2,1)S(1)}, bf16[2,112,640]{2,1,0:T(8,128)(2,1)}, u32[]{:S(2)}) copy-start(bf16[2,112,640]{2,1,0:T(8,128)(2,1)} %copy-done.4) | copy-start | bytes 860164
  216.2 2.5 %copy-start = (bf16[8,2,128,1280]{3,2,1,0:T(8,128)(2,1)S(1)}, bf16[8,2,128,1280]{3,2,1,0:T(8,128)(2,1)}, u32[]{:S(2)}) copy-start(bf16[8,2,128,1280]{3,2,1,0:T(8,128)(2,1)} %all-gather.2.cloned.1.call-done.up_ref) | copy-start | bytes 15728644
  (2 other events, 2.3 us)
Sparse Core Ops, SparseCore 0:
  10.2 106.8 all-gather.1

commit v2 on v1

v2 whole, which is shorter than its diff:
```python
import functools

import jax
import jax.numpy as jnp
from jax import lax
from jax.experimental import pallas as pl
from jax.experimental.pallas import tpu as pltpu
from jax.sharding import PartitionSpec as P

SLOTS = 16
GROUP = 16


def delta_kernel(rank_ref, up_ref, scale_ref, out_ref):
    product = jnp.dot(rank_ref[0], up_ref[0], preferred_element_type=jnp.float32)
    out_ref[...] = (product * scale_ref[...]).astype(jnp.bfloat16)


def corrections(rank, up, scale):
    _, tokens, low_rank = rank.shape
    width = up.shape[2]
    return pl.pallas_call(
        delta_kernel,
        grid=(2,),
        in_specs=[
            pl.BlockSpec((1, tokens, low_rank), lambda j: (j, 0, 0)),
            pl.BlockSpec((1, low_rank, width), lambda j: (j, 0, 0)),
            pl.BlockSpec((tokens, 1), lambda j: (0, 0)),
        ],
        out_specs=pl.BlockSpec((tokens, width), lambda j: (0, j)),
        out_shape=jax.ShapeDtypeStruct((tokens, 2 * width), jnp.bfloat16),
        compiler_params=pltpu.CompilerParams(vmem_limit_bytes=24 * 1024 * 1024),
        cost_estimate=pl.CostEstimate(
            flops=4 * tokens * low_rank * width,
            bytes_accessed=4 * (tokens * width + low_rank * width),
            transcendentals=0,
        ),
    )(rank, up, scale)


def mix_kernel(*refs, adapters, parts):
    deltas, bases = refs[:adapters], refs[adapters : adapters + parts]
    scale_ref, pick_ref, out_ref, rows_ref = refs[adapters + parts :]
    tokens = scale_ref.shape[0]
    groups = tokens // GROUP
    used = adapters * GROUP

    @pl.when(pl.program_id(0) == 0)
    def _():
        rows_ref[:, used + 2 * GROUP :, :] = jnp.zeros_like(rows_ref[:, used + 2 * GROUP :, :])

    base = bases[0][...].astype(jnp.float32)
    for part in bases[1:]:
        base = base + part[...].astype(jnp.float32)
    base = base * scale_ref[...]
    high = base.astype(jnp.bfloat16)
    low = (base - high.astype(jnp.float32)).astype(jnp.bfloat16)
    for g in range(groups):
        here = slice(g * GROUP, (g + 1) * GROUP)
        for a in range(adapters):
            rows_ref[g, a * GROUP : (a + 1) * GROUP, :] = deltas[a][here, :]
        rows_ref[g, used : used + GROUP, :] = high[here, :]
        rows_ref[g, used + GROUP : used + 2 * GROUP, :] = low[here, :]
    for g in range(groups):
        mixed = jnp.dot(pick_ref[g], rows_ref[g], preferred_element_type=jnp.float32)
        out_ref[g] = mixed.astype(jnp.bfloat16)


def mix(deltas, bases, scale, pick, half):
    tokens, width = deltas[0].shape[0], deltas[0].shape[1] // 2
    groups, rows, depth = pick.shape
    block = 256 if width % 256 == 0 else 128
    steps = width // block
    column = pl.BlockSpec((tokens, block), lambda i: (0, half * steps + i))
    out = pl.pallas_call(
        functools.partial(mix_kernel, adapters=len(deltas), parts=len(bases)),
        grid=(steps,),
        in_specs=[column] * (len(deltas) + len(bases))
        + [
            pl.BlockSpec((tokens, 1), lambda i: (0, 0)),
            pl.BlockSpec((groups, rows, depth), lambda i: (0, 0, 0)),
        ],
        out_specs=pl.BlockSpec((groups, rows, block), lambda i: (0, 0, i)),
        scratch_shapes=[pltpu.VMEM((groups, depth, block), jnp.bfloat16)],
        out_shape=jax.ShapeDtypeStruct((groups, rows, width), jnp.bfloat16),
        compiler_params=pltpu.CompilerParams(vmem_limit_bytes=40 * 1024 * 1024),
        cost_estimate=pl.CostEstimate(
            flops=2 * groups * rows * depth * width,
            bytes_accessed=2 * groups * rows * width,
            transcendentals=0,
        ),
    )(*deltas, *bases, scale, pick)
    return out.reshape(tokens, SLOTS, width)


def pick_matrix(
    token_index,
    prompt_token_length,
    prompt_of_request,
    adapter_of_request,
    adapter_slot_index,
    adapters,
    depth,
    order,
):
    tokens = token_index.shape[0]
    ends = jnp.cumsum(prompt_token_length)
    prompt_of = jnp.sum((token_index[:, None] >= ends[None, :]).astype(jnp.int32), axis=1)
    first = jnp.sum((prompt_of_request[None, :] < prompt_of[:, None]).astype(jnp.int32), axis=1)
    after = jnp.sum((prompt_of_request[None, :] <= prompt_of[:, None]).astype(jnp.int32), axis=1)
    hot = adapter_of_request[:, None] == jnp.arange(adapter_slot_index.shape[0], dtype=jnp.int32)[None, :]
    slot_of = jnp.sum(jnp.where(hot, adapter_slot_index[None, :], 0), axis=1)
    request = first[:, None] + jnp.arange(SLOTS, dtype=jnp.int32)[None, :]
    live = request < after[:, None]
    requests = jnp.arange(prompt_of_request.shape[0], dtype=jnp.int32)
    slot = jnp.sum(
        jnp.where(request[:, :, None] == requests[None, None, :], slot_of[None, None, :], 0), axis=2
    )
    place = (jnp.arange(tokens, dtype=jnp.int32) % GROUP)[:, None]
    column = jnp.where(live, order(slot) * GROUP + place, -1)
    columns = jnp.arange(depth, dtype=jnp.int32)[None, None, :]
    used = adapters * GROUP
    of_base = (columns >= used) & (columns < used + 2 * GROUP) & (columns % GROUP == place[:, :, None])
    pick = (columns == column[:, :, None]) | (of_base & live[:, :, None])
    return pick.astype(jnp.bfloat16).reshape(tokens // GROUP, GROUP * SLOTS, depth)


def body(
    prompt_token_states,
    gain,
    projection_weight,
    adapter_down_maps,
    adapter_up_maps,
    prompt_token_length,
    prompt_of_request,
    adapter_of_request,
    adapter_slot_index,
):
    rows, cols = lax.axis_size("row"), lax.axis_size("col")
    row, col = lax.axis_index("row"), lax.axis_index("col")
    lines = cols // 2
    line, side = col // 2, col % 2
    tokens, width = prompt_token_states.shape
    depth_in = projection_weight.shape[0]
    low_rank = adapter_down_maps.shape[2] // 2
    adapters = cols

    def send(value, pairs):
        flat = [(a * cols + b, c * cols + d) for (a, b), (c, d) in pairs]
        return lax.ppermute(value, ("row", "col"), flat)

    every = [(r, c) for r in range(rows) for c in range(cols)]

    def to_side(value):
        return send(value, [((r, c), (r, c ^ 1)) for r, c in every])

    def to_line(value, k):
        return send(value, [((r, c), (r, c ^ (2 * k))) for r, c in every])

    def to_owner(value, k):
        return send(
            value, [((r, 2 * (r ^ k) + s), (r, 2 * r + s)) for r in range(rows) for s in range(2)]
        )

    def over_rows(value, *before_last):
        bit = 2
        while bit < rows:
            got = send(
                value,
                [
                    ((c // 2 ^ e, c), (c // 2 ^ e ^ bit, c))
                    for c in range(cols)
                    for e in range(0, bit, 2)
                ],
            )
            value = jnp.where((row ^ line) & bit != 0, got, value)
            bit *= 2
        if before_last:
            value = lax.optimization_barrier((value, *before_last))[0]
        got = send(
            value,
            [((c // 2 ^ e, c), (c // 2 ^ e ^ 1, c)) for c in range(cols) for e in range(0, rows, 2)],
        )
        return jnp.where((row ^ line) & 1 != 0, got, value)

    def after(value, *others):
        return lax.optimization_barrier((value, *others))[0]

    def pairs_of(lines_pairs):
        return [
            ((r, 2 * a + s), (r, 2 * b + s)) for r in range(rows) for a, b in lines_pairs for s in range(2)
        ]

    across = pairs_of([(1, 2), (2, 1)])
    outward = pairs_of([(1, 0), (2, 3)])
    inner = (line == 1) | (line == 2)
    up_own = adapter_up_maps[0]
    weight = projection_weight.reshape(depth_in, 2 * width)

    states = prompt_token_states.astype(jnp.float32)
    gained = (states * gain.astype(jnp.float32)[None, :]).astype(jnp.bfloat16)

    def halves(values):
        mine = lax.dynamic_slice_in_dim(values, side * depth_in, depth_in, 2)
        theirs = lax.dynamic_slice_in_dim(values, (1 - side) * depth_in, depth_in, 2)
        return mine, send(theirs, [((c // 2, c), (c // 2, c ^ 1)) for c in range(cols)])

    def product(value):
        return jnp.dot(value, weight, preferred_element_type=jnp.float32)

    rest = [to_line(gained, k) for k in range(1, lines)]
    both = over_rows(jnp.stack(halves(gained[None])))
    other_down = to_side(after(adapter_down_maps[0], gained))
    up_other = to_side(after(up_own, gained))
    own_out = to_side(product(both[1, 0]).astype(jnp.bfloat16))
    own_kept = product(both[0, 0])

    late = lax.optimization_barrier((up_own, *rest))
    up_late, rest = late[0], late[1:]
    if lines == 4:
        near = to_line(up_late, 1)
        far_near = send(up_late, across)
    else:
        near = to_line(up_late, 1)
        far_near = near

    mine, got = halves(jnp.stack(rest))
    gathered = jnp.concatenate([gained, *rest], axis=0)
    gathered, other_down, up_other = lax.optimization_barrier((gathered, other_down, up_other))
    down = jnp.concatenate([adapter_down_maps[0], other_down], axis=1)
    partial = jnp.dot(gathered, down, preferred_element_type=jnp.float32)
    got, partial = lax.optimization_barrier((got, partial))
    partial = partial.reshape(lines, tokens, 4 * low_rank)
    parts = {
        m: lax.dynamic_index_in_dim(partial, row ^ line ^ m, 0, keepdims=False) for m in range(rows)
    }
    bit = 1
    while bit < rows:
        leaving = [m for m in parts if m & bit]
        arrived = send(
            jnp.stack([parts.pop(m) for m in leaving]), [((r, c), (r ^ bit, c)) for r, c in every]
        )
        for i, m in enumerate(leaving):
            parts[m ^ bit] = parts[m ^ bit] + arrived[i]
        bit *= 2
    held = parts[0].astype(jnp.bfloat16)

    both = over_rows(jnp.stack([mine, got]), held, near, far_near)
    both = after(both, own_out)
    outs = [product(both[1, k]).astype(jnp.bfloat16) for k in range(lines - 1)]
    kept = [product(both[0, k]) for k in range(lines - 1)]
    came = [None] * (lines - 1)
    for k in reversed(range(lines - 1)):
        came[k] = to_side(outs[k])

    ranks = [held] + [to_owner(held, k) for k in range(1, lines)]
    if lines == 4:
        far_far = send(near, across)
        first = send(far_near, outward)
        far_far, first, *ranks = lax.optimization_barrier((far_far, first, *ranks, came[-1]))[:-1]
        last = jnp.where(inner, far_far, send(far_far, outward))
        first = jnp.where(inner, far_near, first)
        blocks = [near, first, last]
    else:
        blocks = [near] + [to_line(up_own, k) for k in range(2, lines)]
    ranks = over_rows(jnp.stack(ranks))
    ranks = ranks.reshape(lines, tokens, 2, 2, low_rank).transpose(0, 2, 3, 1, 4)
    ranks = ranks.reshape(adapters, 2, tokens, low_rank)
    if lines == 4:
        far = jnp.where(inner, jnp.concatenate([ranks[6:], ranks[4:6]]), ranks[4:])
        ranks = jnp.concatenate([ranks[:4], far])

    ups = [up_own, up_other]
    for value in blocks:
        ups += [value, to_side(after(value, came[-1]))]

    bases = [own_kept + own_out.astype(jnp.float32)]
    for k in reversed(range(lines - 1)):
        total = kept[k] + came[k].astype(jnp.float32)
        bases.append(to_line(total.astype(jnp.bfloat16), k + 1))

    def order(slot):
        place = slot ^ col
        return jnp.where(inner & (place >= 4), place ^ 2, place) if lines == 4 else place

    square_sum = after(jnp.sum(states * states, axis=1), partial)
    total = square_sum
    for j in range(1, rows):
        total = total + send(square_sum, [((r, c), (r ^ j, c)) for r, c in every])
    scale = lax.rsqrt(total / (width * rows) + 1e-05)[:, None]
    depth = -(-(adapters * GROUP + 2 * GROUP) // 128) * 128
    token_index = col * tokens + jnp.arange(tokens, dtype=jnp.int32)
    pick = pick_matrix(
        token_index,
        prompt_token_length,
        prompt_of_request,
        adapter_of_request,
        adapter_slot_index,
        adapters,
        depth,
        order,
    )
    deltas = [corrections(ranks[e], ups[e], scale) for e in range(adapters)]
    return tuple(mix(deltas, bases, scale, pick, half) for half in range(2))


def solution(mesh):
    placed = (
        P("col", "row"),
        P("row"),
        P("col", None, "row"),
        P("col", "row", None),
        P("col", None, None, "row"),
        P(),
        P(),
        P(),
        P(),
    )
    return jax.shard_map(
        body,
        mesh=mesh,
        in_specs=placed,
        out_specs=(P("col", None, "row"), P("col", None, "row")),
        check_vma=False,
    )
```

time: 236 us -> 189 us (0.80)
  the two profiles are of different devices: /device:TPU:21 before, /device:TPU:0 now
where the time goes in v2:
time: 189 us; the launch traced here: 187 us
  waiting for transfers between devices  84.1 us (44%)
  starting transfers between devices  54.6 us (29%)
  Pallas kernels  18.5 us (10%)
  matrix products  12.8 us (7%)
  local copies, waits for them, and re-layouts  8.69 us (5%)
  other arithmetic  7.38 us (4%)
    ppermute x36, waiting for transfers between devices, send(): return lax.ppermute(value, ('row', 'col'), flat)  84.1 us
    ppermute x36, starting transfers between devices, send(): return lax.ppermute(value, ('row', 'col'), flat)  54.6 us
    pallas_call x2, Pallas kernels, mix(): pl.pallas_call(functools.partial(mix_kernel, adapters=len(deltas), parts=...  11.5 us
    dot_general x8, matrix products, product(): return jnp.dot(value, weight, preferred_element_type=jnp.float32)  10.7 us
    pallas_call x8, Pallas kernels, corrections(): pl.pallas_call(delta_kernel, grid=(2,), in_specs=[pl.BlockSpec((1, tokens...  7.05 us
    unnamed x19, local copies, waits for them, and re-layouts  4.3 us
  transfers between devices with their start and end apart: 36, of which 13 were waited for; matrix products, arithmetic and copies ran while one was open for 14% of the time, Pallas kernels for 4%

profile of v2, /device:TPU:0, one launch (start us, length us, event | category | flops | bytes accessed | tf_op | source)
XLA Modules:
  0.0 187.5 jit_solution(13943229830393421866)
XLA Ops:
  1.3 1.1 fusion.7
  2.5 5.1 %collective-permute-start.2 = (bf16[112,1280]{1,0:T(8,128)(2,1)S(1)}, bf16[112,1280]{1,0:T(8,128)(2,1)S(1)}, u32[]{:S(2)}, u32[]{:S(2)}) collective-permute-start(bf16[112,1280]{1,0:T(8,128)(2,1)S(1)} %get-tuple-element.61), channel_id=1, source_target_pairs={{0,6},{1,7},{2,4},{3,5},{4,2},{5,3},{6,0},{7,1},{8,14},{9,15},{10,... | collective-permute-start | bytes 860168 | tf_op jit(solution)/shard_map/ppermute | solution.py:150
  8.3 3.6 %collective-permute-start.17 = (bf16[1,112,640]{2,1,0:T(8,128)(2,1)S(1)}, bf16[1,112,640]{2,1,0:T(8,128)(2,1)S(1)}, u32[]{:S(2)}, u32[]{:S(2)}) collective-permute-start(bf16[1,112,640]{2,1,0:T(8,128)(2,1)S(1)} %get-tuple-element.63), channel_id=1, source_target_pairs={{0,1},{1,0},{10,11},{11,10},{20,21},{21,20},{30,31},{31,30}} | collective-permute-start | bytes 430088 | tf_op jit(solution)/shard_map/ppermute | solution.py:150
  16.1 4.3 %copy.44 = bf16[80,8,2,1280]{3,1,2,0:T(8,128)(2,1)} copy(bf16[80,8,2,1280]{3,2,1,0:T(2,128)(2,1)} %bitcast.112) | data formatting | bytes 6553600
  20.4 1.7 collective-permute-start.9
  22.1 1.3 collective-permute-start.18
  23.4 8.6 %collective-permute-done.1 = bf16[112,1280]{1,0:T(8,128)(2,1)S(1)} collective-permute-done((bf16[112,1280]{1,0:T(8,128)(2,1)S(1)}, bf16[112,1280]{1,0:T(8,128)(2,1)S(1)}, u32[]{:S(2)}, u32[]{:S(2)}) %collective-permute-start.1) | collective-permute-done | bytes 286752 | tf_op jit(solution)/shard_map/ppermute | solution.py:150
  32.2 3.5 %collective-permute-start.7 = (bf16[3,112,640]{2,1,0:T(8,128)(2,1)S(1)}, bf16[3,112,640]{2,1,0:T(8,128)(2,1)S(1)}, u32[]{:S(2)}, u32[]{:S(2)}) collective-permute-start(bf16[3,112,640]{2,1,0:T(8,128)(2,1)S(1)} %get-tuple-element.55), channel_id=1, source_target_pairs={{0,1},{1,0},{10,11},{11,10},{20,21},{21,20},{30,31},{31,30}} | collective-permute-start | bytes 1290248 | tf_op jit(solution)/shard_map/ppermute | solution.py:150
  35.9 1.3 collective-permute-start.19
  37.3 3.4 %collective-permute-done.9.up_ref = bf16[2,128,1280]{2,1,0:T(8,128)(2,1)S(1)} collective-permute-done((bf16[2,128,1280]{2,1,0:T(8,128)(2,1)S(1)}, bf16[2,128,1280]{2,1,0:T(8,128)(2,1)S(1)}, u32[]{:S(2)}, u32[]{:S(2)}) %collective-permute-start.9) | collective-permute-done | bytes 655392 | tf_op jit(solution)/shard_map/ppermute | solution.py:150
  40.7 2.1 %fusion.2 = f32[448,512]{1,0:T(8,128)S(1)} fusion(bf16[448,1280]{1,0:T(8,128)(2,1)S(1)} %pad_maximum_fusion, bf16[1280,256]{1,0:T(8,128)(2,1)} %collective-permute-done.8, bf16[1280,256]{1,0:T(8,128)(2,1)S(1)} %bitcast.141), kind=kOutput, calls=%fused_computation.9 | convolution fusion | flops 589824000 | bytes 3375104 | tf_op jit(solution)/shard_map/dot_general | solution.py:231
  42.8 2.5 %collective-permute-done.7 = bf16[3,112,640]{2,1,0:T(8,128)(2,1)S(1)} collective-permute-done((bf16[3,112,640]{2,1,0:T(8,128)(2,1)S(1)}, bf16[3,112,640]{2,1,0:T(8,128)(2,1)S(1)}, u32[]{:S(2)}, u32[]{:S(2)}) %collective-permute-start.7) | collective-permute-done | bytes 430112 | tf_op jit(solution)/shard_map/ppermute | solution.py:150
  46.3 3.3 %collective-permute-start.3 = (bf16[2,128,1280]{2,1,0:T(8,128)(2,1)S(1)}, bf16[2,128,1280]{2,1,0:T(8,128)(2,1)}, u32[]{:S(2)}, u32[]{:S(2)}) collective-permute-start(bf16[2,128,1280]{2,1,0:T(8,128)(2,1)S(1)} %bitcast.100), channel_id=1, source_target_pairs={{0,2},{1,3},{2,0},{3,1},{4,6},{5,7},{6,4},{7,5},{8,10},{9,11},{10,... | collective-permute-start | bytes 1966088 | tf_op jit(solution)/shard_map/ppermute | solution.py:150
  49.7 4.5 %collective-permute-start.15 = (bf16[2,3,112,640]{3,2,1,0:T(8,128)(2,1)S(1)}, bf16[2,3,112,640]{3,2,1,0:T(8,128)(2,1)S(1)}, u32[]{:S(2)}, u32[]{:S(2)}) collective-permute-start(bf16[2,3,112,640]{3,2,1,0:T(8,128)(2,1)S(1)} %pad_maximum_fusion.2), channel_id=1, source_target_pairs={{0,16},{1,17},{10,26},{11,27},{20,4},{21,5},{30,14},{31,15}} | collective-permute-start | bytes 2580488 | tf_op jit(solution)/shard_map/ppermute | solution.py:150
  54.4 1.5 convolution_convert_fusion.3
  55.9 1.5 collective-permute-start.20
  57.4 9.6 %collective-permute-done.11 = f32[1,112,512]{2,1,0:T(8,128)S(1)} collective-permute-done((f32[1,112,512]{2,1,0:T(8,128)S(1)}, f32[1,112,512]{2,1,0:T(8,128)S(1)}, u32[]{:S(2)}, u32[]{:S(2)}) %collective-permute-start.11) | collective-permute-done | bytes 229408 | tf_op jit(solution)/shard_map/ppermute | solution.py:150
  67.2 2.2 %collective-permute-start.16 = (bf16[2,3,112,640]{3,2,1,0:T(8,128)(2,1)S(1)}, bf16[2,3,112,640]{3,2,1,0:T(8,128)(2,1)}, u32[]{:S(2)}, u32[]{:S(2)}) collective-permute-start(bf16[2,3,112,640]{3,2,1,0:T(8,128)(2,1)S(1)} %broadcast_select_fusion), channel_id=1, source_target_pairs={{0,8},{16,24},{1,9},{17,25},{10,2},{26,18},{11,3},{27,19},{20,28},... | collective-permute-start | bytes 2580488 | tf_op jit(solution)/shard_map/ppermute | solution.py:150
  69.6 2.5 %collective-permute-start.25 = (f32[112]{0:T(128)S(1)}, f32[112]{0:T(128)S(1)}, u32[]{:S(2)}, u32[]{:S(2)}) collective-permute-start(f32[112]{0:T(128)S(1)} %get-tuple-element.41), channel_id=1, source_target_pairs={{0,16},{1,17},{2,18},{3,19},{4,20},{5,21},{6,22},{7,23},{8,24},{9,... | collective-permute-start | bytes 1352 | tf_op jit(solution)/shard_map/ppermute | solution.py:150
  73.8 1.3 collective-permute-start.6
  75.9 2.8 %convolution_add_fusion.refs_8_ = f32[112,2560]{1,0:T(8,128)S(1)} fusion(bf16[640,2560]{1,0:T(8,128)(2,1)} %bitcast.102, bf16[112,2560]{1,0:T(8,128)(2,1)} %collective-permute-done.20, bf16[2,1,112,640]{3,2,1,0:T(8,128)(2,1)S(1)} %broadcast_select_fusion.7), kind=kOutput, calls=%fused_computation | convolution fusion | flops 367575040 | bytes 5140480 | tf_op jit(solution)/shard_map/dot_general | solution.py:209
  78.7 1.3 collective-permute-start.14
  80.0 1.3 collective-permute-start.13
  82.1 1.6 collective-permute-start.21
  84.4 3.0 %collective-permute-done.14 = bf16[112,512]{1,0:T(8,128)(2,1)S(1)} collective-permute-done((bf16[112,512]{1,0:T(8,128)(2,1)S(1)}, bf16[112,512]{1,0:T(8,128)(2,1)S(1)}, u32[]{:S(2)}, u32[]{:S(2)}) %collective-permute-start.14) | collective-permute-done | bytes 114720 | tf_op jit(solution)/shard_map/ppermute | solution.py:150
  87.4 1.3 collective-permute-start.12
  89.3 12.2 %collective-permute-done.13 = bf16[112,512]{1,0:T(8,128)(2,1)S(1)} collective-permute-done((bf16[112,512]{1,0:T(8,128)(2,1)S(1)}, bf16[112,512]{1,0:T(8,128)(2,1)S(1)}, u32[]{:S(2)}, u32[]{:S(2)}) %collective-permute-start.13) | collective-permute-done | bytes 114720 | tf_op jit(solution)/shard_map/ppermute | solution.py:150
  101.5 1.5 collective-permute-start.32
  103.7 4.4 %collective-permute-start.22 = (bf16[4,112,512]{2,1,0:T(8,128)(2,1)S(1)}, bf16[4,112,512]{2,1,0:T(8,128)(2,1)S(1)}, u32[]{:S(2)}, u32[]{:S(2)}) collective-permute-start(bf16[4,112,512]{2,1,0:T(8,128)(2,1)S(1)} %pad_maximum_fusion.4), channel_id=1, source_target_pairs={{0,16},{1,17},{10,26},{11,27},{20,4},{21,5},{30,14},{31,15}} | collective-permute-start | bytes 1376264 | tf_op jit(solution)/shard_map/ppermute | solution.py:150
  108.2 1.5 add_convert_fusion.2
  109.7 1.3 collective-permute-start.29
  111.0 4.6 %collective-permute-done.32 = bf16[112,2560]{1,0:T(8,128)(2,1)S(1)} collective-permute-done((bf16[112,2560]{1,0:T(8,128)(2,1)S(1)}, bf16[112,2560]{1,0:T(8,128)(2,1)S(1)}, u32[]{:S(2)}, u32[]{:S(2)}) %collective-permute-start.32) | collective-permute-done | bytes 573472 | tf_op jit(solution)/shard_map/ppermute | solution.py:150
  115.6 1.5 add_convert_fusion.1
  118.2 9.7 %collective-permute-done.34 = bf16[112,2560]{1,0:T(8,128)(2,1)S(1)} collective-permute-done((bf16[112,2560]{1,0:T(8,128)(2,1)S(1)}, bf16[112,2560]{1,0:T(8,128)(2,1)S(1)}, u32[]{:S(2)}, u32[]{:S(2)}) %collective-permute-start.34) | collective-permute-done | bytes 573472 | tf_op jit(solution)/shard_map/ppermute | solution.py:150
  127.9 1.5 add_convert_fusion
  129.3 1.5 collective-permute-start.28
  130.9 10.1 %collective-permute-done.29 = bf16[2,128,1280]{2,1,0:T(8,128)(2,1)S(1)} collective-permute-done((bf16[2,128,1280]{2,1,0:T(8,128)(2,1)S(1)}, bf16[2,128,1280]{2,1,0:T(8,128)(2,1)S(1)}, u32[]{:S(2)}, u32[]{:S(2)}) %collective-permute-start.29) | collective-permute-done | bytes 655392 | tf_op jit(solution)/shard_map/ppermute | solution.py:150
  141.0 1.9 %collective-permute-start.23 = (bf16[4,112,512]{2,1,0:T(8,128)(2,1)S(1)}, bf16[4,112,512]{2,1,0:T(8,128)(2,1)S(1)}, u32[]{:S(2)}, u32[]{:S(2)}) collective-permute-start(bf16[4,112,512]{2,1,0:T(8,128)(2,1)S(1)} %broadcast_select_fusion.4), channel_id=1, source_target_pairs={{0,8},{16,24},{1,9},{17,25},{10,2},{26,18},{11,3},{27,19},{20,28},... | collective-permute-start | bytes 1376264 | tf_op jit(solution)/shard_map/ppermute | solution.py:150
  143.1 1.1 collective-permute-done.23
  145.1 1.9 %reshape.276 = bf16[4,112,2,2,128]{4,3,2,1,0:T(2,128)(2,1)} reshape(bf16[4,112,512]{2,1,0:T(8,128)(2,1)} %broadcast_select_fusion.5) | data formatting | bytes 917504 | tf_op jit(solution)/shard_map/reshape | solution.py:267
  148.2 2.1 %collective-permute-start.30 = (bf16[2,128,1280]{2,1,0:T(8,128)(2,1)S(1)}, bf16[2,128,1280]{2,1,0:T(8,128)(2,1)S(1)}, u32[]{:S(2)}, u32[]{:S(2)}) collective-permute-start(bf16[2,128,1280]{2,1,0:T(8,128)(2,1)S(1)} %broadcast_select_fusion.2.up_ref), channel_id=1, source_target_pairs={{0,1},{1,0},{2,3},{3,2},{4,5},{5,4},{6,7},{7,6},{8,9},{9,8},{10,11... | collective-permute-start | bytes 1966088 | tf_op jit(solution)/shard_map/ppermute | solution.py:150
  152.5 1.5 shard_map.106.refs_2_
  154.0 1.5 shard_map.109.refs_5_
  155.5 6.6 %collective-permute-done.27.up_ref = bf16[2,128,1280]{2,1,0:T(8,128)(2,1)} collective-permute-done((bf16[2,128,1280]{2,1,0:T(8,128)(2,1)}, bf16[2,128,1280]{2,1,0:T(8,128)(2,1)}, u32[]{:S(2)}, u32[]{:S(2)}) %collective-permute-start.27) | collective-permute-done | bytes 655392 | tf_op jit(solution)/shard_map/ppermute | solution.py:150
  162.1 1.5 shard_map.107.refs_3_
  163.6 11.9 %collective-permute-done.30.up_ref = bf16[2,128,1280]{2,1,0:T(8,128)(2,1)S(1)} collective-permute-done((bf16[2,128,1280]{2,1,0:T(8,128)(2,1)S(1)}, bf16[2,128,1280]{2,1,0:T(8,128)(2,1)S(1)}, u32[]{:S(2)}, u32[]{:S(2)}) %collective-permute-start.30) | collective-permute-done | bytes 655392 | tf_op jit(solution)/shard_map/ppermute | solution.py:150
  176.0 5.7 %shard_map.113 = bf16[7,256,1280]{2,1,0:T(8,128)(2,1)} custom-call(bf16[112,2560]{1,0:T(8,128)(2,1)S(1)} %shard_map.104.refs_0_, bf16[112,2560]{1,0:T(8,128)(2,1)S(1)} %shard_map.105.refs_1_, bf16[112,2560]{1,0:T(8,128)(2,1)S(1)} %shard_map.106.refs_2_, bf16[112,2560]{1,0:T(8,128)(2,1)S(1)} %shard_map.107.refs_3_, bf16[112,2560]{1,0:T(8,128)(2,1)S(1)} %shard_map.108.refs_4_, ...), custom_call_target="tpu_custom_call" | custom-call | flops 1174405120 | bytes 4587520 | tf_op jit(solution)/shard_map/pallas_call | solution.py:75
  181.8 5.7 %shard_map.112 = bf16[7,256,1280]{2,1,0:T(8,128)(2,1)} custom-call(bf16[112,2560]{1,0:T(8,128)(2,1)S(1)} %shard_map.104.refs_0_, bf16[112,2560]{1,0:T(8,128)(2,1)S(1)} %shard_map.105.refs_1_, bf16[112,2560]{1,0:T(8,128)(2,1)S(1)} %shard_map.106.refs_2_, bf16[112,2560]{1,0:T(8,128)(2,1)S(1)} %shard_map.107.refs_3_, bf16[112,2560]{1,0:T(8,128)(2,1)S(1)} %shard_map.108.refs_4_, ...), custom_call_target="tpu_custom_call" | custom-call | flops 1174405120 | bytes 4587520 | tf_op jit(solution)/shard_map/pallas_call | solution.py:75
  (120 shorter events, 18.6 us)
Async XLA Ops:
  2.5 19.6 %collective-permute-start.2 = (bf16[112,1280]{1,0:T(8,128)(2,1)S(1)}, bf16[112,1280]{1,0:T(8,128)(2,1)S(1)}, u32[]{:S(2)}, u32[]{:S(2)}) collective-permute-start(bf16[112,1280]{1,0:T(8,128)(2,1)S(1)} %get-tuple-element.61), channel_id=1, source_target_pairs={{0,6},{1,7},{2,4},{3,5},{4,2},{5,3},{6,0},{7,1},{8,14},{9,15},{10,... | collective-permute-start | bytes 860168 | tf_op jit(solution)/shard_map/ppermute | solution.py:150
  7.6 24.4 %collective-permute-start.1 = (bf16[112,1280]{1,0:T(8,128)(2,1)S(1)}, bf16[112,1280]{1,0:T(8,128)(2,1)S(1)}, u32[]{:S(2)}, u32[]{:S(2)}) collective-permute-start(bf16[112,1280]{1,0:T(8,128)(2,1)S(1)} %get-tuple-element.61), channel_id=1, source_target_pairs={{0,4},{1,5},{2,6},{3,7},{4,0},{5,1},{6,2},{7,3},{8,12},{9,13},{10,... | collective-permute-start | bytes 860168 | tf_op jit(solution)/shard_map/ppermute | solution.py:150
  7.6 24.4 %collective-permute-start = (bf16[112,1280]{1,0:T(8,128)(2,1)S(1)}, bf16[112,1280]{1,0:T(8,128)(2,1)S(1)}, u32[]{:S(2)}, u32[]{:S(2)}) collective-permute-start(bf16[112,1280]{1,0:T(8,128)(2,1)S(1)} %get-tuple-element.61), channel_id=1, source_target_pairs={{0,2},{1,3},{2,0},{3,1},{4,6},{5,7},{6,4},{7,5},{8,10},{9,11},{10,... | collective-permute-start | bytes 860168 | tf_op jit(solution)/shard_map/ppermute | solution.py:150
  8.3 12.1 %collective-permute-start.17 = (bf16[1,112,640]{2,1,0:T(8,128)(2,1)S(1)}, bf16[1,112,640]{2,1,0:T(8,128)(2,1)S(1)}, u32[]{:S(2)}, u32[]{:S(2)}) collective-permute-start(bf16[1,112,640]{2,1,0:T(8,128)(2,1)S(1)} %get-tuple-element.63), channel_id=1, source_target_pairs={{0,1},{1,0},{10,11},{11,10},{20,21},{21,20},{30,31},{31,30}} | collective-permute-start | bytes 430088 | tf_op jit(solution)/shard_map/ppermute | solution.py:150
  11.8 25.4 %collective-permute-start.8 = (bf16[1280,256]{1,0:T(8,128)(2,1)}, bf16[1280,256]{1,0:T(8,128)(2,1)}, u32[]{:S(2)}, u32[]{:S(2)}) collective-permute-start(bf16[1280,256]{1,0:T(8,128)(2,1)} %bitcast.140), channel_id=1, source_target_pairs={{0,1},{1,0},{2,3},{3,2},{4,5},{5,4},{6,7},{7,6},{8,9},{9,8},{10,11... | collective-permute-start | bytes 1966088 | tf_op jit(solution)/shard_map/ppermute | solution.py:150
  16.1 4.3 %copy-start = (bf16[1,2,128,1280]{3,2,1,0:T(8,128)(2,1)S(1)}, bf16[1,2,128,1280]{3,2,1,0:T(8,128)(2,1)}, u32[]{:S(2)}) copy-start(bf16[1,2,128,1280]{3,2,1,0:T(8,128)(2,1)} %param.13) | copy-start | bytes 1966084
  20.4 20.3 %collective-permute-start.9 = (bf16[2,128,1280]{2,1,0:T(8,128)(2,1)S(1)}, bf16[2,128,1280]{2,1,0:T(8,128)(2,1)S(1)}, u32[]{:S(2)}, u32[]{:S(2)}) collective-permute-start(bf16[2,128,1280]{2,1,0:T(8,128)(2,1)S(1)} %bitcast.98), channel_id=1, source_target_pairs={{0,1},{1,0},{2,3},{3,2},{4,5},{5,4},{6,7},{7,6},{8,9},{9,8},{10,11... | collective-permute-start | bytes 1966088 | tf_op jit(solution)/shard_map/ppermute | solution.py:150
  22.1 13.8 %collective-permute-start.18 = (bf16[2,1,112,640]{3,2,1,0:T(8,128)(2,1)S(1)}, bf16[2,1,112,640]{3,2,1,0:T(8,128)(2,1)S(1)}, u32[]{:S(2)}, u32[]{:S(2)}) collective-permute-start(bf16[2,1,112,640]{3,2,1,0:T(8,128)(2,1)S(1)} %pad_maximum_fusion.5), channel_id=1, source_target_pairs={{0,16},{1,17},{10,26},{11,27},{20,4},{21,5},{30,14},{31,15}} | collective-permute-start | bytes 860168 | tf_op jit(solution)/shard_map/ppermute | solution.py:150
  32.1 8.6 %copy-start.8 = (bf16[1,1280,256]{2,1,0:T(8,128)(2,1)S(1)}, bf16[1,1280,256]{2,1,0:T(8,128)(2,1)}, u32[]{:S(2)}) copy-start(bf16[1,1280,256]{2,1,0:T(8,128)(2,1)} %param.12) | copy-start | bytes 1966084
  32.2 13.1 %collective-permute-start.7 = (bf16[3,112,640]{2,1,0:T(8,128)(2,1)S(1)}, bf16[3,112,640]{2,1,0:T(8,128)(2,1)S(1)}, u32[]{:S(2)}, u32[]{:S(2)}) collective-permute-start(bf16[3,112,640]{2,1,0:T(8,128)(2,1)S(1)} %get-tuple-element.55), channel_id=1, source_target_pairs={{0,1},{1,0},{10,11},{11,10},{20,21},{21,20},{30,31},{31,30}} | collective-permute-start | bytes 1290248 | tf_op jit(solution)/shard_map/ppermute | solution.py:150
  35.9 18.2 %collective-permute-start.19 = (bf16[2,1,112,640]{3,2,1,0:T(8,128)(2,1)S(1)}, bf16[2,1,112,640]{3,2,1,0:T(8,128)(2,1)S(1)}, u32[]{:S(2)}, u32[]{:S(2)}) collective-permute-start(bf16[2,1,112,640]{3,2,1,0:T(8,128)(2,1)S(1)} %broadcast_select_fusion.6), channel_id=1, source_target_pairs={{0,8},{16,24},{1,9},{17,25},{10,2},{26,18},{11,3},{27,19},{20,28},... | collective-permute-start | bytes 860168 | tf_op jit(solution)/shard_map/ppermute | solution.py:150
  40.7 2.1 %copy-start.2 = (bf16[2,128,1280]{2,1,0:T(8,128)(2,1)}, bf16[2,128,1280]{2,1,0:T(8,128)(2,1)S(1)}, u32[]{:S(2)}) copy-start(bf16[2,128,1280]{2,1,0:T(8,128)(2,1)S(1)} %collective-permute-done.9.up_ref) | copy-start | bytes 1966084
  45.3 9.0 %copy-start.4 = (bf16[80,8,2,1280]{3,1,2,0:T(8,128)(2,1)S(1)}, bf16[80,8,2,1280]{3,1,2,0:T(8,128)(2,1)}, u32[]{:S(2)}) copy-start(bf16[80,8,2,1280]{3,1,2,0:T(8,128)(2,1)} %copy.44) | copy-start | bytes 9830404
  45.4 8.8 %collective-permute-start.10 = (f32[2,112,512]{2,1,0:T(8,128)S(1)}, f32[2,112,512]{2,1,0:T(8,128)S(1)}, u32[]{:S(2)}, u32[]{:S(2)}) collective-permute-start(f32[2,112,512]{2,1,0:T(8,128)S(1)} %pad_maximum_fusion.3), channel_id=1, source_target_pairs={{0,8},{1,9},{2,10},{3,11},{4,12},{5,13},{6,14},{7,15},{8,0},{9,1},... | collective-permute-start | bytes 1376264 | tf_op jit(solution)/shard_map/ppermute | solution.py:150
  45.5 21.7 %collective-permute-start.5 = (bf16[2,128,1280]{2,1,0:T(8,128)(2,1)S(1)}, bf16[2,128,1280]{2,1,0:T(8,128)(2,1)S(1)}, u32[]{:S(2)}, u32[]{:S(2)}) collective-permute-start(bf16[2,128,1280]{2,1,0:T(8,128)(2,1)S(1)} %bitcast.99), channel_id=1, source_target_pairs={{2,4},{3,5},{4,2},{5,3},{10,12},{11,13},{12,10},{13,11},{18,20},{1... | collective-permute-start | bytes 1966088 | tf_op jit(solution)/shard_map/ppermute | solution.py:150
  46.3 20.9 %collective-permute-start.3 = (bf16[2,128,1280]{2,1,0:T(8,128)(2,1)S(1)}, bf16[2,128,1280]{2,1,0:T(8,128)(2,1)}, u32[]{:S(2)}, u32[]{:S(2)}) collective-permute-start(bf16[2,128,1280]{2,1,0:T(8,128)(2,1)S(1)} %bitcast.100), channel_id=1, source_target_pairs={{0,2},{1,3},{2,0},{3,1},{4,6},{5,7},{6,4},{7,5},{8,10},{9,11},{10,... | collective-permute-start | bytes 1966088 | tf_op jit(solution)/shard_map/ppermute | solution.py:150
  49.7 17.4 %collective-permute-start.15 = (bf16[2,3,112,640]{3,2,1,0:T(8,128)(2,1)S(1)}, bf16[2,3,112,640]{3,2,1,0:T(8,128)(2,1)S(1)}, u32[]{:S(2)}, u32[]{:S(2)}) collective-permute-start(bf16[2,3,112,640]{3,2,1,0:T(8,128)(2,1)S(1)} %pad_maximum_fusion.2), channel_id=1, source_target_pairs={{0,16},{1,17},{10,26},{11,27},{20,4},{21,5},{30,14},{31,15}} | collective-permute-start | bytes 2580488 | tf_op jit(solution)/shard_map/ppermute | solution.py:150
  54.3 12.7 %collective-permute-start.11 = (f32[1,112,512]{2,1,0:T(8,128)S(1)}, f32[1,112,512]{2,1,0:T(8,128)S(1)}, u32[]{:S(2)}, u32[]{:S(2)}) collective-permute-start(f32[1,112,512]{2,1,0:T(8,128)S(1)} %slice_add_fusion), channel_id=1, source_target_pairs={{0,16},{1,17},{2,18},{3,19},{4,20},{5,21},{6,22},{7,23},{8,24},{9,... | collective-permute-start | bytes 688136 | tf_op jit(solution)/shard_map/ppermute | solution.py:150
  55.9 20.0 %collective-permute-start.20 = (bf16[112,2560]{1,0:T(8,128)(2,1)}, bf16[112,2560]{1,0:T(8,128)(2,1)}, u32[]{:S(2)}, u32[]{:S(2)}) collective-permute-start(bf16[112,2560]{1,0:T(8,128)(2,1)} %convolution_convert_fusion.3), channel_id=1, source_target_pairs={{0,1},{1,0},{2,3},{3,2},{4,5},{5,4},{6,7},{7,6},{8,9},{9,8},{10,11... | collective-permute-start | bytes 1720328 | tf_op jit(solution)/shard_map/ppermute | solution.py:150
  67.2 6.5 %copy-start.6 = (bf16[2,128,1280]{2,1,0:T(8,128)(2,1)}, bf16[2,128,1280]{2,1,0:T(8,128)(2,1)S(1)}, u32[]{:S(2)}) copy-start(bf16[2,128,1280]{2,1,0:T(8,128)(2,1)S(1)} %collective-permute-done.5) | copy-start | bytes 1966084
  67.2 14.1 %collective-permute-start.16 = (bf16[2,3,112,640]{3,2,1,0:T(8,128)(2,1)S(1)}, bf16[2,3,112,640]{3,2,1,0:T(8,128)(2,1)}, u32[]{:S(2)}, u32[]{:S(2)}) collective-permute-start(bf16[2,3,112,640]{3,2,1,0:T(8,128)(2,1)S(1)} %broadcast_select_fusion), channel_id=1, source_target_pairs={{0,8},{16,24},{1,9},{17,25},{10,2},{26,18},{11,3},{27,19},{20,28},... | collective-permute-start | bytes 2580488 | tf_op jit(solution)/shard_map/ppermute | solution.py:150
  69.6 3.5 %collective-permute-start.26 = (f32[112]{0:T(128)S(1)}, f32[112]{0:T(128)S(1)}, u32[]{:S(2)}, u32[]{:S(2)}) collective-permute-start(f32[112]{0:T(128)S(1)} %get-tuple-element.41), channel_id=1, source_target_pairs={{0,24},{1,25},{2,26},{3,27},{4,28},{5,29},{6,30},{7,31},{8,16},{9,... | collective-permute-start | bytes 1352 | tf_op jit(solution)/shard_map/ppermute | solution.py:150
  69.6 4.1 %collective-permute-start.25 = (f32[112]{0:T(128)S(1)}, f32[112]{0:T(128)S(1)}, u32[]{:S(2)}, u32[]{:S(2)}) collective-permute-start(f32[112]{0:T(128)S(1)} %get-tuple-element.41), channel_id=1, source_target_pairs={{0,16},{1,17},{2,18},{3,19},{4,20},{5,21},{6,22},{7,23},{8,24},{9,... | collective-permute-start | bytes 1352 | tf_op jit(solution)/shard_map/ppermute | solution.py:150
  72.2 1.5 collective-permute-start.24
  73.8 29.7 %collective-permute-start.6 = (bf16[2,128,1280]{2,1,0:T(8,128)(2,1)}, bf16[2,128,1280]{2,1,0:T(8,128)(2,1)S(1)}, u32[]{:S(2)}, u32[]{:S(2)}) collective-permute-start(bf16[2,128,1280]{2,1,0:T(8,128)(2,1)} %copy-done.6), channel_id=1, source_target_pairs={{2,0},{3,1},{4,6},{5,7},{10,8},{11,9},{12,14},{13,15},{18,16},{19,... | collective-permute-start | bytes 1966088 | tf_op jit(solution)/shard_map/ppermute | solution.py:150
  75.1 28.4 %collective-permute-start.4 = (bf16[2,128,1280]{2,1,0:T(8,128)(2,1)}, bf16[2,128,1280]{2,1,0:T(8,128)(2,1)S(1)}, u32[]{:S(2)}, u32[]{:S(2)}) collective-permute-start(bf16[2,128,1280]{2,1,0:T(8,128)(2,1)} %collective-permute-done.3.up_ref), channel_id=1, source_target_pairs={{2,4},{3,5},{4,2},{5,3},{10,12},{11,13},{12,10},{13,11},{18,20},{1... | collective-permute-start | bytes 1966088 | tf_op jit(solution)/shard_map/ppermute | solution.py:150
  75.8 5.6 %copy-start.5 = (bf16[80,8,2,1280]{3,1,2,0:T(8,128)(2,1)S(1)}, bf16[80,8,2,1280]{3,1,2,0:T(8,128)(2,1)}, u32[]{:S(2)}) copy-start(bf16[80,8,2,1280]{3,1,2,0:T(8,128)(2,1)} %copy.44) | copy-start | bytes 9830404
  78.7 8.6 %collective-permute-start.14 = (bf16[112,512]{1,0:T(8,128)(2,1)S(1)}, bf16[112,512]{1,0:T(8,128)(2,1)S(1)}, u32[]{:S(2)}, u32[]{:S(2)}) collective-permute-start(bf16[112,512]{1,0:T(8,128)(2,1)S(1)} %fusion.31), channel_id=1, source_target_pairs={{6,0},{7,1},{12,10},{13,11},{18,20},{19,21},{24,30},{25,31}} | collective-permute-start | bytes 344072 | tf_op jit(solution)/shard_map/ppermute | solution.py:150
  80.0 21.5 %collective-permute-start.13 = (bf16[112,512]{1,0:T(8,128)(2,1)S(1)}, bf16[112,512]{1,0:T(8,128)(2,1)S(1)}, u32[]{:S(2)}, u32[]{:S(2)}) collective-permute-start(bf16[112,512]{1,0:T(8,128)(2,1)S(1)} %fusion.31), channel_id=1, source_target_pairs={{4,0},{5,1},{14,10},{15,11},{16,20},{17,21},{26,30},{27,31}} | collective-permute-start | bytes 344072 | tf_op jit(solution)/shard_map/ppermute | solution.py:150
  82.1 21.4 %collective-permute-start.21 = (bf16[112,2560]{1,0:T(8,128)(2,1)S(1)}, bf16[112,2560]{1,0:T(8,128)(2,1)S(1)}, u32[]{:S(2)}, u32[]{:S(2)}) collective-permute-start(bf16[112,2560]{1,0:T(8,128)(2,1)S(1)} %convolution_convert_fusion.2), channel_id=1, source_target_pairs={{0,1},{1,0},{2,3},{3,2},{4,5},{5,4},{6,7},{7,6},{8,9},{9,8},{10,11... | collective-permute-start | bytes 1720328 | tf_op jit(solution)/shard_map/ppermute | solution.py:150
  84.3 19.2 %copy-start.7 = (bf16[2,128,1280]{2,1,0:T(8,128)(2,1)S(1)}, bf16[2,128,1280]{2,1,0:T(8,128)(2,1)}, u32[]{:S(2)}) copy-start(bf16[2,128,1280]{2,1,0:T(8,128)(2,1)} %copy-done.6) | copy-start | bytes 1966084
  87.4 15.7 %collective-permute-start.12 = (bf16[112,512]{1,0:T(8,128)(2,1)S(1)}, bf16[112,512]{1,0:T(8,128)(2,1)S(1)}, u32[]{:S(2)}, u32[]{:S(2)}) collective-permute-start(bf16[112,512]{1,0:T(8,128)(2,1)S(1)} %fusion.31), channel_id=1, source_target_pairs={{2,0},{3,1},{8,10},{9,11},{22,20},{23,21},{28,30},{29,31}} | collective-permute-start | bytes 344072 | tf_op jit(solution)/shard_map/ppermute | solution.py:150
  101.5 14.1 %collective-permute-start.32 = (bf16[112,2560]{1,0:T(8,128)(2,1)S(1)}, bf16[112,2560]{1,0:T(8,128)(2,1)S(1)}, u32[]{:S(2)}, u32[]{:S(2)}) collective-permute-start(bf16[112,2560]{1,0:T(8,128)(2,1)S(1)} %convolution_convert_fusion.1), channel_id=1, source_target_pairs={{0,1},{1,0},{2,3},{3,2},{4,5},{5,4},{6,7},{7,6},{8,9},{9,8},{10,11... | collective-permute-start | bytes 1720328 | tf_op jit(solution)/shard_map/ppermute | solution.py:150
  103.0 24.8 %collective-permute-start.34 = (bf16[112,2560]{1,0:T(8,128)(2,1)S(1)}, bf16[112,2560]{1,0:T(8,128)(2,1)S(1)}, u32[]{:S(2)}, u32[]{:S(2)}) collective-permute-start(bf16[112,2560]{1,0:T(8,128)(2,1)S(1)} %convolution_convert_fusion), channel_id=1, source_target_pairs={{0,1},{1,0},{2,3},{3,2},{4,5},{5,4},{6,7},{7,6},{8,9},{9,8},{10,11... | collective-permute-start | bytes 1720328 | tf_op jit(solution)/shard_map/ppermute | solution.py:150
  103.7 25.6 %collective-permute-start.22 = (bf16[4,112,512]{2,1,0:T(8,128)(2,1)S(1)}, bf16[4,112,512]{2,1,0:T(8,128)(2,1)S(1)}, u32[]{:S(2)}, u32[]{:S(2)}) collective-permute-start(bf16[4,112,512]{2,1,0:T(8,128)(2,1)S(1)} %pad_maximum_fusion.4), channel_id=1, source_target_pairs={{0,16},{1,17},{10,26},{11,27},{20,4},{21,5},{30,14},{31,15}} | collective-permute-start | bytes 1376264 | tf_op jit(solution)/shard_map/ppermute | solution.py:150
  109.7 66.3 %collective-permute-start.31 = (bf16[112,2560]{1,0:T(8,128)(2,1)}, bf16[112,2560]{1,0:T(8,128)(2,1)}, u32[]{:S(2)}, u32[]{:S(2)}) collective-permute-start(bf16[112,2560]{1,0:T(8,128)(2,1)} %add_convert_fusion.2), channel_id=1, source_target_pairs={{0,6},{1,7},{2,4},{3,5},{4,2},{5,3},{6,0},{7,1},{8,14},{9,15},{10,... | collective-permute-start | bytes 1720328 | tf_op jit(solution)/shard_map/ppermute | solution.py:150
  109.7 31.4 %collective-permute-start.29 = (bf16[2,128,1280]{2,1,0:T(8,128)(2,1)S(1)}, bf16[2,128,1280]{2,1,0:T(8,128)(2,1)S(1)}, u32[]{:S(2)}, u32[]{:S(2)}) collective-permute-start(bf16[2,128,1280]{2,1,0:T(8,128)(2,1)S(1)} %collective-permute-done.4), channel_id=1, source_target_pairs={{2,0},{3,1},{4,6},{5,7},{10,8},{11,9},{12,14},{13,15},{18,16},{19,... | collective-permute-start | bytes 1966088 | tf_op jit(solution)/shard_map/ppermute | solution.py:150
  117.1 58.9 %collective-permute-start.33 = (bf16[112,2560]{1,0:T(8,128)(2,1)}, bf16[112,2560]{1,0:T(8,128)(2,1)}, u32[]{:S(2)}, u32[]{:S(2)}) collective-permute-start(bf16[112,2560]{1,0:T(8,128)(2,1)} %add_convert_fusion.1), channel_id=1, source_target_pairs={{0,4},{1,5},{2,6},{3,7},{4,0},{5,1},{6,2},{7,3},{8,12},{9,13},{10,... | collective-permute-start | bytes 1720328 | tf_op jit(solution)/shard_map/ppermute | solution.py:150
  129.3 46.7 %collective-permute-start.35 = (bf16[112,2560]{1,0:T(8,128)(2,1)}, bf16[112,2560]{1,0:T(8,128)(2,1)}, u32[]{:S(2)}, u32[]{:S(2)}) collective-permute-start(bf16[112,2560]{1,0:T(8,128)(2,1)} %add_convert_fusion), channel_id=1, source_target_pairs={{0,2},{1,3},{2,0},{3,1},{4,6},{5,7},{6,4},{7,5},{8,10},{9,11},{10,... | collective-permute-start | bytes 1720328 | tf_op jit(solution)/shard_map/ppermute | solution.py:150
  129.3 18.8 %collective-permute-start.28 = (bf16[2,128,1280]{2,1,0:T(8,128)(2,1)S(1)}, bf16[2,128,1280]{2,1,0:T(8,128)(2,1)}, u32[]{:S(2)}, u32[]{:S(2)}) collective-permute-start(bf16[2,128,1280]{2,1,0:T(8,128)(2,1)S(1)} %broadcast_select_fusion.3.up_ref), channel_id=1, source_target_pairs={{0,1},{1,0},{2,3},{3,2},{4,5},{5,4},{6,7},{7,6},{8,9},{9,8},{10,11... | collective-permute-start | bytes 1966088 | tf_op jit(solution)/shard_map/ppermute | solution.py:150
  141.0 3.2 %collective-permute-start.23 = (bf16[4,112,512]{2,1,0:T(8,128)(2,1)S(1)}, bf16[4,112,512]{2,1,0:T(8,128)(2,1)S(1)}, u32[]{:S(2)}, u32[]{:S(2)}) collective-permute-start(bf16[4,112,512]{2,1,0:T(8,128)(2,1)S(1)} %broadcast_select_fusion.4), channel_id=1, source_target_pairs={{0,8},{16,24},{1,9},{17,25},{10,2},{26,18},{11,3},{27,19},{20,28},... | collective-permute-start | bytes 1376264 | tf_op jit(solution)/shard_map/ppermute | solution.py:150
  144.2 17.9 %collective-permute-start.27 = (bf16[2,128,1280]{2,1,0:T(8,128)(2,1)}, bf16[2,128,1280]{2,1,0:T(8,128)(2,1)}, u32[]{:S(2)}, u32[]{:S(2)}) collective-permute-start(bf16[2,128,1280]{2,1,0:T(8,128)(2,1)} %collective-permute-done.3.up_ref), channel_id=1, source_target_pairs={{0,1},{1,0},{2,3},{3,2},{4,5},{5,4},{6,7},{7,6},{8,9},{9,8},{10,11... | collective-permute-start | bytes 1966088 | tf_op jit(solution)/shard_map/ppermute | solution.py:150
  148.1 2.8 %copy-start.1 = (bf16[1,2,128,1280]{3,2,1,0:T(8,128)(2,1)S(1)}, bf16[1,2,128,1280]{3,2,1,0:T(8,128)(2,1)}, u32[]{:S(2)}) copy-start(bf16[1,2,128,1280]{3,2,1,0:T(8,128)(2,1)} %param.13) | copy-start | bytes 1966084
  148.2 27.3 %collective-permute-start.30 = (bf16[2,128,1280]{2,1,0:T(8,128)(2,1)S(1)}, bf16[2,128,1280]{2,1,0:T(8,128)(2,1)S(1)}, u32[]{:S(2)}, u32[]{:S(2)}) collective-permute-start(bf16[2,128,1280]{2,1,0:T(8,128)(2,1)S(1)} %broadcast_select_fusion.2.up_ref), channel_id=1, source_target_pairs={{0,1},{1,0},{2,3},{3,2},{4,5},{5,4},{6,7},{7,6},{8,9},{9,8},{10,11... | collective-permute-start | bytes 1966088 | tf_op jit(solution)/shard_map/ppermute | solution.py:150
  150.3 1.6 copy-start.3

commit v3 on v2

--- a/solution.py
+++ b/solution.py
@@ -69,7 +69,7 @@
 def mix(deltas, bases, scale, pick, half):
     tokens, width = deltas[0].shape[0], deltas[0].shape[1] // 2
     groups, rows, depth = pick.shape
-    block = 256 if width % 256 == 0 else 128
+    block = next(n for n in (640, 256, 128) if width % n == 0)
     steps = width // block
     column = pl.BlockSpec((tokens, block), lambda i: (0, half * steps + i))
     out = pl.pallas_call(
@@ -218,7 +218,8 @@
     late = lax.optimization_barrier((up_own, *rest))
     up_late, rest = late[0], late[1:]
     if lines == 4:
-        near = to_line(up_late, 1)
+        near = to_line(jnp.stack([up_late, up_other]), 1)
+        near, near_other = near[0], near[1]
         far_near = send(up_late, across)
     else:
         near = to_line(up_late, 1)
@@ -245,7 +246,7 @@
         bit *= 2
     held = parts[0].astype(jnp.bfloat16)
 
-    both = over_rows(jnp.stack([mine, got]), held, near, far_near)
+    both = over_rows(jnp.stack([mine, got]), held)
     both = after(both, own_out)
     outs = [product(both[1, k]).astype(jnp.bfloat16) for k in range(lines - 1)]
     kept = [product(both[0, k]) for k in range(lines - 1)]
@@ -260,9 +261,11 @@
         far_far, first, *ranks = lax.optimization_barrier((far_far, first, *ranks, came[-1]))[:-1]
         last = jnp.where(inner, far_far, send(far_far, outward))
         first = jnp.where(inner, far_near, first)
-        blocks = [near, first, last]
+        blocks = [first, last]
+        ups = [up_own, up_other, near, near_other]
     else:
         blocks = [near] + [to_line(up_own, k) for k in range(2, lines)]
+        ups = [up_own, up_other]
     ranks = over_rows(jnp.stack(ranks))
     ranks = ranks.reshape(lines, tokens, 2, 2, low_rank).transpose(0, 2, 3, 1, 4)
     ranks = ranks.reshape(adapters, 2, tokens, low_rank)
@@ -270,7 +273,6 @@
         far = jnp.where(inner, jnp.concatenate([ranks[6:], ranks[4:6]]), ranks[4:])
         ranks = jnp.concatenate([ranks[:4], far])
 
-    ups = [up_own, up_other]
     for value in blocks:
         ups += [value, to_side(after(value, came[-1]))]
 

time: 189 us -> 166 us (0.88)
  waiting for transfers between devices: 84.1 us -> 53.8 us
  other arithmetic: 7.38 us -> 13.8 us
  matrix products: 12.8 us -> 10.5 us
  local copies, waits for them, and re-layouts: 8.69 us -> 10.9 us
    ppermute x36 -> x35, waiting for transfers between devices: 84.1 us -> 53.8 us  [send(): return lax.ppermute(value, ('row', 'col'), flat)]
    squeeze x0 -> x1, local copies, waits for them, and re-layouts: none -> 2.21 us  [body(): near, near_other = (near[0], near[1])]
    another operation x2 -> x3, other arithmetic: 0.93 us -> 3.01 us  [the longest x1 1.17 us: body(): near = to_line(jnp.stack([up_late, up_other]), 1)]
    pallas_call x2, Pallas kernels: 11.5 us -> 9.42 us  [mix(): pl.pallas_call(functools.partial(mix_kernel, adapters=len(deltas), parts=...]
    ppermute x36 -> x35, starting transfers between devices: 54.6 us -> 55.8 us  [send(): return lax.ppermute(value, ('row', 'col'), flat)]
    unnamed x19 -> x35, local copies, waits for them, and re-layouts: 4.3 us -> 4.26 us
  transfers between devices with their start and end apart: 36 -> 35, of which waited for: 13 -> 12; matrix products, arithmetic and copies ran while one was open for 14% -> 20% of each run, Pallas kernels for 4% -> 5%
where the time goes in v3:
time: 166 us; the launch traced here: 164 us
  starting transfers between devices  55.8 us (34%)
  waiting for transfers between devices  53.8 us (32%)
  Pallas kernels  17.5 us (11%)
  other arithmetic  13.8 us (8%)
  local copies, waits for them, and re-layouts  10.9 us (7%)
  matrix products  10.5 us (6%)
    ppermute x35, starting transfers between devices, send(): return lax.ppermute(value, ('row', 'col'), flat)  55.8 us
    ppermute x35, waiting for transfers between devices, send(): return lax.ppermute(value, ('row', 'col'), flat)  53.8 us
    dot_general x8, matrix products, product(): return jnp.dot(value, weight, preferred_element_type=jnp.float32)  9.72 us
    pallas_call x2, Pallas kernels, mix(): pl.pallas_call(functools.partial(mix_kernel, adapters=len(deltas), parts=...  9.42 us
    pallas_call x8, Pallas kernels, corrections(): pl.pallas_call(delta_kernel, grid=(2,), in_specs=[pl.BlockSpec((1, tokens...  8.09 us
    unnamed x35, local copies, waits for them, and re-layouts  4.26 us
  transfers between devices with their start and end apart: 35, of which 12 were waited for; matrix products, arithmetic and copies ran while one was open for 20% of the time, Pallas kernels for 5%

profile of v3, /device:TPU:0, one launch (start us, length us, event | category | flops | bytes accessed | tf_op | source)
XLA Modules:
  0.0 163.7 jit_solution(10265284286121976510)
XLA Ops:
  2.5 5.1 %collective-permute-start.2 = (bf16[112,1280]{1,0:T(8,128)(2,1)S(1)}, bf16[112,1280]{1,0:T(8,128)(2,1)S(1)}, u32[]{:S(2)}, u32[]{:S(2)}) collective-permute-start(bf16[112,1280]{1,0:T(8,128)(2,1)S(1)} %get-tuple-element.61), channel_id=1, source_target_pairs={{0,6},{1,7},{2,4},{3,5},{4,2},{5,3},{6,0},{7,1},{8,14},{9,15},{10,... | collective-permute-start | bytes 860168 | tf_op jit(solution)/shard_map/ppermute | solution.py:150
  8.3 3.6 %collective-permute-start.17 = (bf16[1,112,640]{2,1,0:T(8,128)(2,1)S(1)}, bf16[1,112,640]{2,1,0:T(8,128)(2,1)S(1)}, u32[]{:S(2)}, u32[]{:S(2)}) collective-permute-start(bf16[1,112,640]{2,1,0:T(8,128)(2,1)S(1)} %get-tuple-element.63), channel_id=1, source_target_pairs={{0,1},{1,0},{10,11},{11,10},{20,21},{21,20},{30,31},{31,30}} | collective-permute-start | bytes 430088 | tf_op jit(solution)/shard_map/ppermute | solution.py:150
  15.4 4.2 %copy.44 = bf16[80,8,2,1280]{3,1,2,0:T(8,128)(2,1)} copy(bf16[80,8,2,1280]{3,2,1,0:T(2,128)(2,1)} %bitcast.118) | data formatting | bytes 6553600
  20.5 1.7 %collective-permute-start.9 = (bf16[1280,256]{1,0:T(8,128)(2,1)}, bf16[1280,256]{1,0:T(8,128)(2,1)S(1)}, u32[]{:S(2)}, u32[]{:S(2)}) collective-permute-start(bf16[1280,256]{1,0:T(8,128)(2,1)} %bitcast.145), channel_id=1, source_target_pairs={{0,1},{1,0},{2,3},{3,2},{4,5},{5,4},{6,7},{7,6},{8,9},{9,8},{10,11... | collective-permute-start | bytes 1966088 | tf_op jit(solution)/shard_map/ppermute | solution.py:150
  22.3 1.3 collective-permute-start.18
  23.6 8.4 %collective-permute-done.1 = bf16[112,1280]{1,0:T(8,128)(2,1)S(1)} collective-permute-done((bf16[112,1280]{1,0:T(8,128)(2,1)S(1)}, bf16[112,1280]{1,0:T(8,128)(2,1)S(1)}, u32[]{:S(2)}, u32[]{:S(2)}) %collective-permute-start.1) | collective-permute-done | bytes 286752 | tf_op jit(solution)/shard_map/ppermute | solution.py:150
  32.0 1.5 collective-permute-start.6
  34.8 3.5 %collective-permute-start.8 = (bf16[3,112,640]{2,1,0:T(8,128)(2,1)S(1)}, bf16[3,112,640]{2,1,0:T(8,128)(2,1)S(1)}, u32[]{:S(2)}, u32[]{:S(2)}) collective-permute-start(bf16[3,112,640]{2,1,0:T(8,128)(2,1)S(1)} %get-tuple-element.55), channel_id=1, source_target_pairs={{0,1},{1,0},{10,11},{11,10},{20,21},{21,20},{30,31},{31,30}} | collective-permute-start | bytes 1290248 | tf_op jit(solution)/shard_map/ppermute | solution.py:150
  39.6 1.3 collective-permute-start.19
  41.7 3.7 %collective-permute-done.8 = bf16[3,112,640]{2,1,0:T(8,128)(2,1)S(1)} collective-permute-done((bf16[3,112,640]{2,1,0:T(8,128)(2,1)S(1)}, bf16[3,112,640]{2,1,0:T(8,128)(2,1)S(1)}, u32[]{:S(2)}, u32[]{:S(2)}) %collective-permute-start.8) | collective-permute-done | bytes 430112 | tf_op jit(solution)/shard_map/ppermute | solution.py:150
  46.7 2.5 %collective-permute-start.4 = (bf16[2,2,128,1280]{3,2,1,0:T(8,128)(2,1)}, bf16[2,2,128,1280]{3,2,1,0:T(8,128)(2,1)}, u32[]{:S(2)}, u32[]{:S(2)}) collective-permute-start(bf16[2,2,128,1280]{3,2,1,0:T(8,128)(2,1)} %pad_maximum_fusion), channel_id=1, source_target_pairs={{0,2},{1,3},{2,0},{3,1},{4,6},{5,7},{6,4},{7,5},{8,10},{9,11},{10,... | collective-permute-start | bytes 3932168 | tf_op jit(solution)/shard_map/ppermute | solution.py:150
  50.2 1.4 collective-permute-start.25
  51.7 3.5 %collective-permute-start.15 = (bf16[2,3,112,640]{3,2,1,0:T(8,128)(2,1)}, bf16[2,3,112,640]{3,2,1,0:T(8,128)(2,1)}, u32[]{:S(2)}, u32[]{:S(2)}) collective-permute-start(bf16[2,3,112,640]{3,2,1,0:T(8,128)(2,1)} %pad_maximum_fusion.3), channel_id=1, source_target_pairs={{0,16},{1,17},{10,26},{11,27},{20,4},{21,5},{30,14},{31,15}} | collective-permute-start | bytes 2580488 | tf_op jit(solution)/shard_map/ppermute | solution.py:150
  55.4 1.5 convolution_convert_fusion.3
  56.9 1.5 collective-permute-start.20
  58.5 1.3 collective-permute-start.7
  59.8 9.8 %collective-permute-done.11 = f32[1,112,512]{2,1,0:T(8,128)} collective-permute-done((f32[1,112,512]{2,1,0:T(8,128)S(1)}, f32[1,112,512]{2,1,0:T(8,128)}, u32[]{:S(2)}, u32[]{:S(2)}) %collective-permute-start.11) | collective-permute-done | bytes 229408 | tf_op jit(solution)/shard_map/ppermute | solution.py:150
  69.7 1.4 fusion.31
  71.2 1.3 collective-permute-start.16
  72.5 1.8 %convolution_add_fusion.refs_8_ = f32[112,2560]{1,0:T(8,128)S(1)} fusion(bf16[640,2560]{1,0:T(8,128)(2,1)S(1)} %bitcast.109, bf16[112,2560]{1,0:T(8,128)(2,1)} %collective-permute-done.20, bf16[2,1,112,640]{3,2,1,0:T(8,128)(2,1)} %copy-done.11), kind=kOutput, calls=%fused_computation | convolution fusion | flops 367575040 | bytes 5140480 | tf_op jit(solution)/shard_map/dot_general | solution.py:209
  74.4 1.3 collective-permute-start.14
  75.7 1.3 collective-permute-start.13
  77.0 2.1 %collective-permute-done.4 = bf16[2,2,128,1280]{3,2,1,0:T(8,128)(2,1)} collective-permute-done((bf16[2,2,128,1280]{3,2,1,0:T(8,128)(2,1)}, bf16[2,2,128,1280]{3,2,1,0:T(8,128)(2,1)}, u32[]{:S(2)}, u32[]{:S(2)}) %collective-permute-start.4) | collective-permute-done | bytes 1310752 | tf_op jit(solution)/shard_map/ppermute | solution.py:150
  79.1 2.2 %slice_bitcast_fusion = (bf16[2,128,1280]{2,1,0:T(8,128)(2,1)}, bf16[2,128,1280]{2,1,0:T(8,128)(2,1)S(1)}) fusion(bf16[2,2,128,1280]{3,2,1,0:T(8,128)(2,1)} %collective-permute-done.4), kind=kLoop, calls=%fused_computation.26 | loop fusion | bytes 2621440 | tf_op jit(solution)/shard_map/squeeze | solution.py:222
  82.8 1.6 collective-permute-start.21
  85.0 1.3 collective-permute-start.12
  87.6 8.5 %collective-permute-done.12 = bf16[112,512]{1,0:T(8,128)(2,1)S(1)} collective-permute-done((bf16[112,512]{1,0:T(8,128)(2,1)S(1)}, bf16[112,512]{1,0:T(8,128)(2,1)S(1)}, u32[]{:S(2)}, u32[]{:S(2)}) %collective-permute-start.12) | collective-permute-done | bytes 114720 | tf_op jit(solution)/shard_map/ppermute | solution.py:150
  96.1 1.5 collective-permute-start.33
  99.8 4.2 %collective-permute-start.22 = (bf16[4,112,512]{2,1,0:T(8,128)(2,1)S(1)}, bf16[4,112,512]{2,1,0:T(8,128)(2,1)S(1)}, u32[]{:S(2)}, u32[]{:S(2)}) collective-permute-start(bf16[4,112,512]{2,1,0:T(8,128)(2,1)S(1)} %pad_maximum_fusion.5), channel_id=1, source_target_pairs={{0,16},{1,17},{10,26},{11,27},{20,4},{21,5},{30,14},{31,15}} | collective-permute-start | bytes 1376264 | tf_op jit(solution)/shard_map/ppermute | solution.py:150
  104.0 1.5 add_convert_fusion.2
  106.8 4.3 %collective-permute-done.31 = bf16[112,2560]{1,0:T(8,128)(2,1)S(1)} collective-permute-done((bf16[112,2560]{1,0:T(8,128)(2,1)S(1)}, bf16[112,2560]{1,0:T(8,128)(2,1)S(1)}, u32[]{:S(2)}, u32[]{:S(2)}) %collective-permute-start.31) | collective-permute-done | bytes 573472 | tf_op jit(solution)/shard_map/ppermute | solution.py:150
  111.1 1.5 add_convert_fusion.1
  112.5 4.0 %collective-permute-start.32 = (bf16[112,2560]{1,0:T(8,128)(2,1)}, bf16[112,2560]{1,0:T(8,128)(2,1)}, u32[]{:S(2)}, u32[]{:S(2)}) collective-permute-start(bf16[112,2560]{1,0:T(8,128)(2,1)} %add_convert_fusion.1), channel_id=1, source_target_pairs={{0,4},{1,5},{2,6},{3,7},{4,0},{5,1},{6,2},{7,3},{8,12},{9,13},{10,... | collective-permute-start | bytes 1720328 | tf_op jit(solution)/shard_map/ppermute | solution.py:150
  116.5 4.7 %collective-permute-done.33 = bf16[112,2560]{1,0:T(8,128)(2,1)S(1)} collective-permute-done((bf16[112,2560]{1,0:T(8,128)(2,1)S(1)}, bf16[112,2560]{1,0:T(8,128)(2,1)S(1)}, u32[]{:S(2)}, u32[]{:S(2)}) %collective-permute-start.33) | collective-permute-done | bytes 573472 | tf_op jit(solution)/shard_map/ppermute | solution.py:150
  121.2 1.5 add_convert_fusion
  122.7 2.7 %collective-permute-start.34 = (bf16[112,2560]{1,0:T(8,128)(2,1)}, bf16[112,2560]{1,0:T(8,128)(2,1)}, u32[]{:S(2)}, u32[]{:S(2)}) collective-permute-start(bf16[112,2560]{1,0:T(8,128)(2,1)} %add_convert_fusion), channel_id=1, source_target_pairs={{0,2},{1,3},{2,0},{3,1},{4,6},{5,7},{6,4},{7,5},{8,10},{9,11},{10,... | collective-permute-start | bytes 1720328 | tf_op jit(solution)/shard_map/ppermute | solution.py:150
  125.3 1.5 collective-permute-start.27
  126.9 4.3 %collective-permute-done.28 = bf16[2,128,1280]{2,1,0:T(8,128)(2,1)S(1)} collective-permute-done((bf16[2,128,1280]{2,1,0:T(8,128)(2,1)S(1)}, bf16[2,128,1280]{2,1,0:T(8,128)(2,1)S(1)}, u32[]{:S(2)}, u32[]{:S(2)}) %collective-permute-start.28) | collective-permute-done | bytes 655392 | tf_op jit(solution)/shard_map/ppermute | solution.py:150
  131.2 1.5 collective-permute-start.23
  133.9 1.5 collective-permute-start.29
  136.3 1.9 %reshape.276 = bf16[4,112,2,2,128]{4,3,2,1,0:T(2,128)(2,1)} reshape(bf16[4,112,512]{2,1,0:T(8,128)(2,1)} %broadcast_select_fusion.5) | data formatting | bytes 917504 | tf_op jit(solution)/shard_map/reshape | solution.py:270
  140.1 1.5 shard_map.108.refs_4_
  142.2 1.6 shard_map.110.refs_6_
  144.8 1.5 shard_map.109.refs_5_
  146.3 6.0 %collective-permute-done.29.up_ref = bf16[2,128,1280]{2,1,0:T(8,128)(2,1)} collective-permute-done((bf16[2,128,1280]{2,1,0:T(8,128)(2,1)}, bf16[2,128,1280]{2,1,0:T(8,128)(2,1)}, u32[]{:S(2)}, u32[]{:S(2)}) %collective-permute-start.29) | collective-permute-done | bytes 655392 | tf_op jit(solution)/shard_map/ppermute | solution.py:150
  152.2 1.5 shard_map.111.refs_7_
  154.2 4.7 %shard_map.113 = bf16[7,256,1280]{2,1,0:T(8,128)(2,1)} custom-call(bf16[112,2560]{1,0:T(8,128)(2,1)S(1)} %shard_map.104.refs_0_, bf16[112,2560]{1,0:T(8,128)(2,1)S(1)} %shard_map.105.refs_1_, bf16[112,2560]{1,0:T(8,128)(2,1)S(1)} %shard_map.106.refs_2_, bf16[112,2560]{1,0:T(8,128)(2,1)S(1)} %shard_map.107.refs_3_, bf16[112,2560]{1,0:T(8,128)(2,1)S(1)} %shard_map.108.refs_4_, ...), custom_call_target="tpu_custom_call" | custom-call | flops 1174405120 | bytes 4587520 | tf_op jit(solution)/shard_map/pallas_call | solution.py:75
  159.0 4.7 %shard_map.112 = bf16[7,256,1280]{2,1,0:T(8,128)(2,1)} custom-call(bf16[112,2560]{1,0:T(8,128)(2,1)S(1)} %shard_map.104.refs_0_, bf16[112,2560]{1,0:T(8,128)(2,1)S(1)} %shard_map.105.refs_1_, bf16[112,2560]{1,0:T(8,128)(2,1)S(1)} %shard_map.106.refs_2_, bf16[112,2560]{1,0:T(8,128)(2,1)S(1)} %shard_map.107.refs_3_, bf16[112,2560]{1,0:T(8,128)(2,1)S(1)} %shard_map.108.refs_4_, ...), custom_call_target="tpu_custom_call" | custom-call | flops 1174405120 | bytes 4587520 | tf_op jit(solution)/shard_map/pallas_call | solution.py:75
  (136 shorter events, 25.8 us)
Async XLA Ops:
  0.6 13.6 %copy-start.15 = (s32[32]{0:T(128)S(1)}, s32[32]{0:T(128)}, u32[]{:S(2)}) copy-start(s32[32]{0:T(128)} %param.17) | copy-start | bytes 388
  0.6 13.6 %copy-start.14 = (s32[144]{0:T(256)S(1)}, s32[144]{0:T(256)}, u32[]{:S(2)}) copy-start(s32[144]{0:T(256)} %param.16) | copy-start | bytes 1732
  2.5 19.7 %collective-permute-start.2 = (bf16[112,1280]{1,0:T(8,128)(2,1)S(1)}, bf16[112,1280]{1,0:T(8,128)(2,1)S(1)}, u32[]{:S(2)}, u32[]{:S(2)}) collective-permute-start(bf16[112,1280]{1,0:T(8,128)(2,1)S(1)} %get-tuple-element.61), channel_id=1, source_target_pairs={{0,6},{1,7},{2,4},{3,5},{4,2},{5,3},{6,0},{7,1},{8,14},{9,15},{10,... | collective-permute-start | bytes 860168 | tf_op jit(solution)/shard_map/ppermute | solution.py:150
  7.6 24.4 %collective-permute-start.1 = (bf16[112,1280]{1,0:T(8,128)(2,1)S(1)}, bf16[112,1280]{1,0:T(8,128)(2,1)S(1)}, u32[]{:S(2)}, u32[]{:S(2)}) collective-permute-start(bf16[112,1280]{1,0:T(8,128)(2,1)S(1)} %get-tuple-element.61), channel_id=1, source_target_pairs={{0,4},{1,5},{2,6},{3,7},{4,0},{5,1},{6,2},{7,3},{8,12},{9,13},{10,... | collective-permute-start | bytes 860168 | tf_op jit(solution)/shard_map/ppermute | solution.py:150
  7.6 24.4 %collective-permute-start = (bf16[112,1280]{1,0:T(8,128)(2,1)S(1)}, bf16[112,1280]{1,0:T(8,128)(2,1)}, u32[]{:S(2)}, u32[]{:S(2)}) collective-permute-start(bf16[112,1280]{1,0:T(8,128)(2,1)S(1)} %get-tuple-element.61), channel_id=1, source_target_pairs={{0,2},{1,3},{2,0},{3,1},{4,6},{5,7},{6,4},{7,5},{8,10},{9,11},{10,... | collective-permute-start | bytes 860168 | tf_op jit(solution)/shard_map/ppermute | solution.py:150
  8.3 12.2 %collective-permute-start.17 = (bf16[1,112,640]{2,1,0:T(8,128)(2,1)S(1)}, bf16[1,112,640]{2,1,0:T(8,128)(2,1)S(1)}, u32[]{:S(2)}, u32[]{:S(2)}) collective-permute-start(bf16[1,112,640]{2,1,0:T(8,128)(2,1)S(1)} %get-tuple-element.63), channel_id=1, source_target_pairs={{0,1},{1,0},{10,11},{11,10},{20,21},{21,20},{30,31},{31,30}} | collective-permute-start | bytes 430088 | tf_op jit(solution)/shard_map/ppermute | solution.py:150
  11.8 29.0 %collective-permute-start.3 = (bf16[2,128,1280]{2,1,0:T(8,128)(2,1)}, bf16[2,128,1280]{2,1,0:T(8,128)(2,1)S(1)}, u32[]{:S(2)}, u32[]{:S(2)}) collective-permute-start(bf16[2,128,1280]{2,1,0:T(8,128)(2,1)} %bitcast.104), channel_id=1, source_target_pairs={{0,1},{1,0},{2,3},{3,2},{4,5},{5,4},{6,7},{7,6},{8,9},{9,8},{10,11... | collective-permute-start | bytes 1966088 | tf_op jit(solution)/shard_map/ppermute | solution.py:150
  19.6 12.5 %copy-start = (bf16[1,2,128,1280]{3,2,1,0:T(8,128)(2,1)S(1)}, bf16[1,2,128,1280]{3,2,1,0:T(8,128)(2,1)}, u32[]{:S(2)}) copy-start(bf16[1,2,128,1280]{3,2,1,0:T(8,128)(2,1)} %param.13) | copy-start | bytes 1966084
  20.5 13.1 %copy-start.6 = (bf16[1,112,640]{2,1,0:T(8,128)(2,1)}, bf16[1,112,640]{2,1,0:T(8,128)(2,1)S(1)}, u32[]{:S(2)}) copy-start(bf16[1,112,640]{2,1,0:T(8,128)(2,1)S(1)} %collective-permute-done.17) | copy-start | bytes 430084
  20.5 20.4 %collective-permute-start.9 = (bf16[1280,256]{1,0:T(8,128)(2,1)}, bf16[1280,256]{1,0:T(8,128)(2,1)S(1)}, u32[]{:S(2)}, u32[]{:S(2)}) collective-permute-start(bf16[1280,256]{1,0:T(8,128)(2,1)} %bitcast.145), channel_id=1, source_target_pairs={{0,1},{1,0},{2,3},{3,2},{4,5},{5,4},{6,7},{7,6},{8,9},{9,8},{10,11... | collective-permute-start | bytes 1966088 | tf_op jit(solution)/shard_map/ppermute | solution.py:150
  22.3 11.3 %copy-start.8 = (bf16[112,1280]{1,0:T(8,128)(2,1)}, bf16[112,1280]{1,0:T(8,128)(2,1)S(1)}, u32[]{:S(2)}) copy-start(bf16[112,1280]{1,0:T(8,128)(2,1)S(1)} %collective-permute-done.2) | copy-start | bytes 860164
  22.3 17.2 %collective-permute-start.18 = (bf16[2,1,112,640]{3,2,1,0:T(8,128)(2,1)S(1)}, bf16[2,1,112,640]{3,2,1,0:T(8,128)(2,1)S(1)}, u32[]{:S(2)}, u32[]{:S(2)}) collective-permute-start(bf16[2,1,112,640]{3,2,1,0:T(8,128)(2,1)S(1)} %pad_maximum_fusion.6), channel_id=1, source_target_pairs={{0,16},{1,17},{10,26},{11,27},{20,4},{21,5},{30,14},{31,15}} | collective-permute-start | bytes 860168 | tf_op jit(solution)/shard_map/ppermute | solution.py:150
  32.0 26.5 %collective-permute-start.6 = (bf16[2,128,1280]{2,1,0:T(8,128)(2,1)S(1)}, bf16[2,128,1280]{2,1,0:T(8,128)(2,1)}, u32[]{:S(2)}, u32[]{:S(2)}) collective-permute-start(bf16[2,128,1280]{2,1,0:T(8,128)(2,1)S(1)} %bitcast.105), channel_id=1, source_target_pairs={{2,4},{3,5},{4,2},{5,3},{10,12},{11,13},{12,10},{13,11},{18,20},{1... | collective-permute-start | bytes 1966088 | tf_op jit(solution)/shard_map/ppermute | solution.py:150
  34.6 3.7 %copy-start.9 = (bf16[112,1280]{1,0:T(8,128)(2,1)S(1)}, bf16[112,1280]{1,0:T(8,128)(2,1)}, u32[]{:S(2)}) copy-start(bf16[112,1280]{1,0:T(8,128)(2,1)} %copy-done.8) | copy-start | bytes 860164
  34.8 4.7 %copy-start.7 = (bf16[1,112,640]{2,1,0:T(8,128)(2,1)S(1)}, bf16[1,112,640]{2,1,0:T(8,128)(2,1)}, u32[]{:S(2)}) copy-start(bf16[1,112,640]{2,1,0:T(8,128)(2,1)} %copy-done.6) | copy-start | bytes 430084
  34.8 6.1 %copy-start.16 = (bf16[1,1280,256]{2,1,0:T(8,128)(2,1)S(1)}, bf16[1,1280,256]{2,1,0:T(8,128)(2,1)}, u32[]{:S(2)}) copy-start(bf16[1,1280,256]{2,1,0:T(8,128)(2,1)} %param.12) | copy-start | bytes 1966084
  34.8 10.6 %collective-permute-start.8 = (bf16[3,112,640]{2,1,0:T(8,128)(2,1)S(1)}, bf16[3,112,640]{2,1,0:T(8,128)(2,1)S(1)}, u32[]{:S(2)}, u32[]{:S(2)}) collective-permute-start(bf16[3,112,640]{2,1,0:T(8,128)(2,1)S(1)} %get-tuple-element.55), channel_id=1, source_target_pairs={{0,1},{1,0},{10,11},{11,10},{20,21},{21,20},{30,31},{31,30}} | collective-permute-start | bytes 1290248 | tf_op jit(solution)/shard_map/ppermute | solution.py:150
  39.6 10.7 %collective-permute-start.19 = (bf16[2,1,112,640]{3,2,1,0:T(8,128)(2,1)S(1)}, bf16[2,1,112,640]{3,2,1,0:T(8,128)(2,1)S(1)}, u32[]{:S(2)}, u32[]{:S(2)}) collective-permute-start(bf16[2,1,112,640]{3,2,1,0:T(8,128)(2,1)S(1)} %broadcast_select_fusion.6), channel_id=1, source_target_pairs={{0,8},{16,24},{1,9},{17,25},{10,2},{26,18},{11,3},{27,19},{20,28},... | collective-permute-start | bytes 860168 | tf_op jit(solution)/shard_map/ppermute | solution.py:150
  41.7 13.5 %copy-start.12 = (f32[448,512]{1,0:T(8,128)}, f32[448,512]{1,0:T(8,128)S(1)}, u32[]{:S(2)}) copy-start(f32[448,512]{1,0:T(8,128)S(1)} %fusion.2) | copy-start | bytes 2752516
  45.4 6.2 %collective-permute-start.10 = (f32[2,112,512]{2,1,0:T(8,128)S(1)}, f32[2,112,512]{2,1,0:T(8,128)S(1)}, u32[]{:S(2)}, u32[]{:S(2)}) collective-permute-start(f32[2,112,512]{2,1,0:T(8,128)S(1)} %pad_maximum_fusion.4), channel_id=1, source_target_pairs={{0,8},{1,9},{2,10},{3,11},{4,12},{5,13},{6,14},{7,15},{8,0},{9,1},... | collective-permute-start | bytes 1376264 | tf_op jit(solution)/shard_map/ppermute | solution.py:150
  46.7 32.4 %collective-permute-start.4 = (bf16[2,2,128,1280]{3,2,1,0:T(8,128)(2,1)}, bf16[2,2,128,1280]{3,2,1,0:T(8,128)(2,1)}, u32[]{:S(2)}, u32[]{:S(2)}) collective-permute-start(bf16[2,2,128,1280]{3,2,1,0:T(8,128)(2,1)} %pad_maximum_fusion), channel_id=1, source_target_pairs={{0,2},{1,3},{2,0},{3,1},{4,6},{5,7},{6,4},{7,5},{8,10},{9,11},{10,... | collective-permute-start | bytes 3932168 | tf_op jit(solution)/shard_map/ppermute | solution.py:150
  49.2 6.0 %collective-permute-start.26 = (f32[112]{0:T(128)S(1)}, f32[112]{0:T(128)S(1)}, u32[]{:S(2)}, u32[]{:S(2)}) collective-permute-start(f32[112]{0:T(128)S(1)} %get-tuple-element.40), channel_id=1, source_target_pairs={{0,24},{1,25},{2,26},{3,27},{4,28},{5,29},{6,30},{7,31},{8,16},{9,... | collective-permute-start | bytes 1352 | tf_op jit(solution)/shard_map/ppermute | solution.py:150
  49.2 6.2 %copy-start.4 = (bf16[80,8,2,1280]{3,1,2,0:T(8,128)(2,1)S(1)}, bf16[80,8,2,1280]{3,1,2,0:T(8,128)(2,1)}, u32[]{:S(2)}) copy-start(bf16[80,8,2,1280]{3,1,2,0:T(8,128)(2,1)} %copy.44) | copy-start | bytes 9830404
  50.2 5.1 %collective-permute-start.25 = (f32[112]{0:T(128)S(1)}, f32[112]{0:T(128)S(1)}, u32[]{:S(2)}, u32[]{:S(2)}) collective-permute-start(f32[112]{0:T(128)S(1)} %get-tuple-element.40), channel_id=1, source_target_pairs={{0,16},{1,17},{2,18},{3,19},{4,20},{5,21},{6,22},{7,23},{8,24},{9,... | collective-permute-start | bytes 1352 | tf_op jit(solution)/shard_map/ppermute | solution.py:150
  51.6 6.8 %copy-start.11 = (bf16[2,1,112,640]{3,2,1,0:T(8,128)(2,1)}, bf16[2,1,112,640]{3,2,1,0:T(8,128)(2,1)S(1)}, u32[]{:S(2)}) copy-start(bf16[2,1,112,640]{3,2,1,0:T(8,128)(2,1)S(1)} %broadcast_select_fusion.7) | copy-start | bytes 860164
  51.7 5.2 %copy-start.13 = (f32[2,112,512]{2,1,0:T(8,128)}, f32[2,112,512]{2,1,0:T(8,128)S(1)}, u32[]{:S(2)}) copy-start(f32[2,112,512]{2,1,0:T(8,128)S(1)} %collective-permute-done.10) | copy-start | bytes 1376260
  51.7 19.3 %collective-permute-start.15 = (bf16[2,3,112,640]{3,2,1,0:T(8,128)(2,1)}, bf16[2,3,112,640]{3,2,1,0:T(8,128)(2,1)}, u32[]{:S(2)}, u32[]{:S(2)}) collective-permute-start(bf16[2,3,112,640]{3,2,1,0:T(8,128)(2,1)} %pad_maximum_fusion.3), channel_id=1, source_target_pairs={{0,16},{1,17},{10,26},{11,27},{20,4},{21,5},{30,14},{31,15}} | collective-permute-start | bytes 2580488 | tf_op jit(solution)/shard_map/ppermute | solution.py:150
  55.2 1.7 %collective-permute-start.24 = (f32[112]{0:T(128)S(1)}, f32[112]{0:T(128)S(1)}, u32[]{:S(2)}, u32[]{:S(2)}) collective-permute-start(f32[112]{0:T(128)S(1)} %get-tuple-element.40), channel_id=1, source_target_pairs={{0,8},{1,9},{2,10},{3,11},{4,12},{5,13},{6,14},{7,15},{8,0},{9,1},... | collective-permute-start | bytes 1352 | tf_op jit(solution)/shard_map/ppermute | solution.py:150
  55.3 14.4 %collective-permute-start.11 = (f32[1,112,512]{2,1,0:T(8,128)S(1)}, f32[1,112,512]{2,1,0:T(8,128)}, u32[]{:S(2)}, u32[]{:S(2)}) collective-permute-start(f32[1,112,512]{2,1,0:T(8,128)S(1)} %slice_add_fusion), channel_id=1, source_target_pairs={{0,16},{1,17},{2,18},{3,19},{4,20},{5,21},{6,22},{7,23},{8,24},{9,... | collective-permute-start | bytes 688136 | tf_op jit(solution)/shard_map/ppermute | solution.py:150
  56.9 15.6 %collective-permute-start.20 = (bf16[112,2560]{1,0:T(8,128)(2,1)}, bf16[112,2560]{1,0:T(8,128)(2,1)}, u32[]{:S(2)}, u32[]{:S(2)}) collective-permute-start(bf16[112,2560]{1,0:T(8,128)(2,1)} %convolution_convert_fusion.3), channel_id=1, source_target_pairs={{0,1},{1,0},{2,3},{3,2},{4,5},{5,4},{6,7},{7,6},{8,9},{9,8},{10,11... | collective-permute-start | bytes 1720328 | tf_op jit(solution)/shard_map/ppermute | solution.py:150
  58.5 39.1 %collective-permute-start.7 = (bf16[2,128,1280]{2,1,0:T(8,128)(2,1)}, bf16[2,128,1280]{2,1,0:T(8,128)(2,1)S(1)}, u32[]{:S(2)}, u32[]{:S(2)}) collective-permute-start(bf16[2,128,1280]{2,1,0:T(8,128)(2,1)} %collective-permute-done.6), channel_id=1, source_target_pairs={{2,0},{3,1},{4,6},{5,7},{10,8},{11,9},{12,14},{13,15},{18,16},{19,... | collective-permute-start | bytes 1966088 | tf_op jit(solution)/shard_map/ppermute | solution.py:150
  69.7 2.9 %copy-start.5 = (bf16[80,8,2,1280]{3,1,2,0:T(8,128)(2,1)S(1)}, bf16[80,8,2,1280]{3,1,2,0:T(8,128)(2,1)}, u32[]{:S(2)}) copy-start(bf16[80,8,2,1280]{3,1,2,0:T(8,128)(2,1)} %copy.44) | copy-start | bytes 9830404
  71.2 10.8 %collective-permute-start.16 = (bf16[2,3,112,640]{3,2,1,0:T(8,128)(2,1)S(1)}, bf16[2,3,112,640]{3,2,1,0:T(8,128)(2,1)S(1)}, u32[]{:S(2)}, u32[]{:S(2)}) collective-permute-start(bf16[2,3,112,640]{3,2,1,0:T(8,128)(2,1)S(1)} %broadcast_select_fusion), channel_id=1, source_target_pairs={{0,8},{16,24},{1,9},{17,25},{10,2},{26,18},{11,3},{27,19},{20,28},... | collective-permute-start | bytes 2580488 | tf_op jit(solution)/shard_map/ppermute | solution.py:150
  74.4 10.6 %collective-permute-start.14 = (bf16[112,512]{1,0:T(8,128)(2,1)S(1)}, bf16[112,512]{1,0:T(8,128)(2,1)S(1)}, u32[]{:S(2)}, u32[]{:S(2)}) collective-permute-start(bf16[112,512]{1,0:T(8,128)(2,1)S(1)} %fusion.31), channel_id=1, source_target_pairs={{6,0},{7,1},{12,10},{13,11},{18,20},{19,21},{24,30},{25,31}} | collective-permute-start | bytes 344072 | tf_op jit(solution)/shard_map/ppermute | solution.py:150
  75.7 11.3 %collective-permute-start.13 = (bf16[112,512]{1,0:T(8,128)(2,1)S(1)}, bf16[112,512]{1,0:T(8,128)(2,1)S(1)}, u32[]{:S(2)}, u32[]{:S(2)}) collective-permute-start(bf16[112,512]{1,0:T(8,128)(2,1)S(1)} %fusion.31), channel_id=1, source_target_pairs={{4,0},{5,1},{14,10},{15,11},{16,20},{17,21},{26,30},{27,31}} | collective-permute-start | bytes 344072 | tf_op jit(solution)/shard_map/ppermute | solution.py:150
  81.3 16.3 %collective-permute-start.5 = (bf16[2,128,1280]{2,1,0:T(8,128)(2,1)S(1)}, bf16[2,128,1280]{2,1,0:T(8,128)(2,1)S(1)}, u32[]{:S(2)}, u32[]{:S(2)}) collective-permute-start(bf16[2,128,1280]{2,1,0:T(8,128)(2,1)S(1)} %get-tuple-element.51.up_ref), channel_id=1, source_target_pairs={{2,4},{3,5},{4,2},{5,3},{10,12},{11,13},{12,10},{13,11},{18,20},{1... | collective-permute-start | bytes 1966088 | tf_op jit(solution)/shard_map/ppermute | solution.py:150
  82.8 16.0 %collective-permute-start.21 = (bf16[112,2560]{1,0:T(8,128)(2,1)S(1)}, bf16[112,2560]{1,0:T(8,128)(2,1)S(1)}, u32[]{:S(2)}, u32[]{:S(2)}) collective-permute-start(bf16[112,2560]{1,0:T(8,128)(2,1)S(1)} %convolution_convert_fusion.2), channel_id=1, source_target_pairs={{0,1},{1,0},{2,3},{3,2},{4,5},{5,4},{6,7},{7,6},{8,9},{9,8},{10,11... | collective-permute-start | bytes 1720328 | tf_op jit(solution)/shard_map/ppermute | solution.py:150
  85.0 11.1 %collective-permute-start.12 = (bf16[112,512]{1,0:T(8,128)(2,1)S(1)}, bf16[112,512]{1,0:T(8,128)(2,1)S(1)}, u32[]{:S(2)}, u32[]{:S(2)}) collective-permute-start(bf16[112,512]{1,0:T(8,128)(2,1)S(1)} %fusion.31), channel_id=1, source_target_pairs={{2,0},{3,1},{8,10},{9,11},{22,20},{23,21},{28,30},{29,31}} | collective-permute-start | bytes 344072 | tf_op jit(solution)/shard_map/ppermute | solution.py:150
  87.0 24.1 %collective-permute-start.31 = (bf16[112,2560]{1,0:T(8,128)(2,1)S(1)}, bf16[112,2560]{1,0:T(8,128)(2,1)S(1)}, u32[]{:S(2)}, u32[]{:S(2)}) collective-permute-start(bf16[112,2560]{1,0:T(8,128)(2,1)S(1)} %convolution_convert_fusion.1), channel_id=1, source_target_pairs={{0,1},{1,0},{2,3},{3,2},{4,5},{5,4},{6,7},{7,6},{8,9},{9,8},{10,11... | collective-permute-start | bytes 1720328 | tf_op jit(solution)/shard_map/ppermute | solution.py:150
  96.1 25.1 %collective-permute-start.33 = (bf16[112,2560]{1,0:T(8,128)(2,1)S(1)}, bf16[112,2560]{1,0:T(8,128)(2,1)S(1)}, u32[]{:S(2)}, u32[]{:S(2)}) collective-permute-start(bf16[112,2560]{1,0:T(8,128)(2,1)S(1)} %convolution_convert_fusion), channel_id=1, source_target_pairs={{0,1},{1,0},{2,3},{3,2},{4,5},{5,4},{6,7},{7,6},{8,9},{9,8},{10,11... | collective-permute-start | bytes 1720328 | tf_op jit(solution)/shard_map/ppermute | solution.py:150
  99.8 25.6 %collective-permute-start.22 = (bf16[4,112,512]{2,1,0:T(8,128)(2,1)S(1)}, bf16[4,112,512]{2,1,0:T(8,128)(2,1)S(1)}, u32[]{:S(2)}, u32[]{:S(2)}) collective-permute-start(bf16[4,112,512]{2,1,0:T(8,128)(2,1)S(1)} %pad_maximum_fusion.5), channel_id=1, source_target_pairs={{0,16},{1,17},{10,26},{11,27},{20,4},{21,5},{30,14},{31,15}} | collective-permute-start | bytes 1376264 | tf_op jit(solution)/shard_map/ppermute | solution.py:150
  105.5 48.3 %collective-permute-start.30 = (bf16[112,2560]{1,0:T(8,128)(2,1)}, bf16[112,2560]{1,0:T(8,128)(2,1)}, u32[]{:S(2)}, u32[]{:S(2)}) collective-permute-start(bf16[112,2560]{1,0:T(8,128)(2,1)} %add_convert_fusion.2), channel_id=1, source_target_pairs={{0,6},{1,7},{2,4},{3,5},{4,2},{5,3},{6,0},{7,1},{8,14},{9,15},{10,... | collective-permute-start | bytes 1720328 | tf_op jit(solution)/shard_map/ppermute | solution.py:150
  105.5 25.8 %collective-permute-start.28 = (bf16[2,128,1280]{2,1,0:T(8,128)(2,1)S(1)}, bf16[2,128,1280]{2,1,0:T(8,128)(2,1)S(1)}, u32[]{:S(2)}, u32[]{:S(2)}) collective-permute-start(bf16[2,128,1280]{2,1,0:T(8,128)(2,1)S(1)} %collective-permute-done.5), channel_id=1, source_target_pairs={{2,0},{3,1},{4,6},{5,7},{10,8},{11,9},{12,14},{13,15},{18,16},{19,... | collective-permute-start | bytes 1966088 | tf_op jit(solution)/shard_map/ppermute | solution.py:150
  112.5 41.2 %collective-permute-start.32 = (bf16[112,2560]{1,0:T(8,128)(2,1)}, bf16[112,2560]{1,0:T(8,128)(2,1)}, u32[]{:S(2)}, u32[]{:S(2)}) collective-permute-start(bf16[112,2560]{1,0:T(8,128)(2,1)} %add_convert_fusion.1), channel_id=1, source_target_pairs={{0,4},{1,5},{2,6},{3,7},{4,0},{5,1},{6,2},{7,3},{8,12},{9,13},{10,... | collective-permute-start | bytes 1720328 | tf_op jit(solution)/shard_map/ppermute | solution.py:150
  122.7 31.6 %collective-permute-start.34 = (bf16[112,2560]{1,0:T(8,128)(2,1)}, bf16[112,2560]{1,0:T(8,128)(2,1)}, u32[]{:S(2)}, u32[]{:S(2)}) collective-permute-start(bf16[112,2560]{1,0:T(8,128)(2,1)} %add_convert_fusion), channel_id=1, source_target_pairs={{0,2},{1,3},{2,0},{3,1},{4,6},{5,7},{6,4},{7,5},{8,10},{9,11},{10,... | collective-permute-start | bytes 1720328 | tf_op jit(solution)/shard_map/ppermute | solution.py:150
  125.3 19.4 %collective-permute-start.27 = (bf16[2,128,1280]{2,1,0:T(8,128)(2,1)}, bf16[2,128,1280]{2,1,0:T(8,128)(2,1)}, u32[]{:S(2)}, u32[]{:S(2)}) collective-permute-start(bf16[2,128,1280]{2,1,0:T(8,128)(2,1)} %broadcast_select_fusion.3.up_ref), channel_id=1, source_target_pairs={{0,1},{1,0},{2,3},{3,2},{4,5},{5,4},{6,7},{7,6},{8,9},{9,8},{10,11... | collective-permute-start | bytes 1966088 | tf_op jit(solution)/shard_map/ppermute | solution.py:150
  131.2 2.7 %collective-permute-start.23 = (bf16[4,112,512]{2,1,0:T(8,128)(2,1)S(1)}, bf16[4,112,512]{2,1,0:T(8,128)(2,1)S(1)}, u32[]{:S(2)}, u32[]{:S(2)}) collective-permute-start(bf16[4,112,512]{2,1,0:T(8,128)(2,1)S(1)} %broadcast_select_fusion.4), channel_id=1, source_target_pairs={{0,8},{16,24},{1,9},{17,25},{10,2},{26,18},{11,3},{27,19},{20,28},... | collective-permute-start | bytes 1376264 | tf_op jit(solution)/shard_map/ppermute | solution.py:150
  133.9 18.3 %collective-permute-start.29 = (bf16[2,128,1280]{2,1,0:T(8,128)(2,1)}, bf16[2,128,1280]{2,1,0:T(8,128)(2,1)}, u32[]{:S(2)}, u32[]{:S(2)}) collective-permute-start(bf16[2,128,1280]{2,1,0:T(8,128)(2,1)} %broadcast_select_fusion.2.up_ref), channel_id=1, source_target_pairs={{0,1},{1,0},{2,3},{3,2},{4,5},{5,4},{6,7},{7,6},{8,9},{9,8},{10,11... | collective-permute-start | bytes 1966088 | tf_op jit(solution)/shard_map/ppermute | solution.py:150
  (4 other events, 7.6 us)

commit v4 on v3

--- a/solution.py
+++ b/solution.py
@@ -18,21 +18,21 @@
 
 def corrections(rank, up, scale):
     _, tokens, low_rank = rank.shape
-    width = up.shape[2]
+    n, _, width = up.shape
     return pl.pallas_call(
         delta_kernel,
-        grid=(2,),
+        grid=(n,),
         in_specs=[
             pl.BlockSpec((1, tokens, low_rank), lambda j: (j, 0, 0)),
             pl.BlockSpec((1, low_rank, width), lambda j: (j, 0, 0)),
             pl.BlockSpec((tokens, 1), lambda j: (0, 0)),
         ],
         out_specs=pl.BlockSpec((tokens, width), lambda j: (0, j)),
-        out_shape=jax.ShapeDtypeStruct((tokens, 2 * width), jnp.bfloat16),
+        out_shape=jax.ShapeDtypeStruct((tokens, n * width), jnp.bfloat16),
         compiler_params=pltpu.CompilerParams(vmem_limit_bytes=24 * 1024 * 1024),
         cost_estimate=pl.CostEstimate(
-            flops=4 * tokens * low_rank * width,
-            bytes_accessed=4 * (tokens * width + low_rank * width),
+            flops=2 * n * tokens * low_rank * width,
+            bytes_accessed=2 * n * (tokens * width + low_rank * width),
             transcendentals=0,
         ),
     )(rank, up, scale)
@@ -72,10 +72,11 @@
     block = next(n for n in (640, 256, 128) if width % n == 0)
     steps = width // block
     column = pl.BlockSpec((tokens, block), lambda i: (0, half * steps + i))
+    single = pl.BlockSpec((tokens, block), lambda i: (0, i))
     out = pl.pallas_call(
         functools.partial(mix_kernel, adapters=len(deltas), parts=len(bases)),
         grid=(steps,),
-        in_specs=[column] * (len(deltas) + len(bases))
+        in_specs=[column if value.shape[1] > width else single for value in (*deltas, *bases)]
         + [
             pl.BlockSpec((tokens, 1), lambda i: (0, 0)),
             pl.BlockSpec((groups, rows, depth), lambda i: (0, 0, 0)),
@@ -162,7 +163,7 @@
             value, [((r, 2 * (r ^ k) + s), (r, 2 * r + s)) for r in range(rows) for s in range(2)]
         )
 
-    def over_rows(value, *before_last):
+    def to_far_rows(value):
         bit = 2
         while bit < rows:
             got = send(
@@ -175,13 +176,17 @@
             )
             value = jnp.where((row ^ line) & bit != 0, got, value)
             bit *= 2
-        if before_last:
-            value = lax.optimization_barrier((value, *before_last))[0]
+        return value
+
+    def to_next_row(value):
         got = send(
             value,
             [((c // 2 ^ e, c), (c // 2 ^ e ^ 1, c)) for c in range(cols) for e in range(0, rows, 2)],
         )
         return jnp.where((row ^ line) & 1 != 0, got, value)
+
+    def over_rows(value):
+        return to_next_row(to_far_rows(value))
 
     def after(value, *others):
         return lax.optimization_barrier((value, *others))[0]
@@ -215,17 +220,17 @@
     own_out = to_side(product(both[1, 0]).astype(jnp.bfloat16))
     own_kept = product(both[0, 0])
 
-    late = lax.optimization_barrier((up_own, *rest))
-    up_late, rest = late[0], late[1:]
+    late = lax.optimization_barrier((up_own, up_other, *rest))
+    up_late, up_other, rest = late[0], late[1], late[2:]
     if lines == 4:
         near = to_line(jnp.stack([up_late, up_other]), 1)
         near, near_other = near[0], near[1]
         far_near = send(up_late, across)
     else:
         near = to_line(up_late, 1)
-        far_near = near
 
     mine, got = halves(jnp.stack(rest))
+    mine_far = to_far_rows(mine)
     gathered = jnp.concatenate([gained, *rest], axis=0)
     gathered, other_down, up_other = lax.optimization_barrier((gathered, other_down, up_other))
     down = jnp.concatenate([adapter_down_maps[0], other_down], axis=1)
@@ -235,19 +240,20 @@
     parts = {
         m: lax.dynamic_index_in_dim(partial, row ^ line ^ m, 0, keepdims=False) for m in range(rows)
     }
+    squares = after(jnp.sum(states * states, axis=1), partial)
+    squares = jnp.pad(squares[None], ((0, 7), (0, 4 * low_rank - tokens)))
     bit = 1
     while bit < rows:
         leaving = [m for m in parts if m & bit]
-        arrived = send(
-            jnp.stack([parts.pop(m) for m in leaving]), [((r, c), (r ^ bit, c)) for r, c in every]
-        )
+        message = jnp.concatenate([parts.pop(m) for m in leaving] + [squares])
+        arrived = send(message, [((r, c), (r ^ bit, c)) for r, c in every])
         for i, m in enumerate(leaving):
-            parts[m ^ bit] = parts[m ^ bit] + arrived[i]
+            parts[m ^ bit] = parts[m ^ bit] + arrived[i * tokens : (i + 1) * tokens]
+        squares = squares + arrived[len(leaving) * tokens :]
         bit *= 2
     held = parts[0].astype(jnp.bfloat16)
 
-    both = over_rows(jnp.stack([mine, got]), held)
-    both = after(both, own_out)
+    both = to_next_row(after(jnp.stack([mine_far, to_far_rows(got)]), held))
     outs = [product(both[1, k]).astype(jnp.bfloat16) for k in range(lines - 1)]
     kept = [product(both[0, k]) for k in range(lines - 1)]
     came = [None] * (lines - 1)
@@ -273,9 +279,13 @@
         far = jnp.where(inner, jnp.concatenate([ranks[6:], ranks[4:6]]), ranks[4:])
         ranks = jnp.concatenate([ranks[:4], far])
 
-    for value in blocks:
+    for value in blocks[:-1]:
         ups += [value, to_side(after(value, came[-1]))]
-
+    value = after(blocks[-1], came[-1])
+    ups += [blocks[-1], [to_side(value[:1]), to_side(value[1:])]]
+
+    if lines == 4:
+        came = [after(value, far_far) for value in came]
     bases = [own_kept + own_out.astype(jnp.float32)]
     for k in reversed(range(lines - 1)):
         total = kept[k] + came[k].astype(jnp.float32)
@@ -285,11 +295,7 @@
         place = slot ^ col
         return jnp.where(inner & (place >= 4), place ^ 2, place) if lines == 4 else place
 
-    square_sum = after(jnp.sum(states * states, axis=1), partial)
-    total = square_sum
-    for j in range(1, rows):
-        total = total + send(square_sum, [((r, c), (r ^ j, c)) for r, c in every])
-    scale = lax.rsqrt(total / (width * rows) + 1e-05)[:, None]
+    scale = lax.rsqrt(squares[0, :tokens] / (width * rows) + 1e-05)[:, None]
     depth = -(-(adapters * GROUP + 2 * GROUP) // 128) * 128
     token_index = col * tokens + jnp.arange(tokens, dtype=jnp.int32)
     pick = pick_matrix(
@@ -302,8 +308,16 @@
         depth,
         order,
     )
-    deltas = [corrections(ranks[e], ups[e], scale) for e in range(adapters)]
-    return tuple(mix(deltas, bases, scale, pick, half) for half in range(2))
+    outs = []
+    deltas = [corrections(ranks[e], ups[e], scale) for e in range(adapters) if not isinstance(ups[e], list)]
+    for half in range(2):
+        own = [
+            corrections(ranks[e, half : half + 1], ups[e][half], scale)
+            for e in range(adapters)
+            if isinstance(ups[e], list)
+        ]
+        outs.append(mix(deltas + own, bases, scale, pick, half))
+    return tuple(outs)
 
 
 def solution(mesh):

time: 166 us -> 161 us (0.970); the launches traced: 164 us -> 161 us
  starting transfers between devices: 55.8 us -> 49.7 us
  waiting for transfers between devices: 53.8 us -> 57.1 us
  matrix products: 10.5 us -> 8.51 us
    ppermute x35 -> x34, starting transfers between devices: 55.8 us -> 49.7 us  [send(): return lax.ppermute(value, ('row', 'col'), flat)]
    ppermute x35 -> x34, waiting for transfers between devices: 53.8 us -> 57.1 us  [send(): return lax.ppermute(value, ('row', 'col'), flat)]
    dot_general x8, matrix products: 9.72 us -> 7.76 us  [product(): return jnp.dot(value, weight, preferred_element_type=jnp.float32)]
    pallas_call x8 -> x9, Pallas kernels: 8.09 us -> 7.01 us  [corrections(): pl.pallas_call(delta_kernel, grid=(n,), in_specs=[pl.BlockSpec((1, tokens...]
    unnamed x35 -> x29, local copies, waits for them, and re-layouts: 4.26 us -> 4.38 us
  transfers between devices with their start and end apart: 35 -> 34, of which waited for: 12 -> 15; matrix products, arithmetic and copies ran while one was open for 20% -> 21% of each run, Pallas kernels for 5% -> 4%
where the time goes in v4:
time: 161 us
  waiting for transfers between devices  57.1 us (35%)
  starting transfers between devices  49.7 us (31%)
  Pallas kernels  16.5 us (10%)
  other arithmetic  15.3 us (10%)
  local copies, waits for them, and re-layouts  12 us (7%)
  matrix products  8.51 us (5%)
    ppermute x34, waiting for transfers between devices, send(): return lax.ppermute(value, ('row', 'col'), flat)  57.1 us
    ppermute x34, starting transfers between devices, send(): return lax.ppermute(value, ('row', 'col'), flat)  49.7 us
    pallas_call x2, Pallas kernels, mix(): pl.pallas_call(functools.partial(mix_kernel, adapters=len(deltas), parts=...  9.45 us
    dot_general x8, matrix products, product(): return jnp.dot(value, weight, preferred_element_type=jnp.float32)  7.76 us
    pallas_call x9, Pallas kernels, corrections(): pl.pallas_call(delta_kernel, grid=(n,), in_specs=[pl.BlockSpec((1, tokens...  7.01 us
    unnamed x29, local copies, waits for them, and re-layouts  4.38 us
  transfers between devices with their start and end apart: 34, of which 15 were waited for; matrix products, arithmetic and copies ran while one was open for 21% of the time, Pallas kernels for 4%

profile of v4, /device:TPU:0, one launch (start us, length us, event | category | flops | bytes accessed | tf_op | source)
XLA Modules:
  0.0 160.6 jit_solution(11740731654801744511)
XLA Ops:
  2.5 5.1 %collective-permute-start.3 = (bf16[112,1280]{1,0:T(8,128)(2,1)S(1)}, bf16[112,1280]{1,0:T(8,128)(2,1)S(1)}, u32[]{:S(2)}, u32[]{:S(2)}) collective-permute-start(bf16[112,1280]{1,0:T(8,128)(2,1)S(1)} %get-tuple-element.71), channel_id=1, source_target_pairs={{0,6},{1,7},{2,4},{3,5},{4,2},{5,3},{6,0},{7,1},{8,14},{9,15},{10,... | collective-permute-start | bytes 860168 | tf_op jit(solution)/shard_map/ppermute | solution.py:151
  8.3 3.6 %collective-permute-start.24 = (bf16[1,112,640]{2,1,0:T(8,128)(2,1)S(1)}, bf16[1,112,640]{2,1,0:T(8,128)(2,1)S(1)}, u32[]{:S(2)}, u32[]{:S(2)}) collective-permute-start(bf16[1,112,640]{2,1,0:T(8,128)(2,1)S(1)} %get-tuple-element.69), channel_id=1, source_target_pairs={{0,1},{1,0},{10,11},{11,10},{20,21},{21,20},{30,31},{31,30}} | collective-permute-start | bytes 430088 | tf_op jit(solution)/shard_map/ppermute | solution.py:151
  17.6 2.0 %collective-permute-start.25 = (bf16[2,1,112,640]{3,2,1,0:T(8,128)(2,1)}, bf16[2,1,112,640]{3,2,1,0:T(8,128)(2,1)}, u32[]{:S(2)}, u32[]{:S(2)}) collective-permute-start(bf16[2,1,112,640]{3,2,1,0:T(8,128)(2,1)} %pad_maximum_fusion.6), channel_id=1, source_target_pairs={{0,16},{1,17},{10,26},{11,27},{20,4},{21,5},{30,14},{31,15}} | collective-permute-start | bytes 860168 | tf_op jit(solution)/shard_map/ppermute | solution.py:151
  20.5 4.3 %copy.47 = bf16[80,8,2,1280]{3,1,2,0:T(8,128)(2,1)} copy(bf16[80,8,2,1280]{3,2,1,0:T(2,128)(2,1)} %bitcast.122) | data formatting | bytes 6553600
  24.8 1.6 %collective-permute-start.9 = (bf16[1280,256]{1,0:T(8,128)(2,1)}, bf16[1280,256]{1,0:T(8,128)(2,1)S(1)}, u32[]{:S(2)}, u32[]{:S(2)}) collective-permute-start(bf16[1280,256]{1,0:T(8,128)(2,1)} %bitcast.149), channel_id=1, source_target_pairs={{0,1},{1,0},{2,3},{3,2},{4,5},{5,4},{6,7},{7,6},{8,9},{9,8},{10,11... | collective-permute-start | bytes 1966088 | tf_op jit(solution)/shard_map/ppermute | solution.py:151
  26.5 1.3 collective-permute-start.26
  27.8 4.2 %collective-permute-done.2 = bf16[112,1280]{1,0:T(8,128)(2,1)S(1)} collective-permute-done((bf16[112,1280]{1,0:T(8,128)(2,1)S(1)}, bf16[112,1280]{1,0:T(8,128)(2,1)S(1)}, u32[]{:S(2)}, u32[]{:S(2)}) %collective-permute-start.2) | collective-permute-done | bytes 286752 | tf_op jit(solution)/shard_map/ppermute | solution.py:151
  32.0 1.5 collective-permute-start.6
  34.7 3.4 %collective-permute-start.8 = (bf16[3,112,640]{2,1,0:T(8,128)(2,1)S(1)}, bf16[3,112,640]{2,1,0:T(8,128)(2,1)S(1)}, u32[]{:S(2)}, u32[]{:S(2)}) collective-permute-start(bf16[3,112,640]{2,1,0:T(8,128)(2,1)S(1)} %get-tuple-element.61), channel_id=1, source_target_pairs={{0,1},{1,0},{10,11},{11,10},{20,21},{21,20},{30,31},{31,30}} | collective-permute-start | bytes 1290248 | tf_op jit(solution)/shard_map/ppermute | solution.py:151
  38.1 1.3 collective-permute-start.15
  43.1 2.2 %collective-permute-done.8 = bf16[3,112,640]{2,1,0:T(8,128)(2,1)S(1)} collective-permute-done((bf16[3,112,640]{2,1,0:T(8,128)(2,1)S(1)}, bf16[3,112,640]{2,1,0:T(8,128)(2,1)S(1)}, u32[]{:S(2)}, u32[]{:S(2)}) %collective-permute-start.8) | collective-permute-done | bytes 430112 | tf_op jit(solution)/shard_map/ppermute | solution.py:151
  46.1 1.6 collective-permute-start.27
  47.7 1.8 %collective-permute-start.16 = (bf16[3,112,640]{2,1,0:T(8,128)(2,1)S(1)}, bf16[3,112,640]{2,1,0:T(8,128)(2,1)S(1)}, u32[]{:S(2)}, u32[]{:S(2)}) collective-permute-start(bf16[3,112,640]{2,1,0:T(8,128)(2,1)S(1)} %collective-permute-done.8), channel_id=1, source_target_pairs={{0,16},{1,17},{10,26},{11,27},{20,4},{21,5},{30,14},{31,15}} | collective-permute-start | bytes 1290248 | tf_op jit(solution)/shard_map/ppermute | solution.py:151
  49.7 6.7 %collective-permute-done.16 = bf16[3,112,640]{2,1,0:T(8,128)(2,1)S(1)} collective-permute-done((bf16[3,112,640]{2,1,0:T(8,128)(2,1)S(1)}, bf16[3,112,640]{2,1,0:T(8,128)(2,1)S(1)}, u32[]{:S(2)}, u32[]{:S(2)}) %collective-permute-start.16) | collective-permute-done | bytes 430112 | tf_op jit(solution)/shard_map/ppermute | solution.py:151
  57.5 1.6 collective-permute-done.11
  59.2 2.2 %collective-permute-start.17 = (bf16[2,3,112,640]{3,2,1,0:T(8,128)(2,1)}, bf16[2,3,112,640]{3,2,1,0:T(8,128)(2,1)}, u32[]{:S(2)}, u32[]{:S(2)}) collective-permute-start(bf16[2,3,112,640]{3,2,1,0:T(8,128)(2,1)} %pad_maximum_fusion.3), channel_id=1, source_target_pairs={{0,8},{16,24},{1,9},{17,25},{10,2},{26,18},{11,3},{27,19},{20,28},... | collective-permute-start | bytes 2580488 | tf_op jit(solution)/shard_map/ppermute | solution.py:151
  62.3 1.3 collective-permute-start.7
  63.6 1.3 collective-permute-start.14
  64.9 1.3 collective-permute-start.13
  66.3 9.4 %collective-permute-done.4 = bf16[2,2,128,1280]{3,2,1,0:T(8,128)(2,1)} collective-permute-done((bf16[2,2,128,1280]{3,2,1,0:T(8,128)(2,1)}, bf16[2,2,128,1280]{3,2,1,0:T(8,128)(2,1)}, u32[]{:S(2)}, u32[]{:S(2)}) %collective-permute-start.4) | collective-permute-done | bytes 1310752 | tf_op jit(solution)/shard_map/ppermute | solution.py:151
  75.7 2.4 %slice_bitcast_fusion = (bf16[2,128,1280]{2,1,0:T(8,128)(2,1)}, bf16[2,128,1280]{2,1,0:T(8,128)(2,1)S(1)}) fusion(bf16[2,2,128,1280]{3,2,1,0:T(8,128)(2,1)} %collective-permute-done.4), kind=kLoop, calls=%fused_computation.28 | loop fusion | bytes 2621440 | tf_op jit(solution)/shard_map/squeeze | solution.py:227
  80.7 1.3 collective-permute-start.18
  82.7 1.3 collective-permute-start.12
  85.5 4.6 %collective-permute-done.12 = bf16[112,512]{1,0:T(8,128)(2,1)S(1)} collective-permute-done((bf16[112,512]{1,0:T(8,128)(2,1)S(1)}, bf16[112,512]{1,0:T(8,128)(2,1)S(1)}, u32[]{:S(2)}, u32[]{:S(2)}) %collective-permute-start.12) | collective-permute-done | bytes 114720 | tf_op jit(solution)/shard_map/ppermute | solution.py:151
  90.1 1.5 collective-permute-start.31
  91.6 5.1 %collective-permute-done.18 = bf16[112,2560]{1,0:T(8,128)(2,1)S(1)} collective-permute-done((bf16[112,2560]{1,0:T(8,128)(2,1)S(1)}, bf16[112,2560]{1,0:T(8,128)(2,1)S(1)}, u32[]{:S(2)}, u32[]{:S(2)}) %collective-permute-start.18) | collective-permute-done | bytes 573472 | tf_op jit(solution)/shard_map/ppermute | solution.py:151
  96.7 2.0 %broadcast_select_fusion.2.up_ref = bf16[2,128,1280]{2,1,0:T(8,128)(2,1)} fusion(bf16[2,128,1280]{2,1,0:T(8,128)(2,1)} %collective-permute-done.6, bf16[2,128,1280]{2,1,0:T(8,128)(2,1)} %collective-permute-done.7, pred[]{:T(512)S(6)} %or.7), kind=kLoop, calls=%fused_computation.31 | loop fusion | flops 327680 | bytes 1966081 | tf_op jit(solution)/shard_map/jit(_where)/select_n | solution.py:269
  98.7 1.3 collective-permute-start.22
  100.1 1.3 collective-permute-start.19
  101.4 1.5 fusion
  102.9 6.1 %collective-permute-done.29 = bf16[112,2560]{1,0:T(8,128)(2,1)S(1)} collective-permute-done((bf16[112,2560]{1,0:T(8,128)(2,1)S(1)}, bf16[112,2560]{1,0:T(8,128)(2,1)S(1)}, u32[]{:S(2)}, u32[]{:S(2)}) %collective-permute-start.29) | collective-permute-done | bytes 573472 | tf_op jit(solution)/shard_map/ppermute | solution.py:151
  109.0 1.5 fusion.1
  110.5 1.7 %collective-permute-start.30 = (bf16[112,2560]{1,0:T(8,128)(2,1)}, bf16[112,2560]{1,0:T(8,128)(2,1)}, u32[]{:S(2)}, u32[]{:S(2)}) collective-permute-start(bf16[112,2560]{1,0:T(8,128)(2,1)} %fusion.1), channel_id=1, source_target_pairs={{0,4},{1,5},{2,6},{3,7},{4,0},{5,1},{6,2},{7,3},{8,12},{9,13},{10,... | collective-permute-start | bytes 1720328 | tf_op jit(solution)/shard_map/ppermute | solution.py:151
  112.2 5.8 %collective-permute-done.31 = bf16[112,2560]{1,0:T(8,128)(2,1)S(1)} collective-permute-done((bf16[112,2560]{1,0:T(8,128)(2,1)S(1)}, bf16[112,2560]{1,0:T(8,128)(2,1)S(1)}, u32[]{:S(2)}, u32[]{:S(2)}) %collective-permute-start.31) | collective-permute-done | bytes 573472 | tf_op jit(solution)/shard_map/ppermute | solution.py:151
  118.0 1.5 fusion.2
  119.5 2.0 %collective-permute-start.32 = (bf16[112,2560]{1,0:T(8,128)(2,1)}, bf16[112,2560]{1,0:T(8,128)(2,1)}, u32[]{:S(2)}, u32[]{:S(2)}) collective-permute-start(bf16[112,2560]{1,0:T(8,128)(2,1)} %fusion.2), channel_id=1, source_target_pairs={{0,2},{1,3},{2,0},{3,1},{4,6},{5,7},{6,4},{7,5},{8,10},{9,11},{10,... | collective-permute-start | bytes 1720328 | tf_op jit(solution)/shard_map/ppermute | solution.py:151
  121.5 1.5 collective-permute-start.21
  123.1 3.7 %collective-permute-done.22 = bf16[2,128,1280]{2,1,0:T(8,128)(2,1)S(1)} collective-permute-done((bf16[2,128,1280]{2,1,0:T(8,128)(2,1)S(1)}, bf16[2,128,1280]{2,1,0:T(8,128)(2,1)S(1)}, u32[]{:S(2)}, u32[]{:S(2)}) %collective-permute-start.22) | collective-permute-done | bytes 655392 | tf_op jit(solution)/shard_map/ppermute | solution.py:151
  126.8 1.5 collective-permute-start.20
  129.5 2.3 %collective-permute-start.33 = (bf16[1,128,1280]{2,1,0:T(8,128)(2,1)}, bf16[1,128,1280]{2,1,0:T(8,128)(2,1)}, u32[]{:S(2)}, u32[]{:S(2)}) collective-permute-start(bf16[1,128,1280]{2,1,0:T(8,128)(2,1)} %get-tuple-element.62), channel_id=1, source_target_pairs={{0,1},{1,0},{2,3},{3,2},{4,5},{5,4},{6,7},{7,6},{8,9},{9,8},{10,11... | collective-permute-start | bytes 983048 | tf_op jit(solution)/shard_map/ppermute | solution.py:151
  132.7 1.9 %reshape.294 = bf16[4,112,2,2,128]{4,3,2,1,0:T(2,128)(2,1)} reshape(bf16[4,112,512]{2,1,0:T(8,128)(2,1)} %broadcast_select_fusion.4) | data formatting | bytes 917504 | tf_op jit(solution)/shard_map/reshape | solution.py:276
  135.8 3.6 %collective-permute-done.21.up_ref = bf16[2,128,1280]{2,1,0:T(8,128)(2,1)} collective-permute-done((bf16[2,128,1280]{2,1,0:T(8,128)(2,1)}, bf16[2,128,1280]{2,1,0:T(8,128)(2,1)}, u32[]{:S(2)}, u32[]{:S(2)}) %collective-permute-start.21) | collective-permute-done | bytes 655392 | tf_op jit(solution)/shard_map/ppermute | solution.py:151
  139.5 1.5 collective-permute-start.23
  141.6 1.5 shard_map.108.refs_4_
  145.3 1.5 shard_map.109.refs_5_
  148.0 2.9 %collective-permute-done.23.up_ref = bf16[1,128,1280]{2,1,0:T(8,128)(2,1)S(1)} collective-permute-done((bf16[1,128,1280]{2,1,0:T(8,128)(2,1)S(1)}, bf16[1,128,1280]{2,1,0:T(8,128)(2,1)S(1)}, u32[]{:S(2)}, u32[]{:S(2)}) %collective-permute-start.23) | collective-permute-done | bytes 327712 | tf_op jit(solution)/shard_map/ppermute | solution.py:151
  151.1 4.7 %shard_map.112 = bf16[7,256,1280]{2,1,0:T(8,128)(2,1)} custom-call(bf16[112,2560]{1,0:T(8,128)(2,1)S(1)} %shard_map.104.refs_0_, bf16[112,2560]{1,0:T(8,128)(2,1)S(1)} %shard_map.105.refs_1_, bf16[112,2560]{1,0:T(8,128)(2,1)S(1)} %shard_map.106.refs_2_, bf16[112,2560]{1,0:T(8,128)(2,1)S(1)} %shard_map.107.refs_3_, bf16[112,2560]{1,0:T(8,128)(2,1)S(1)} %shard_map.108.refs_4_, ...), custom_call_target="tpu_custom_call" | custom-call | flops 1174405120 | bytes 4587520 | tf_op jit(solution)/shard_map/pallas_call | solution.py:76
  155.8 4.7 %shard_map.114 = bf16[7,256,1280]{2,1,0:T(8,128)(2,1)} custom-call(bf16[112,2560]{1,0:T(8,128)(2,1)S(1)} %shard_map.104.refs_0_, bf16[112,2560]{1,0:T(8,128)(2,1)S(1)} %shard_map.105.refs_1_, bf16[112,2560]{1,0:T(8,128)(2,1)S(1)} %shard_map.106.refs_2_, bf16[112,2560]{1,0:T(8,128)(2,1)S(1)} %shard_map.107.refs_3_, bf16[112,2560]{1,0:T(8,128)(2,1)S(1)} %shard_map.108.refs_4_, ...), custom_call_target="tpu_custom_call" | custom-call | flops 1174405120 | bytes 4587520 | tf_op jit(solution)/shard_map/pallas_call | solution.py:76
  (136 shorter events, 29.4 us)
Async XLA Ops:
  2.5 24.0 %collective-permute-start.3 = (bf16[112,1280]{1,0:T(8,128)(2,1)S(1)}, bf16[112,1280]{1,0:T(8,128)(2,1)S(1)}, u32[]{:S(2)}, u32[]{:S(2)}) collective-permute-start(bf16[112,1280]{1,0:T(8,128)(2,1)S(1)} %get-tuple-element.71), channel_id=1, source_target_pairs={{0,6},{1,7},{2,4},{3,5},{4,2},{5,3},{6,0},{7,1},{8,14},{9,15},{10,... | collective-permute-start | bytes 860168 | tf_op jit(solution)/shard_map/ppermute | solution.py:151
  7.6 24.4 %collective-permute-start.2 = (bf16[112,1280]{1,0:T(8,128)(2,1)S(1)}, bf16[112,1280]{1,0:T(8,128)(2,1)S(1)}, u32[]{:S(2)}, u32[]{:S(2)}) collective-permute-start(bf16[112,1280]{1,0:T(8,128)(2,1)S(1)} %get-tuple-element.71), channel_id=1, source_target_pairs={{0,4},{1,5},{2,6},{3,7},{4,0},{5,1},{6,2},{7,3},{8,12},{9,13},{10,... | collective-permute-start | bytes 860168 | tf_op jit(solution)/shard_map/ppermute | solution.py:151
  7.6 24.4 %collective-permute-start.1 = (bf16[112,1280]{1,0:T(8,128)(2,1)S(1)}, bf16[112,1280]{1,0:T(8,128)(2,1)}, u32[]{:S(2)}, u32[]{:S(2)}) collective-permute-start(bf16[112,1280]{1,0:T(8,128)(2,1)S(1)} %get-tuple-element.71), channel_id=1, source_target_pairs={{0,2},{1,3},{2,0},{3,1},{4,6},{5,7},{6,4},{7,5},{8,10},{9,11},{10,... | collective-permute-start | bytes 860168 | tf_op jit(solution)/shard_map/ppermute | solution.py:151
  8.3 8.6 %collective-permute-start.24 = (bf16[1,112,640]{2,1,0:T(8,128)(2,1)S(1)}, bf16[1,112,640]{2,1,0:T(8,128)(2,1)S(1)}, u32[]{:S(2)}, u32[]{:S(2)}) collective-permute-start(bf16[1,112,640]{2,1,0:T(8,128)(2,1)S(1)} %get-tuple-element.69), channel_id=1, source_target_pairs={{0,1},{1,0},{10,11},{11,10},{20,21},{21,20},{30,31},{31,30}} | collective-permute-start | bytes 430088 | tf_op jit(solution)/shard_map/ppermute | solution.py:151
  11.8 20.2 %collective-permute-start = (bf16[2,128,1280]{2,1,0:T(8,128)(2,1)}, bf16[2,128,1280]{2,1,0:T(8,128)(2,1)S(1)}, u32[]{:S(2)}, u32[]{:S(2)}) collective-permute-start(bf16[2,128,1280]{2,1,0:T(8,128)(2,1)} %bitcast.108), channel_id=1, source_target_pairs={{0,1},{1,0},{2,3},{3,2},{4,5},{5,4},{6,7},{7,6},{8,9},{9,8},{10,11... | collective-permute-start | bytes 1966088 | tf_op jit(solution)/shard_map/ppermute | solution.py:151
  17.6 7.2 %collective-permute-start.25 = (bf16[2,1,112,640]{3,2,1,0:T(8,128)(2,1)}, bf16[2,1,112,640]{3,2,1,0:T(8,128)(2,1)}, u32[]{:S(2)}, u32[]{:S(2)}) collective-permute-start(bf16[2,1,112,640]{3,2,1,0:T(8,128)(2,1)} %pad_maximum_fusion.6), channel_id=1, source_target_pairs={{0,16},{1,17},{10,26},{11,27},{20,4},{21,5},{30,14},{31,15}} | collective-permute-start | bytes 860168 | tf_op jit(solution)/shard_map/ppermute | solution.py:151
  20.5 11.5 %copy-start = (bf16[1,2,128,1280]{3,2,1,0:T(8,128)(2,1)S(1)}, bf16[1,2,128,1280]{3,2,1,0:T(8,128)(2,1)}, u32[]{:S(2)}) copy-start(bf16[1,2,128,1280]{3,2,1,0:T(8,128)(2,1)} %param.13) | copy-start | bytes 1966084
  24.8 17.0 %collective-permute-start.9 = (bf16[1280,256]{1,0:T(8,128)(2,1)}, bf16[1280,256]{1,0:T(8,128)(2,1)S(1)}, u32[]{:S(2)}, u32[]{:S(2)}) collective-permute-start(bf16[1280,256]{1,0:T(8,128)(2,1)} %bitcast.149), channel_id=1, source_target_pairs={{0,1},{1,0},{2,3},{3,2},{4,5},{5,4},{6,7},{7,6},{8,9},{9,8},{10,11... | collective-permute-start | bytes 1966088 | tf_op jit(solution)/shard_map/ppermute | solution.py:151
  26.5 16.5 %collective-permute-start.26 = (bf16[2,1,112,640]{3,2,1,0:T(8,128)(2,1)S(1)}, bf16[2,1,112,640]{3,2,1,0:T(8,128)(2,1)S(1)}, u32[]{:S(2)}, u32[]{:S(2)}) collective-permute-start(bf16[2,1,112,640]{3,2,1,0:T(8,128)(2,1)S(1)} %broadcast_select_fusion.5), channel_id=1, source_target_pairs={{0,8},{16,24},{1,9},{17,25},{10,2},{26,18},{11,3},{27,19},{20,28},... | collective-permute-start | bytes 860168 | tf_op jit(solution)/shard_map/ppermute | solution.py:151
  32.0 7.4 %copy-start.1 = (bf16[2,128,1280]{2,1,0:T(8,128)(2,1)}, bf16[2,128,1280]{2,1,0:T(8,128)(2,1)S(1)}, u32[]{:S(2)}) copy-start(bf16[2,128,1280]{2,1,0:T(8,128)(2,1)S(1)} %collective-permute-done.up_ref) | copy-start | bytes 1966084
  32.0 30.3 %collective-permute-start.6 = (bf16[2,128,1280]{2,1,0:T(8,128)(2,1)S(1)}, bf16[2,128,1280]{2,1,0:T(8,128)(2,1)}, u32[]{:S(2)}, u32[]{:S(2)}) collective-permute-start(bf16[2,128,1280]{2,1,0:T(8,128)(2,1)S(1)} %bitcast.109), channel_id=1, source_target_pairs={{2,4},{3,5},{4,2},{5,3},{10,12},{11,13},{12,10},{13,11},{18,20},{1... | collective-permute-start | bytes 1966088 | tf_op jit(solution)/shard_map/ppermute | solution.py:151
  34.7 10.6 %collective-permute-start.8 = (bf16[3,112,640]{2,1,0:T(8,128)(2,1)S(1)}, bf16[3,112,640]{2,1,0:T(8,128)(2,1)S(1)}, u32[]{:S(2)}, u32[]{:S(2)}) collective-permute-start(bf16[3,112,640]{2,1,0:T(8,128)(2,1)S(1)} %get-tuple-element.61), channel_id=1, source_target_pairs={{0,1},{1,0},{10,11},{11,10},{20,21},{21,20},{30,31},{31,30}} | collective-permute-start | bytes 1290248 | tf_op jit(solution)/shard_map/ppermute | solution.py:151
  38.1 9.6 %collective-permute-start.15 = (bf16[3,112,640]{2,1,0:T(8,128)(2,1)S(1)}, bf16[3,112,640]{2,1,0:T(8,128)(2,1)S(1)}, u32[]{:S(2)}, u32[]{:S(2)}) collective-permute-start(bf16[3,112,640]{2,1,0:T(8,128)(2,1)S(1)} %get-tuple-element.60), channel_id=1, source_target_pairs={{0,16},{1,17},{10,26},{11,27},{20,4},{21,5},{30,14},{31,15}} | collective-permute-start | bytes 1290248 | tf_op jit(solution)/shard_map/ppermute | solution.py:151
  40.6 1.6 copy-start.13
  41.7 34.0 %collective-permute-start.4 = (bf16[2,2,128,1280]{3,2,1,0:T(8,128)(2,1)}, bf16[2,2,128,1280]{3,2,1,0:T(8,128)(2,1)}, u32[]{:S(2)}, u32[]{:S(2)}) collective-permute-start(bf16[2,2,128,1280]{3,2,1,0:T(8,128)(2,1)} %pad_maximum_fusion), channel_id=1, source_target_pairs={{0,2},{1,3},{2,0},{3,1},{4,6},{5,7},{6,4},{7,5},{8,10},{9,11},{10,... | collective-permute-start | bytes 3932168 | tf_op jit(solution)/shard_map/ppermute | solution.py:151
  42.2 3.3 %copy-start.6 = (bf16[80,8,2,1280]{3,1,2,0:T(8,128)(2,1)S(1)}, bf16[80,8,2,1280]{3,1,2,0:T(8,128)(2,1)}, u32[]{:S(2)}) copy-start(bf16[80,8,2,1280]{3,1,2,0:T(8,128)(2,1)} %copy.47) | copy-start | bytes 9830404
  45.4 4.2 %collective-permute-start.10 = (f32[232,512]{1,0:T(8,128)S(1)}, f32[232,512]{1,0:T(8,128)S(1)}, u32[]{:S(2)}, u32[]{:S(2)}) collective-permute-start(f32[232,512]{1,0:T(8,128)S(1)} %pad_maximum_fusion.4), channel_id=1, source_target_pairs={{0,8},{1,9},{2,10},{3,11},{4,12},{5,13},{6,14},{7,15},{8,0},{9,1},... | collective-permute-start | bytes 1425416 | tf_op jit(solution)/shard_map/ppermute | solution.py:151
  46.1 15.4 %collective-permute-start.27 = (bf16[112,2560]{1,0:T(8,128)(2,1)S(1)}, bf16[112,2560]{1,0:T(8,128)(2,1)S(1)}, u32[]{:S(2)}, u32[]{:S(2)}) collective-permute-start(bf16[112,2560]{1,0:T(8,128)(2,1)S(1)} %convolution_convert_fusion.2), channel_id=1, source_target_pairs={{0,1},{1,0},{2,3},{3,2},{4,5},{5,4},{6,7},{7,6},{8,9},{9,8},{10,11... | collective-permute-start | bytes 1720328 | tf_op jit(solution)/shard_map/ppermute | solution.py:151
  47.7 8.8 %collective-permute-start.16 = (bf16[3,112,640]{2,1,0:T(8,128)(2,1)S(1)}, bf16[3,112,640]{2,1,0:T(8,128)(2,1)S(1)}, u32[]{:S(2)}, u32[]{:S(2)}) collective-permute-start(bf16[3,112,640]{2,1,0:T(8,128)(2,1)S(1)} %collective-permute-done.8), channel_id=1, source_target_pairs={{0,16},{1,17},{10,26},{11,27},{20,4},{21,5},{30,14},{31,15}} | collective-permute-start | bytes 1290248 | tf_op jit(solution)/shard_map/ppermute | solution.py:151
  49.7 9.4 %collective-permute-start.11 = (f32[120,512]{1,0:T(8,128)S(1)}, f32[120,512]{1,0:T(8,128)S(1)}, u32[]{:S(2)}, u32[]{:S(2)}) collective-permute-start(f32[120,512]{1,0:T(8,128)S(1)} %pad_maximum_fusion.7), channel_id=1, source_target_pairs={{0,16},{1,17},{2,18},{3,19},{4,20},{5,21},{6,22},{7,23},{8,24},{9,... | collective-permute-start | bytes 737288 | tf_op jit(solution)/shard_map/ppermute | solution.py:151
  59.2 19.6 %collective-permute-start.17 = (bf16[2,3,112,640]{3,2,1,0:T(8,128)(2,1)}, bf16[2,3,112,640]{3,2,1,0:T(8,128)(2,1)}, u32[]{:S(2)}, u32[]{:S(2)}) collective-permute-start(bf16[2,3,112,640]{3,2,1,0:T(8,128)(2,1)} %pad_maximum_fusion.3), channel_id=1, source_target_pairs={{0,8},{16,24},{1,9},{17,25},{10,2},{26,18},{11,3},{27,19},{20,28},... | collective-permute-start | bytes 2580488 | tf_op jit(solution)/shard_map/ppermute | solution.py:151
  62.3 29.3 %collective-permute-start.7 = (bf16[2,128,1280]{2,1,0:T(8,128)(2,1)}, bf16[2,128,1280]{2,1,0:T(8,128)(2,1)}, u32[]{:S(2)}, u32[]{:S(2)}) collective-permute-start(bf16[2,128,1280]{2,1,0:T(8,128)(2,1)} %collective-permute-done.6), channel_id=1, source_target_pairs={{2,0},{3,1},{4,6},{5,7},{10,8},{11,9},{12,14},{13,15},{18,16},{19,... | collective-permute-start | bytes 1966088 | tf_op jit(solution)/shard_map/ppermute | solution.py:151
  63.6 19.1 %collective-permute-start.14 = (bf16[112,512]{1,0:T(8,128)(2,1)S(1)}, bf16[112,512]{1,0:T(8,128)(2,1)S(1)}, u32[]{:S(2)}, u32[]{:S(2)}) collective-permute-start(bf16[112,512]{1,0:T(8,128)(2,1)S(1)} %fusion.11), channel_id=1, source_target_pairs={{6,0},{7,1},{12,10},{13,11},{18,20},{19,21},{24,30},{25,31}} | collective-permute-start | bytes 344072 | tf_op jit(solution)/shard_map/ppermute | solution.py:151
  64.9 19.8 %collective-permute-start.13 = (bf16[112,512]{1,0:T(8,128)(2,1)S(1)}, bf16[112,512]{1,0:T(8,128)(2,1)S(1)}, u32[]{:S(2)}, u32[]{:S(2)}) collective-permute-start(bf16[112,512]{1,0:T(8,128)(2,1)S(1)} %fusion.11), channel_id=1, source_target_pairs={{4,0},{5,1},{14,10},{15,11},{16,20},{17,21},{26,30},{27,31}} | collective-permute-start | bytes 344072 | tf_op jit(solution)/shard_map/ppermute | solution.py:151
  75.7 4.3 %copy-start.7 = (bf16[80,8,2,1280]{3,1,2,0:T(8,128)(2,1)S(1)}, bf16[80,8,2,1280]{3,1,2,0:T(8,128)(2,1)}, u32[]{:S(2)}) copy-start(bf16[80,8,2,1280]{3,1,2,0:T(8,128)(2,1)} %copy.47) | copy-start | bytes 9830404
  78.1 2.7 %copy-start.4 = (bf16[2,128,1280]{2,1,0:T(8,128)(2,1)}, bf16[2,128,1280]{2,1,0:T(8,128)(2,1)S(1)}, u32[]{:S(2)}) copy-start(bf16[2,128,1280]{2,1,0:T(8,128)(2,1)S(1)} %get-tuple-element.57.up_ref) | copy-start | bytes 1966084
  78.1 13.6 %collective-permute-start.5 = (bf16[2,128,1280]{2,1,0:T(8,128)(2,1)S(1)}, bf16[2,128,1280]{2,1,0:T(8,128)(2,1)S(1)}, u32[]{:S(2)}, u32[]{:S(2)}) collective-permute-start(bf16[2,128,1280]{2,1,0:T(8,128)(2,1)S(1)} %get-tuple-element.57.up_ref), channel_id=1, source_target_pairs={{2,4},{3,5},{4,2},{5,3},{10,12},{11,13},{12,10},{13,11},{18,20},{1... | collective-permute-start | bytes 1966088 | tf_op jit(solution)/shard_map/ppermute | solution.py:151
  80.7 16.0 %collective-permute-start.18 = (bf16[112,2560]{1,0:T(8,128)(2,1)S(1)}, bf16[112,2560]{1,0:T(8,128)(2,1)S(1)}, u32[]{:S(2)}, u32[]{:S(2)}) collective-permute-start(bf16[112,2560]{1,0:T(8,128)(2,1)S(1)} %convolution_convert_fusion.3), channel_id=1, source_target_pairs={{0,1},{1,0},{2,3},{3,2},{4,5},{5,4},{6,7},{7,6},{8,9},{9,8},{10,11... | collective-permute-start | bytes 1720328 | tf_op jit(solution)/shard_map/ppermute | solution.py:151
  82.7 40.3 %copy-start.8 = (bf16[112,512]{1,0:T(8,128)(2,1)}, bf16[112,512]{1,0:T(8,128)(2,1)S(1)}, u32[]{:S(2)}) copy-start(bf16[112,512]{1,0:T(8,128)(2,1)S(1)} %collective-permute-done.14) | copy-start | bytes 344068
  82.7 7.4 %collective-permute-start.12 = (bf16[112,512]{1,0:T(8,128)(2,1)S(1)}, bf16[112,512]{1,0:T(8,128)(2,1)S(1)}, u32[]{:S(2)}, u32[]{:S(2)}) collective-permute-start(bf16[112,512]{1,0:T(8,128)(2,1)S(1)} %fusion.11), channel_id=1, source_target_pairs={{2,0},{3,1},{8,10},{9,11},{22,20},{23,21},{28,30},{29,31}} | collective-permute-start | bytes 344072 | tf_op jit(solution)/shard_map/ppermute | solution.py:151
  84.7 38.3 %copy-start.10 = (bf16[112,512]{1,0:T(8,128)(2,1)}, bf16[112,512]{1,0:T(8,128)(2,1)S(1)}, u32[]{:S(2)}) copy-start(bf16[112,512]{1,0:T(8,128)(2,1)S(1)} %collective-permute-done.13) | copy-start | bytes 344068
  84.7 24.3 %collective-permute-start.29 = (bf16[112,2560]{1,0:T(8,128)(2,1)S(1)}, bf16[112,2560]{1,0:T(8,128)(2,1)S(1)}, u32[]{:S(2)}, u32[]{:S(2)}) collective-permute-start(bf16[112,2560]{1,0:T(8,128)(2,1)S(1)} %convolution_convert_fusion.1), channel_id=1, source_target_pairs={{0,1},{1,0},{2,3},{3,2},{4,5},{5,4},{6,7},{7,6},{8,9},{9,8},{10,11... | collective-permute-start | bytes 1720328 | tf_op jit(solution)/shard_map/ppermute | solution.py:151
  90.1 27.8 %collective-permute-start.31 = (bf16[112,2560]{1,0:T(8,128)(2,1)S(1)}, bf16[112,2560]{1,0:T(8,128)(2,1)S(1)}, u32[]{:S(2)}, u32[]{:S(2)}) collective-permute-start(bf16[112,2560]{1,0:T(8,128)(2,1)S(1)} %convolution_convert_fusion), channel_id=1, source_target_pairs={{0,1},{1,0},{2,3},{3,2},{4,5},{5,4},{6,7},{7,6},{8,9},{9,8},{10,11... | collective-permute-start | bytes 1720328 | tf_op jit(solution)/shard_map/ppermute | solution.py:151
  98.7 28.1 %collective-permute-start.22 = (bf16[2,128,1280]{2,1,0:T(8,128)(2,1)S(1)}, bf16[2,128,1280]{2,1,0:T(8,128)(2,1)S(1)}, u32[]{:S(2)}, u32[]{:S(2)}) collective-permute-start(bf16[2,128,1280]{2,1,0:T(8,128)(2,1)S(1)} %collective-permute-done.5), channel_id=1, source_target_pairs={{2,0},{3,1},{4,6},{5,7},{10,8},{11,9},{12,14},{13,15},{18,16},{19,... | collective-permute-start | bytes 1966088 | tf_op jit(solution)/shard_map/ppermute | solution.py:151
  100.1 21.4 %collective-permute-start.19 = (bf16[4,112,512]{2,1,0:T(8,128)(2,1)S(1)}, bf16[4,112,512]{2,1,0:T(8,128)(2,1)S(1)}, u32[]{:S(2)}, u32[]{:S(2)}) collective-permute-start(bf16[4,112,512]{2,1,0:T(8,128)(2,1)S(1)} %pad_maximum_fusion.5), channel_id=1, source_target_pairs={{0,16},{1,17},{10,26},{11,27},{20,4},{21,5},{30,14},{31,15}} | collective-permute-start | bytes 1376264 | tf_op jit(solution)/shard_map/ppermute | solution.py:151
  102.8 48.2 %collective-permute-start.28 = (bf16[112,2560]{1,0:T(8,128)(2,1)}, bf16[112,2560]{1,0:T(8,128)(2,1)}, u32[]{:S(2)}, u32[]{:S(2)}) collective-permute-start(bf16[112,2560]{1,0:T(8,128)(2,1)} %fusion), channel_id=1, source_target_pairs={{0,6},{1,7},{2,4},{3,5},{4,2},{5,3},{6,0},{7,1},{8,14},{9,15},{10,... | collective-permute-start | bytes 1720328 | tf_op jit(solution)/shard_map/ppermute | solution.py:151
  110.5 40.6 %collective-permute-start.30 = (bf16[112,2560]{1,0:T(8,128)(2,1)}, bf16[112,2560]{1,0:T(8,128)(2,1)}, u32[]{:S(2)}, u32[]{:S(2)}) collective-permute-start(bf16[112,2560]{1,0:T(8,128)(2,1)} %fusion.1), channel_id=1, source_target_pairs={{0,4},{1,5},{2,6},{3,7},{4,0},{5,1},{6,2},{7,3},{8,12},{9,13},{10,... | collective-permute-start | bytes 1720328 | tf_op jit(solution)/shard_map/ppermute | solution.py:151
  119.5 31.6 %collective-permute-start.32 = (bf16[112,2560]{1,0:T(8,128)(2,1)}, bf16[112,2560]{1,0:T(8,128)(2,1)}, u32[]{:S(2)}, u32[]{:S(2)}) collective-permute-start(bf16[112,2560]{1,0:T(8,128)(2,1)} %fusion.2), channel_id=1, source_target_pairs={{0,2},{1,3},{2,0},{3,1},{4,6},{5,7},{6,4},{7,5},{8,10},{9,11},{10,... | collective-permute-start | bytes 1720328 | tf_op jit(solution)/shard_map/ppermute | solution.py:151
  121.5 18.0 %collective-permute-start.21 = (bf16[2,128,1280]{2,1,0:T(8,128)(2,1)}, bf16[2,128,1280]{2,1,0:T(8,128)(2,1)}, u32[]{:S(2)}, u32[]{:S(2)}) collective-permute-start(bf16[2,128,1280]{2,1,0:T(8,128)(2,1)} %broadcast_select_fusion.2.up_ref), channel_id=1, source_target_pairs={{0,1},{1,0},{2,3},{3,2},{4,5},{5,4},{6,7},{7,6},{8,9},{9,8},{10,11... | collective-permute-start | bytes 1966088 | tf_op jit(solution)/shard_map/ppermute | solution.py:151
  123.1 8.7 %copy-start.9 = (bf16[112,512]{1,0:T(8,128)(2,1)S(1)}, bf16[112,512]{1,0:T(8,128)(2,1)}, u32[]{:S(2)}) copy-start(bf16[112,512]{1,0:T(8,128)(2,1)} %copy-done.8) | copy-start | bytes 344068
  123.1 8.7 %copy-start.11 = (bf16[112,512]{1,0:T(8,128)(2,1)S(1)}, bf16[112,512]{1,0:T(8,128)(2,1)}, u32[]{:S(2)}) copy-start(bf16[112,512]{1,0:T(8,128)(2,1)} %copy-done.10) | copy-start | bytes 344068
  126.8 2.7 %collective-permute-start.20 = (bf16[4,112,512]{2,1,0:T(8,128)(2,1)S(1)}, bf16[4,112,512]{2,1,0:T(8,128)(2,1)S(1)}, u32[]{:S(2)}, u32[]{:S(2)}) collective-permute-start(bf16[4,112,512]{2,1,0:T(8,128)(2,1)S(1)} %broadcast_select_fusion.3), channel_id=1, source_target_pairs={{0,8},{16,24},{1,9},{17,25},{10,2},{26,18},{11,3},{27,19},{20,28},... | collective-permute-start | bytes 1376264 | tf_op jit(solution)/shard_map/ppermute | solution.py:151
  129.5 17.3 %collective-permute-start.33 = (bf16[1,128,1280]{2,1,0:T(8,128)(2,1)}, bf16[1,128,1280]{2,1,0:T(8,128)(2,1)}, u32[]{:S(2)}, u32[]{:S(2)}) collective-permute-start(bf16[1,128,1280]{2,1,0:T(8,128)(2,1)} %get-tuple-element.62), channel_id=1, source_target_pairs={{0,1},{1,0},{2,3},{3,2},{4,5},{5,4},{6,7},{7,6},{8,9},{9,8},{10,11... | collective-permute-start | bytes 983048 | tf_op jit(solution)/shard_map/ppermute | solution.py:151
  135.7 3.8 %copy-start.12 = (bf16[1,128,1280]{2,1,0:T(8,128)(2,1)S(1)}, bf16[1,128,1280]{2,1,0:T(8,128)(2,1)}, u32[]{:S(2)}) copy-start(bf16[1,128,1280]{2,1,0:T(8,128)(2,1)} %get-tuple-element.63) | copy-start | bytes 983044
  135.7 5.3 %copy-start.5 = (bf16[2,128,1280]{2,1,0:T(8,128)(2,1)S(1)}, bf16[2,128,1280]{2,1,0:T(8,128)(2,1)}, u32[]{:S(2)}) copy-start(bf16[2,128,1280]{2,1,0:T(8,128)(2,1)} %copy-done.4) | copy-start | bytes 1966084
  139.5 11.4 %collective-permute-start.23 = (bf16[1,128,1280]{2,1,0:T(8,128)(2,1)S(1)}, bf16[1,128,1280]{2,1,0:T(8,128)(2,1)S(1)}, u32[]{:S(2)}, u32[]{:S(2)}) collective-permute-start(bf16[1,128,1280]{2,1,0:T(8,128)(2,1)S(1)} %copy-done.12), channel_id=1, source_target_pairs={{0,1},{1,0},{2,3},{3,2},{4,5},{5,4},{6,7},{7,6},{8,9},{9,8},{10,11... | collective-permute-start | bytes 983048 | tf_op jit(solution)/shard_map/ppermute | solution.py:151
  143.1 1.1 copy-start.2
  143.6 1.1 copy-start.3

commit v5 on v4

--- a/solution.py
+++ b/solution.py
@@ -38,9 +38,10 @@
     )(rank, up, scale)
 
 
-def mix_kernel(*refs, adapters, parts):
+def mix_kernel(*refs, adapters, parts, steps):
     deltas, bases = refs[:adapters], refs[adapters : adapters + parts]
-    scale_ref, pick_ref, out_ref, rows_ref = refs[adapters + parts :]
+    last_ref, scale_ref, pick_ref, query_ref, value_ref, rows_ref = refs[adapters + parts :]
+    half = pl.program_id(0) // steps
     tokens = scale_ref.shape[0]
     groups = tokens // GROUP
     used = adapters * GROUP
@@ -58,40 +59,56 @@
     for g in range(groups):
         here = slice(g * GROUP, (g + 1) * GROUP)
         for a in range(adapters):
-            rows_ref[g, a * GROUP : (a + 1) * GROUP, :] = deltas[a][here, :]
+            delta = deltas[a][here, :]
+            if a == adapters - 1:
+                delta = jnp.where(half == 0, delta, last_ref[here, :])
+            rows_ref[g, a * GROUP : (a + 1) * GROUP, :] = delta
         rows_ref[g, used : used + GROUP, :] = high[here, :]
         rows_ref[g, used + GROUP : used + 2 * GROUP, :] = low[here, :]
-    for g in range(groups):
-        mixed = jnp.dot(pick_ref[g], rows_ref[g], preferred_element_type=jnp.float32)
-        out_ref[g] = mixed.astype(jnp.bfloat16)
-
-
-def mix(deltas, bases, scale, pick, half):
-    tokens, width = deltas[0].shape[0], deltas[0].shape[1] // 2
+
+    def fill(out_ref):
+        for g in range(groups):
+            mixed = jnp.dot(pick_ref[g], rows_ref[g], preferred_element_type=jnp.float32)
+            out_ref[g] = mixed.astype(jnp.bfloat16)
+
+    pl.when(half == 0)(lambda: fill(query_ref))
+    pl.when(half == 1)(lambda: fill(value_ref))
+
+
+def mix(deltas, bases, scale, pick):
+    tokens, width = deltas[-1].shape
     groups, rows, depth = pick.shape
     block = next(n for n in (640, 256, 128) if width % n == 0)
     steps = width // block
-    column = pl.BlockSpec((tokens, block), lambda i: (0, half * steps + i))
-    single = pl.BlockSpec((tokens, block), lambda i: (0, i))
-    out = pl.pallas_call(
-        functools.partial(mix_kernel, adapters=len(deltas), parts=len(bases)),
-        grid=(steps,),
-        in_specs=[column if value.shape[1] > width else single for value in (*deltas, *bases)]
+    column = pl.BlockSpec((tokens, block), lambda i: (0, i))
+    query = pl.BlockSpec((tokens, block), lambda i: (0, jnp.minimum(i, steps - 1)))
+    value = pl.BlockSpec((tokens, block), lambda i: (0, jnp.maximum(i - steps, 0)))
+    shape = jax.ShapeDtypeStruct((groups, rows, width), jnp.bfloat16)
+    outs = pl.pallas_call(
+        functools.partial(mix_kernel, adapters=len(deltas) - 1, parts=len(bases), steps=steps),
+        grid=(2 * steps,),
+        in_specs=[column] * (len(deltas) - 2)
+        + [query]
+        + [column] * len(bases)
         + [
+            value,
             pl.BlockSpec((tokens, 1), lambda i: (0, 0)),
             pl.BlockSpec((groups, rows, depth), lambda i: (0, 0, 0)),
         ],
-        out_specs=pl.BlockSpec((groups, rows, block), lambda i: (0, 0, i)),
+        out_specs=[
+            pl.BlockSpec((groups, rows, block), lambda i: (0, 0, jnp.minimum(i, steps - 1))),
+            pl.BlockSpec((groups, rows, block), lambda i: (0, 0, jnp.maximum(i - steps, 0))),
+        ],
         scratch_shapes=[pltpu.VMEM((groups, depth, block), jnp.bfloat16)],
-        out_shape=jax.ShapeDtypeStruct((groups, rows, width), jnp.bfloat16),
-        compiler_params=pltpu.CompilerParams(vmem_limit_bytes=40 * 1024 * 1024),
+        out_shape=[shape, shape],
+        compiler_params=pltpu.CompilerParams(vmem_limit_bytes=58 * 1024 * 1024),
         cost_estimate=pl.CostEstimate(
-            flops=2 * groups * rows * depth * width,
-            bytes_accessed=2 * groups * rows * width,
+            flops=4 * groups * rows * depth * width,
+            bytes_accessed=4 * groups * rows * width,
             transcendentals=0,
         ),
-    )(*deltas, *bases, scale, pick)
-    return out.reshape(tokens, SLOTS, width)
+    )(*deltas[:-1], *bases, deltas[-1], scale, pick)
+    return tuple(out.reshape(tokens, SLOTS, width) for out in outs)
 
 
 def pick_matrix(
@@ -308,16 +325,10 @@
         depth,
         order,
     )
-    outs = []
-    deltas = [corrections(ranks[e], ups[e], scale) for e in range(adapters) if not isinstance(ups[e], list)]
-    for half in range(2):
-        own = [
-            corrections(ranks[e, half : half + 1], ups[e][half], scale)
-            for e in range(adapters)
-            if isinstance(ups[e], list)
-        ]
-        outs.append(mix(deltas + own, bases, scale, pick, half))
-    return tuple(outs)
+    deltas = [corrections(ranks[e], ups[e], scale) for e in range(adapters - 1)]
+    last = ups[-1] if isinstance(ups[-1], list) else [ups[-1][:1], ups[-1][1:]]
+    deltas += [corrections(ranks[-1, half : half + 1], last[half], scale) for half in range(2)]
+    return mix(deltas, bases, scale, pick)
 
 
 def solution(mesh):

time: 161 us -> 164 us (1.019)
  local copies, waits for them, and re-layouts: 12 us -> 15.2 us
  other arithmetic: 15.3 us -> 13.4 us
    unnamed x29 -> x39, local copies, waits for them, and re-layouts: 4.38 us -> 8.43 us
    pallas_call x2 -> x1, Pallas kernels: 9.45 us -> 9.8 us  [mix(): pl.pallas_call(functools.partial(mix_kernel, adapters=len(deltas) - 1, pa...]
  transfers between devices with their start and end apart: 34 -> 34, of which waited for: 15 -> 16; matrix products, arithmetic and copies ran while one was open for 21% -> 20% of each run, Pallas kernels for 4% -> 5%
where the time goes in v5:
time: 164 us; the launch traced here: 163 us
  waiting for transfers between devices  57.6 us (35%)
  starting transfers between devices  48.9 us (30%)
  Pallas kernels  17.2 us (10%)
  local copies, waits for them, and re-layouts  15.2 us (9%)
  other arithmetic  13.4 us (8%)
  matrix products  9.56 us (6%)
    ppermute x34, waiting for transfers between devices, send(): return lax.ppermute(value, ('row', 'col'), flat)  57.6 us
    ppermute x34, starting transfers between devices, send(): return lax.ppermute(value, ('row', 'col'), flat)  48.9 us
    pallas_call x1, Pallas kernels, mix(): pl.pallas_call(functools.partial(mix_kernel, adapters=len(deltas) - 1, pa...  9.8 us
    dot_general x8, matrix products, product(): return jnp.dot(value, weight, preferred_element_type=jnp.float32)  8.81 us
    unnamed x39, local copies, waits for them, and re-layouts  8.43 us
    pallas_call x9, Pallas kernels, corrections(): pl.pallas_call(delta_kernel, grid=(n,), in_specs=[pl.BlockSpec((1, tokens...  7.37 us
  transfers between devices with their start and end apart: 34, of which 16 were waited for; matrix products, arithmetic and copies ran while one was open for 20% of the time, Pallas kernels for 5%

profile of v5, /device:TPU:0, one launch (start us, length us, event | category | flops | bytes accessed | tf_op | source)
XLA Modules:
  0.0 163.4 jit_solution(17844519168987500761)
XLA Ops:
  2.5 5.1 %collective-permute-start.3 = (bf16[112,1280]{1,0:T(8,128)(2,1)S(1)}, bf16[112,1280]{1,0:T(8,128)(2,1)S(1)}, u32[]{:S(2)}, u32[]{:S(2)}) collective-permute-start(bf16[112,1280]{1,0:T(8,128)(2,1)S(1)} %get-tuple-element.75), channel_id=1, source_target_pairs={{0,6},{1,7},{2,4},{3,5},{4,2},{5,3},{6,0},{7,1},{8,14},{9,15},{10,... | collective-permute-start | bytes 860168 | tf_op jit(solution)/shard_map/ppermute | solution.py:168
  8.3 3.6 %collective-permute-start.24 = (bf16[1,112,640]{2,1,0:T(8,128)(2,1)S(1)}, bf16[1,112,640]{2,1,0:T(8,128)(2,1)S(1)}, u32[]{:S(2)}, u32[]{:S(2)}) collective-permute-start(bf16[1,112,640]{2,1,0:T(8,128)(2,1)S(1)} %get-tuple-element.73), channel_id=1, source_target_pairs={{0,1},{1,0},{10,11},{11,10},{20,21},{21,20},{30,31},{31,30}} | collective-permute-start | bytes 430088 | tf_op jit(solution)/shard_map/ppermute | solution.py:168
  16.9 1.3 collective-permute-start.25
  18.4 1.5 fusion.4.refs_14_
  19.9 4.2 %copy.44 = bf16[80,8,2,1280]{3,1,2,0:T(8,128)(2,1)} copy(bf16[80,8,2,1280]{3,2,1,0:T(2,128)(2,1)} %bitcast.120) | data formatting | bytes 6553600
  24.1 1.6 %collective-permute-start.9 = (bf16[1280,256]{1,0:T(8,128)(2,1)}, bf16[1280,256]{1,0:T(8,128)(2,1)S(1)}, u32[]{:S(2)}, u32[]{:S(2)}) collective-permute-start(bf16[1280,256]{1,0:T(8,128)(2,1)} %bitcast.148), channel_id=1, source_target_pairs={{0,1},{1,0},{2,3},{3,2},{4,5},{5,4},{6,7},{7,6},{8,9},{9,8},{10,11... | collective-permute-start | bytes 1966088 | tf_op jit(solution)/shard_map/ppermute | solution.py:168
  25.8 1.3 collective-permute-start.26
  27.2 4.8 %collective-permute-done.2 = bf16[112,1280]{1,0:T(8,128)(2,1)S(1)} collective-permute-done((bf16[112,1280]{1,0:T(8,128)(2,1)S(1)}, bf16[112,1280]{1,0:T(8,128)(2,1)S(1)}, u32[]{:S(2)}, u32[]{:S(2)}) %collective-permute-start.2) | collective-permute-done | bytes 286752 | tf_op jit(solution)/shard_map/ppermute | solution.py:168
  32.0 1.5 collective-permute-start.6
  33.7 3.4 %collective-permute-start.8 = (bf16[3,112,640]{2,1,0:T(8,128)(2,1)S(1)}, bf16[3,112,640]{2,1,0:T(8,128)(2,1)S(1)}, u32[]{:S(2)}, u32[]{:S(2)}) collective-permute-start(bf16[3,112,640]{2,1,0:T(8,128)(2,1)S(1)} %get-tuple-element.65), channel_id=1, source_target_pairs={{0,1},{1,0},{10,11},{11,10},{20,21},{21,20},{30,31},{31,30}} | collective-permute-start | bytes 1290248 | tf_op jit(solution)/shard_map/ppermute | solution.py:168
  37.2 1.3 collective-permute-start.15
  40.7 1.5 collective-permute-start.4
  43.0 2.3 %collective-permute-done.8 = bf16[3,112,640]{2,1,0:T(8,128)(2,1)S(1)} collective-permute-done((bf16[3,112,640]{2,1,0:T(8,128)(2,1)S(1)}, bf16[3,112,640]{2,1,0:T(8,128)(2,1)S(1)}, u32[]{:S(2)}, u32[]{:S(2)}) %collective-permute-start.8) | collective-permute-done | bytes 430112 | tf_op jit(solution)/shard_map/ppermute | solution.py:168
  46.2 1.6 collective-permute-start.27
  47.7 1.3 collective-permute-start.16
  49.3 7.2 %collective-permute-done.16 = bf16[3,112,640]{2,1,0:T(8,128)(2,1)S(1)} collective-permute-done((bf16[3,112,640]{2,1,0:T(8,128)(2,1)S(1)}, bf16[3,112,640]{2,1,0:T(8,128)(2,1)S(1)}, u32[]{:S(2)}, u32[]{:S(2)}) %collective-permute-start.16) | collective-permute-done | bytes 430112 | tf_op jit(solution)/shard_map/ppermute | solution.py:168
  57.6 1.5 collective-permute-done.11
  59.2 2.2 %collective-permute-start.17 = (bf16[2,3,112,640]{3,2,1,0:T(8,128)(2,1)}, bf16[2,3,112,640]{3,2,1,0:T(8,128)(2,1)}, u32[]{:S(2)}, u32[]{:S(2)}) collective-permute-start(bf16[2,3,112,640]{3,2,1,0:T(8,128)(2,1)} %pad_maximum_fusion.3), channel_id=1, source_target_pairs={{0,8},{16,24},{1,9},{17,25},{10,2},{26,18},{11,3},{27,19},{20,28},... | collective-permute-start | bytes 2580488 | tf_op jit(solution)/shard_map/ppermute | solution.py:168
  61.6 1.7 %convolution_add_fusion.3.refs_8_ = f32[112,2560]{1,0:T(8,128)} fusion(bf16[640,2560]{1,0:T(8,128)(2,1)S(1)} %bitcast.113, bf16[112,2560]{1,0:T(8,128)(2,1)S(1)} %collective-permute-done.27, bf16[2,1,112,640]{3,2,1,0:T(8,128)(2,1)S(1)} %broadcast_select_fusion.6), kind=kOutput, calls=%fused_computation.3 | convolution fusion | flops 367575040 | bytes 5140480 | tf_op jit(solution)/shard_map/dot_general | solution.py:231
  63.3 1.3 collective-permute-start.7
  64.6 1.3 collective-permute-start.14
  65.9 1.3 collective-permute-start.13
  67.4 7.4 %collective-permute-done.4 = bf16[2,2,128,1280]{3,2,1,0:T(8,128)(2,1)} collective-permute-done((bf16[2,2,128,1280]{3,2,1,0:T(8,128)(2,1)}, bf16[2,2,128,1280]{3,2,1,0:T(8,128)(2,1)}, u32[]{:S(2)}, u32[]{:S(2)}) %collective-permute-start.4) | collective-permute-done | bytes 1310752 | tf_op jit(solution)/shard_map/ppermute | solution.py:168
  74.8 1.5 slice_bitcast_fusion
  79.0 1.4 collective-permute-start.18
  81.0 1.3 collective-permute-start.12
  83.8 6.3 %collective-permute-done.12 = bf16[112,512]{1,0:T(8,128)(2,1)S(1)} collective-permute-done((bf16[112,512]{1,0:T(8,128)(2,1)S(1)}, bf16[112,512]{1,0:T(8,128)(2,1)S(1)}, u32[]{:S(2)}, u32[]{:S(2)}) %collective-permute-start.12) | collective-permute-done | bytes 114720 | tf_op jit(solution)/shard_map/ppermute | solution.py:168
  90.1 1.5 collective-permute-start.31
  91.6 3.3 %collective-permute-done.18 = bf16[112,2560]{1,0:T(8,128)(2,1)S(1)} collective-permute-done((bf16[112,2560]{1,0:T(8,128)(2,1)S(1)}, bf16[112,2560]{1,0:T(8,128)(2,1)S(1)}, u32[]{:S(2)}, u32[]{:S(2)}) %collective-permute-start.18) | collective-permute-done | bytes 573472 | tf_op jit(solution)/shard_map/ppermute | solution.py:168
  94.9 2.0 %broadcast_select_fusion.2.up_ref = bf16[2,128,1280]{2,1,0:T(8,128)(2,1)} fusion(bf16[2,128,1280]{2,1,0:T(8,128)(2,1)} %collective-permute-done.6, bf16[2,128,1280]{2,1,0:T(8,128)(2,1)} %collective-permute-done.7, pred[]{:T(512)S(6)} %or.7), kind=kLoop, calls=%fused_computation.31 | loop fusion | flops 327680 | bytes 1966081 | tf_op jit(solution)/shard_map/jit(_where)/select_n | solution.py:286
  98.3 2.9 %collective-permute-start.19 = (bf16[4,112,512]{2,1,0:T(8,128)(2,1)S(1)}, bf16[4,112,512]{2,1,0:T(8,128)(2,1)S(1)}, u32[]{:S(2)}, u32[]{:S(2)}) collective-permute-start(bf16[4,112,512]{2,1,0:T(8,128)(2,1)S(1)} %pad_maximum_fusion.5), channel_id=1, source_target_pairs={{0,16},{1,17},{10,26},{11,27},{20,4},{21,5},{30,14},{31,15}} | collective-permute-start | bytes 1376264 | tf_op jit(solution)/shard_map/ppermute | solution.py:168
  101.1 1.5 fusion
  102.6 4.6 %collective-permute-done.29 = bf16[112,2560]{1,0:T(8,128)(2,1)S(1)} collective-permute-done((bf16[112,2560]{1,0:T(8,128)(2,1)S(1)}, bf16[112,2560]{1,0:T(8,128)(2,1)S(1)}, u32[]{:S(2)}, u32[]{:S(2)}) %collective-permute-start.29) | collective-permute-done | bytes 573472 | tf_op jit(solution)/shard_map/ppermute | solution.py:168
  107.2 1.5 fusion.1
  108.7 2.1 %collective-permute-start.30 = (bf16[112,2560]{1,0:T(8,128)(2,1)}, bf16[112,2560]{1,0:T(8,128)(2,1)}, u32[]{:S(2)}, u32[]{:S(2)}) collective-permute-start(bf16[112,2560]{1,0:T(8,128)(2,1)} %fusion.1), channel_id=1, source_target_pairs={{0,4},{1,5},{2,6},{3,7},{4,0},{5,1},{6,2},{7,3},{8,12},{9,13},{10,... | collective-permute-start | bytes 1720328 | tf_op jit(solution)/shard_map/ppermute | solution.py:168
  110.8 7.5 %collective-permute-done.31 = bf16[112,2560]{1,0:T(8,128)(2,1)S(1)} collective-permute-done((bf16[112,2560]{1,0:T(8,128)(2,1)S(1)}, bf16[112,2560]{1,0:T(8,128)(2,1)S(1)}, u32[]{:S(2)}, u32[]{:S(2)}) %collective-permute-start.31) | collective-permute-done | bytes 573472 | tf_op jit(solution)/shard_map/ppermute | solution.py:168
  118.3 1.5 fusion.2
  119.8 1.7 %collective-permute-start.32 = (bf16[112,2560]{1,0:T(8,128)(2,1)}, bf16[112,2560]{1,0:T(8,128)(2,1)}, u32[]{:S(2)}, u32[]{:S(2)}) collective-permute-start(bf16[112,2560]{1,0:T(8,128)(2,1)} %fusion.2), channel_id=1, source_target_pairs={{0,2},{1,3},{2,0},{3,1},{4,6},{5,7},{6,4},{7,5},{8,10},{9,11},{10,... | collective-permute-start | bytes 1720328 | tf_op jit(solution)/shard_map/ppermute | solution.py:168
  122.4 6.4 %collective-permute-done.22 = bf16[2,128,1280]{2,1,0:T(8,128)(2,1)S(1)} collective-permute-done((bf16[2,128,1280]{2,1,0:T(8,128)(2,1)S(1)}, bf16[2,128,1280]{2,1,0:T(8,128)(2,1)S(1)}, u32[]{:S(2)}, u32[]{:S(2)}) %collective-permute-start.22) | collective-permute-done | bytes 655392 | tf_op jit(solution)/shard_map/ppermute | solution.py:168
  128.7 1.5 collective-permute-start.20
  131.5 1.3 collective-permute-start.33
  133.7 1.9 %reshape.294 = bf16[4,112,2,2,128]{4,3,2,1,0:T(2,128)(2,1)} reshape(bf16[4,112,512]{2,1,0:T(8,128)(2,1)} %broadcast_select_fusion.4) | data formatting | bytes 917504 | tf_op jit(solution)/shard_map/reshape | solution.py:293
  136.8 2.6 %collective-permute-done.21.up_ref = bf16[2,128,1280]{2,1,0:T(8,128)(2,1)} collective-permute-done((bf16[2,128,1280]{2,1,0:T(8,128)(2,1)}, bf16[2,128,1280]{2,1,0:T(8,128)(2,1)}, u32[]{:S(2)}, u32[]{:S(2)}) %collective-permute-start.21) | collective-permute-done | bytes 655392 | tf_op jit(solution)/shard_map/ppermute | solution.py:168
  141.6 1.5 shard_map.108.refs_4_
  147.1 1.7 %shard_map.109.refs_5_ = bf16[112,2560]{1,0:T(8,128)(2,1)S(1)} custom-call(bf16[2,112,128]{2,1,0:T(8,128)(2,1)S(1)} %get-tuple-element.79.rank_ref, bf16[2,128,1280]{2,1,0:T(8,128)(2,1)} %collective-permute-done.21.up_ref, f32[112,1]{1,0:T(8,128)S(1)} %copy.33.scale_ref.refs_13_), custom_call_target="tpu_custom_call" | custom-call | flops 73400320 | bytes 1228800 | tf_op jit(solution)/shard_map/pallas_call | solution.py:22
  148.9 1.4 shard_map.112.refs_12_
  151.0 1.5 collective-permute-done.23.up_ref
  153.4 9.8 %shard_map.113 = (bf16[7,256,1280]{2,1,0:T(8,128)(2,1)}, bf16[7,256,1280]{2,1,0:T(8,128)(2,1)}) custom-call(bf16[112,2560]{1,0:T(8,128)(2,1)} %copy-done.4, bf16[112,2560]{1,0:T(8,128)(2,1)} %copy-done.6, bf16[112,2560]{1,0:T(8,128)(2,1)} %copy-done.2, bf16[112,2560]{1,0:T(8,128)(2,1)} %copy-done.7, bf16[112,2560]{1,0:T(8,128)(2,1)} %copy-done.3, ...), custom_call_target="tpu_custom_call" | custom-call | flops 2348810240 | bytes 9175040 | tf_op jit(solution)/shard_map/pallas_call | solution.py:87
  (145 shorter events, 31.6 us)
Async XLA Ops:
  2.5 23.4 %collective-permute-start.3 = (bf16[112,1280]{1,0:T(8,128)(2,1)S(1)}, bf16[112,1280]{1,0:T(8,128)(2,1)S(1)}, u32[]{:S(2)}, u32[]{:S(2)}) collective-permute-start(bf16[112,1280]{1,0:T(8,128)(2,1)S(1)} %get-tuple-element.75), channel_id=1, source_target_pairs={{0,6},{1,7},{2,4},{3,5},{4,2},{5,3},{6,0},{7,1},{8,14},{9,15},{10,... | collective-permute-start | bytes 860168 | tf_op jit(solution)/shard_map/ppermute | solution.py:168
  7.6 24.4 %collective-permute-start.2 = (bf16[112,1280]{1,0:T(8,128)(2,1)S(1)}, bf16[112,1280]{1,0:T(8,128)(2,1)S(1)}, u32[]{:S(2)}, u32[]{:S(2)}) collective-permute-start(bf16[112,1280]{1,0:T(8,128)(2,1)S(1)} %get-tuple-element.75), channel_id=1, source_target_pairs={{0,4},{1,5},{2,6},{3,7},{4,0},{5,1},{6,2},{7,3},{8,12},{9,13},{10,... | collective-permute-start | bytes 860168 | tf_op jit(solution)/shard_map/ppermute | solution.py:168
  7.6 24.4 %collective-permute-start.1 = (bf16[112,1280]{1,0:T(8,128)(2,1)S(1)}, bf16[112,1280]{1,0:T(8,128)(2,1)S(1)}, u32[]{:S(2)}, u32[]{:S(2)}) collective-permute-start(bf16[112,1280]{1,0:T(8,128)(2,1)S(1)} %get-tuple-element.75), channel_id=1, source_target_pairs={{0,2},{1,3},{2,0},{3,1},{4,6},{5,7},{6,4},{7,5},{8,10},{9,11},{10,... | collective-permute-start | bytes 860168 | tf_op jit(solution)/shard_map/ppermute | solution.py:168
  8.3 8.6 %collective-permute-start.24 = (bf16[1,112,640]{2,1,0:T(8,128)(2,1)S(1)}, bf16[1,112,640]{2,1,0:T(8,128)(2,1)S(1)}, u32[]{:S(2)}, u32[]{:S(2)}) collective-permute-start(bf16[1,112,640]{2,1,0:T(8,128)(2,1)S(1)} %get-tuple-element.73), channel_id=1, source_target_pairs={{0,1},{1,0},{10,11},{11,10},{20,21},{21,20},{30,31},{31,30}} | collective-permute-start | bytes 430088 | tf_op jit(solution)/shard_map/ppermute | solution.py:168
  11.8 20.2 %collective-permute-start = (bf16[2,128,1280]{2,1,0:T(8,128)(2,1)}, bf16[2,128,1280]{2,1,0:T(8,128)(2,1)S(1)}, u32[]{:S(2)}, u32[]{:S(2)}) collective-permute-start(bf16[2,128,1280]{2,1,0:T(8,128)(2,1)} %bitcast.108), channel_id=1, source_target_pairs={{0,1},{1,0},{2,3},{3,2},{4,5},{5,4},{6,7},{7,6},{8,9},{9,8},{10,11... | collective-permute-start | bytes 1966088 | tf_op jit(solution)/shard_map/ppermute | solution.py:168
  16.9 7.3 %collective-permute-start.25 = (bf16[2,1,112,640]{3,2,1,0:T(8,128)(2,1)S(1)}, bf16[2,1,112,640]{3,2,1,0:T(8,128)(2,1)S(1)}, u32[]{:S(2)}, u32[]{:S(2)}) collective-permute-start(bf16[2,1,112,640]{3,2,1,0:T(8,128)(2,1)S(1)} %pad_maximum_fusion.6), channel_id=1, source_target_pairs={{0,16},{1,17},{10,26},{11,27},{20,4},{21,5},{30,14},{31,15}} | collective-permute-start | bytes 860168 | tf_op jit(solution)/shard_map/ppermute | solution.py:168
  19.9 12.1 %copy-start.1 = (bf16[1,2,128,1280]{3,2,1,0:T(8,128)(2,1)S(1)}, bf16[1,2,128,1280]{3,2,1,0:T(8,128)(2,1)}, u32[]{:S(2)}) copy-start(bf16[1,2,128,1280]{3,2,1,0:T(8,128)(2,1)} %param.13) | copy-start | bytes 1966084
  24.1 16.6 %collective-permute-start.9 = (bf16[1280,256]{1,0:T(8,128)(2,1)}, bf16[1280,256]{1,0:T(8,128)(2,1)S(1)}, u32[]{:S(2)}, u32[]{:S(2)}) collective-permute-start(bf16[1280,256]{1,0:T(8,128)(2,1)} %bitcast.148), channel_id=1, source_target_pairs={{0,1},{1,0},{2,3},{3,2},{4,5},{5,4},{6,7},{7,6},{8,9},{9,8},{10,11... | collective-permute-start | bytes 1966088 | tf_op jit(solution)/shard_map/ppermute | solution.py:168
  25.8 17.1 %collective-permute-start.26 = (bf16[2,1,112,640]{3,2,1,0:T(8,128)(2,1)S(1)}, bf16[2,1,112,640]{3,2,1,0:T(8,128)(2,1)S(1)}, u32[]{:S(2)}, u32[]{:S(2)}) collective-permute-start(bf16[2,1,112,640]{3,2,1,0:T(8,128)(2,1)S(1)} %broadcast_select_fusion.5), channel_id=1, source_target_pairs={{0,8},{16,24},{1,9},{17,25},{10,2},{26,18},{11,3},{27,19},{20,28},... | collective-permute-start | bytes 860168 | tf_op jit(solution)/shard_map/ppermute | solution.py:168
  32.0 31.3 %collective-permute-start.6 = (bf16[2,128,1280]{2,1,0:T(8,128)(2,1)S(1)}, bf16[2,128,1280]{2,1,0:T(8,128)(2,1)}, u32[]{:S(2)}, u32[]{:S(2)}) collective-permute-start(bf16[2,128,1280]{2,1,0:T(8,128)(2,1)S(1)} %bitcast.109), channel_id=1, source_target_pairs={{2,4},{3,5},{4,2},{5,3},{10,12},{11,13},{12,10},{13,11},{18,20},{1... | collective-permute-start | bytes 1966088 | tf_op jit(solution)/shard_map/ppermute | solution.py:168
  33.7 11.6 %collective-permute-start.8 = (bf16[3,112,640]{2,1,0:T(8,128)(2,1)S(1)}, bf16[3,112,640]{2,1,0:T(8,128)(2,1)S(1)}, u32[]{:S(2)}, u32[]{:S(2)}) collective-permute-start(bf16[3,112,640]{2,1,0:T(8,128)(2,1)S(1)} %get-tuple-element.65), channel_id=1, source_target_pairs={{0,1},{1,0},{10,11},{11,10},{20,21},{21,20},{30,31},{31,30}} | collective-permute-start | bytes 1290248 | tf_op jit(solution)/shard_map/ppermute | solution.py:168
  37.2 10.6 %collective-permute-start.15 = (bf16[3,112,640]{2,1,0:T(8,128)(2,1)S(1)}, bf16[3,112,640]{2,1,0:T(8,128)(2,1)S(1)}, u32[]{:S(2)}, u32[]{:S(2)}) collective-permute-start(bf16[3,112,640]{2,1,0:T(8,128)(2,1)S(1)} %get-tuple-element.64), channel_id=1, source_target_pairs={{0,16},{1,17},{10,26},{11,27},{20,4},{21,5},{30,14},{31,15}} | collective-permute-start | bytes 1290248 | tf_op jit(solution)/shard_map/ppermute | solution.py:168
  39.6 2.6 %copy-start.18 = (bf16[1,1280,256]{2,1,0:T(8,128)(2,1)S(1)}, bf16[1,1280,256]{2,1,0:T(8,128)(2,1)}, u32[]{:S(2)}) copy-start(bf16[1,1280,256]{2,1,0:T(8,128)(2,1)} %param.12) | copy-start | bytes 1966084
  40.7 34.1 %collective-permute-start.4 = (bf16[2,2,128,1280]{3,2,1,0:T(8,128)(2,1)}, bf16[2,2,128,1280]{3,2,1,0:T(8,128)(2,1)}, u32[]{:S(2)}, u32[]{:S(2)}) collective-permute-start(bf16[2,2,128,1280]{3,2,1,0:T(8,128)(2,1)} %pad_maximum_fusion), channel_id=1, source_target_pairs={{0,2},{1,3},{2,0},{3,1},{4,6},{5,7},{6,4},{7,5},{8,10},{9,11},{10,... | collective-permute-start | bytes 3932168 | tf_op jit(solution)/shard_map/ppermute | solution.py:168
  42.2 3.3 %copy-start.11 = (bf16[80,8,2,1280]{3,1,2,0:T(8,128)(2,1)S(1)}, bf16[80,8,2,1280]{3,1,2,0:T(8,128)(2,1)}, u32[]{:S(2)}) copy-start(bf16[80,8,2,1280]{3,1,2,0:T(8,128)(2,1)} %copy.44) | copy-start | bytes 9830404
  45.4 3.7 %collective-permute-start.10 = (f32[232,512]{1,0:T(8,128)S(1)}, f32[232,512]{1,0:T(8,128)S(1)}, u32[]{:S(2)}, u32[]{:S(2)}) collective-permute-start(f32[232,512]{1,0:T(8,128)S(1)} %pad_maximum_fusion.4), channel_id=1, source_target_pairs={{0,8},{1,9},{2,10},{3,11},{4,12},{5,13},{6,14},{7,15},{8,0},{9,1},... | collective-permute-start | bytes 1425416 | tf_op jit(solution)/shard_map/ppermute | solution.py:168
  46.2 15.4 %collective-permute-start.27 = (bf16[112,2560]{1,0:T(8,128)(2,1)S(1)}, bf16[112,2560]{1,0:T(8,128)(2,1)S(1)}, u32[]{:S(2)}, u32[]{:S(2)}) collective-permute-start(bf16[112,2560]{1,0:T(8,128)(2,1)S(1)} %convolution_convert_fusion.2), channel_id=1, source_target_pairs={{0,1},{1,0},{2,3},{3,2},{4,5},{5,4},{6,7},{7,6},{8,9},{9,8},{10,11... | collective-permute-start | bytes 1720328 | tf_op jit(solution)/shard_map/ppermute | solution.py:168
  47.7 8.8 %collective-permute-start.16 = (bf16[3,112,640]{2,1,0:T(8,128)(2,1)S(1)}, bf16[3,112,640]{2,1,0:T(8,128)(2,1)S(1)}, u32[]{:S(2)}, u32[]{:S(2)}) collective-permute-start(bf16[3,112,640]{2,1,0:T(8,128)(2,1)S(1)} %collective-permute-done.8), channel_id=1, source_target_pairs={{0,16},{1,17},{10,26},{11,27},{20,4},{21,5},{30,14},{31,15}} | collective-permute-start | bytes 1290248 | tf_op jit(solution)/shard_map/ppermute | solution.py:168
  49.2 9.9 %collective-permute-start.11 = (f32[120,512]{1,0:T(8,128)S(1)}, f32[120,512]{1,0:T(8,128)S(1)}, u32[]{:S(2)}, u32[]{:S(2)}) collective-permute-start(f32[120,512]{1,0:T(8,128)S(1)} %pad_maximum_fusion.7), channel_id=1, source_target_pairs={{0,16},{1,17},{2,18},{3,19},{4,20},{5,21},{6,22},{7,23},{8,24},{9,... | collective-permute-start | bytes 737288 | tf_op jit(solution)/shard_map/ppermute | solution.py:168
  59.2 17.8 %collective-permute-start.17 = (bf16[2,3,112,640]{3,2,1,0:T(8,128)(2,1)}, bf16[2,3,112,640]{3,2,1,0:T(8,128)(2,1)}, u32[]{:S(2)}, u32[]{:S(2)}) collective-permute-start(bf16[2,3,112,640]{3,2,1,0:T(8,128)(2,1)} %pad_maximum_fusion.3), channel_id=1, source_target_pairs={{0,8},{16,24},{1,9},{17,25},{10,2},{26,18},{11,3},{27,19},{20,28},... | collective-permute-start | bytes 2580488 | tf_op jit(solution)/shard_map/ppermute | solution.py:168
  63.3 28.3 %collective-permute-start.7 = (bf16[2,128,1280]{2,1,0:T(8,128)(2,1)}, bf16[2,128,1280]{2,1,0:T(8,128)(2,1)}, u32[]{:S(2)}, u32[]{:S(2)}) collective-permute-start(bf16[2,128,1280]{2,1,0:T(8,128)(2,1)} %collective-permute-done.6), channel_id=1, source_target_pairs={{2,0},{3,1},{4,6},{5,7},{10,8},{11,9},{12,14},{13,15},{18,16},{19,... | collective-permute-start | bytes 1966088 | tf_op jit(solution)/shard_map/ppermute | solution.py:168
  64.6 16.4 %collective-permute-start.14 = (bf16[112,512]{1,0:T(8,128)(2,1)S(1)}, bf16[112,512]{1,0:T(8,128)(2,1)S(1)}, u32[]{:S(2)}, u32[]{:S(2)}) collective-permute-start(bf16[112,512]{1,0:T(8,128)(2,1)S(1)} %fusion.11), channel_id=1, source_target_pairs={{6,0},{7,1},{12,10},{13,11},{18,20},{19,21},{24,30},{25,31}} | collective-permute-start | bytes 344072 | tf_op jit(solution)/shard_map/ppermute | solution.py:168
  65.9 17.1 %collective-permute-start.13 = (bf16[112,512]{1,0:T(8,128)(2,1)S(1)}, bf16[112,512]{1,0:T(8,128)(2,1)S(1)}, u32[]{:S(2)}, u32[]{:S(2)}) collective-permute-start(bf16[112,512]{1,0:T(8,128)(2,1)S(1)} %fusion.11), channel_id=1, source_target_pairs={{4,0},{5,1},{14,10},{15,11},{16,20},{17,21},{26,30},{27,31}} | collective-permute-start | bytes 344072 | tf_op jit(solution)/shard_map/ppermute | solution.py:168
  67.3 85.1 %copy-start = (f32[112,1]{1,0:T(8,128)}, f32[112,1]{1,0:T(8,128)S(1)}, u32[]{:S(2)}) copy-start(f32[112,1]{1,0:T(8,128)S(1)} %copy.33.scale_ref.refs_13_) | copy-start | bytes 1348
  74.8 3.5 %copy-start.12 = (bf16[80,8,2,1280]{3,1,2,0:T(8,128)(2,1)S(1)}, bf16[80,8,2,1280]{3,1,2,0:T(8,128)(2,1)}, u32[]{:S(2)}) copy-start(bf16[80,8,2,1280]{3,1,2,0:T(8,128)(2,1)} %copy.44) | copy-start | bytes 9830404
  76.3 15.3 %collective-permute-start.5 = (bf16[2,128,1280]{2,1,0:T(8,128)(2,1)S(1)}, bf16[2,128,1280]{2,1,0:T(8,128)(2,1)S(1)}, u32[]{:S(2)}, u32[]{:S(2)}) collective-permute-start(bf16[2,128,1280]{2,1,0:T(8,128)(2,1)S(1)} %get-tuple-element.61.up_ref), channel_id=1, source_target_pairs={{2,4},{3,5},{4,2},{5,3},{10,12},{11,13},{12,10},{13,11},{18,20},{1... | collective-permute-start | bytes 1966088 | tf_op jit(solution)/shard_map/ppermute | solution.py:168
  79.0 15.9 %collective-permute-start.18 = (bf16[112,2560]{1,0:T(8,128)(2,1)S(1)}, bf16[112,2560]{1,0:T(8,128)(2,1)S(1)}, u32[]{:S(2)}, u32[]{:S(2)}) collective-permute-start(bf16[112,2560]{1,0:T(8,128)(2,1)S(1)} %convolution_convert_fusion.3), channel_id=1, source_target_pairs={{0,1},{1,0},{2,3},{3,2},{4,5},{5,4},{6,7},{7,6},{8,9},{9,8},{10,11... | collective-permute-start | bytes 1720328 | tf_op jit(solution)/shard_map/ppermute | solution.py:168
  81.0 41.2 %copy-start.13 = (bf16[112,512]{1,0:T(8,128)(2,1)}, bf16[112,512]{1,0:T(8,128)(2,1)S(1)}, u32[]{:S(2)}) copy-start(bf16[112,512]{1,0:T(8,128)(2,1)S(1)} %collective-permute-done.14) | copy-start | bytes 344068
  81.0 9.1 %collective-permute-start.12 = (bf16[112,512]{1,0:T(8,128)(2,1)S(1)}, bf16[112,512]{1,0:T(8,128)(2,1)S(1)}, u32[]{:S(2)}, u32[]{:S(2)}) collective-permute-start(bf16[112,512]{1,0:T(8,128)(2,1)S(1)} %fusion.11), channel_id=1, source_target_pairs={{2,0},{3,1},{8,10},{9,11},{22,20},{23,21},{28,30},{29,31}} | collective-permute-start | bytes 344072 | tf_op jit(solution)/shard_map/ppermute | solution.py:168
  83.0 39.3 %copy-start.15 = (bf16[112,512]{1,0:T(8,128)(2,1)}, bf16[112,512]{1,0:T(8,128)(2,1)S(1)}, u32[]{:S(2)}) copy-start(bf16[112,512]{1,0:T(8,128)(2,1)S(1)} %collective-permute-done.13) | copy-start | bytes 344068
  83.0 24.2 %collective-permute-start.29 = (bf16[112,2560]{1,0:T(8,128)(2,1)S(1)}, bf16[112,2560]{1,0:T(8,128)(2,1)S(1)}, u32[]{:S(2)}, u32[]{:S(2)}) collective-permute-start(bf16[112,2560]{1,0:T(8,128)(2,1)S(1)} %convolution_convert_fusion.1), channel_id=1, source_target_pairs={{0,1},{1,0},{2,3},{3,2},{4,5},{5,4},{6,7},{7,6},{8,9},{9,8},{10,11... | collective-permute-start | bytes 1720328 | tf_op jit(solution)/shard_map/ppermute | solution.py:168
  90.1 28.1 %collective-permute-start.31 = (bf16[112,2560]{1,0:T(8,128)(2,1)S(1)}, bf16[112,2560]{1,0:T(8,128)(2,1)S(1)}, u32[]{:S(2)}, u32[]{:S(2)}) collective-permute-start(bf16[112,2560]{1,0:T(8,128)(2,1)S(1)} %convolution_convert_fusion), channel_id=1, source_target_pairs={{0,1},{1,0},{2,3},{3,2},{4,5},{5,4},{6,7},{7,6},{8,9},{9,8},{10,11... | collective-permute-start | bytes 1720328 | tf_op jit(solution)/shard_map/ppermute | solution.py:168
  96.9 31.8 %collective-permute-start.22 = (bf16[2,128,1280]{2,1,0:T(8,128)(2,1)S(1)}, bf16[2,128,1280]{2,1,0:T(8,128)(2,1)S(1)}, u32[]{:S(2)}, u32[]{:S(2)}) collective-permute-start(bf16[2,128,1280]{2,1,0:T(8,128)(2,1)S(1)} %collective-permute-done.5), channel_id=1, source_target_pairs={{2,0},{3,1},{4,6},{5,7},{10,8},{11,9},{12,14},{13,15},{18,16},{19,... | collective-permute-start | bytes 1966088 | tf_op jit(solution)/shard_map/ppermute | solution.py:168
  98.3 23.2 %collective-permute-start.19 = (bf16[4,112,512]{2,1,0:T(8,128)(2,1)S(1)}, bf16[4,112,512]{2,1,0:T(8,128)(2,1)S(1)}, u32[]{:S(2)}, u32[]{:S(2)}) collective-permute-start(bf16[4,112,512]{2,1,0:T(8,128)(2,1)S(1)} %pad_maximum_fusion.5), channel_id=1, source_target_pairs={{0,16},{1,17},{10,26},{11,27},{20,4},{21,5},{30,14},{31,15}} | collective-permute-start | bytes 1376264 | tf_op jit(solution)/shard_map/ppermute | solution.py:168
  102.6 50.8 %collective-permute-start.28 = (bf16[112,2560]{1,0:T(8,128)(2,1)}, bf16[112,2560]{1,0:T(8,128)(2,1)}, u32[]{:S(2)}, u32[]{:S(2)}) collective-permute-start(bf16[112,2560]{1,0:T(8,128)(2,1)} %fusion), channel_id=1, source_target_pairs={{0,6},{1,7},{2,4},{3,5},{4,2},{5,3},{6,0},{7,1},{8,14},{9,15},{10,... | collective-permute-start | bytes 1720328 | tf_op jit(solution)/shard_map/ppermute | solution.py:168
  108.7 44.7 %collective-permute-start.30 = (bf16[112,2560]{1,0:T(8,128)(2,1)}, bf16[112,2560]{1,0:T(8,128)(2,1)}, u32[]{:S(2)}, u32[]{:S(2)}) collective-permute-start(bf16[112,2560]{1,0:T(8,128)(2,1)} %fusion.1), channel_id=1, source_target_pairs={{0,4},{1,5},{2,6},{3,7},{4,0},{5,1},{6,2},{7,3},{8,12},{9,13},{10,... | collective-permute-start | bytes 1720328 | tf_op jit(solution)/shard_map/ppermute | solution.py:168
  119.8 33.6 %collective-permute-start.32 = (bf16[112,2560]{1,0:T(8,128)(2,1)}, bf16[112,2560]{1,0:T(8,128)(2,1)}, u32[]{:S(2)}, u32[]{:S(2)}) collective-permute-start(bf16[112,2560]{1,0:T(8,128)(2,1)} %fusion.2), channel_id=1, source_target_pairs={{0,2},{1,3},{2,0},{3,1},{4,6},{5,7},{6,4},{7,5},{8,10},{9,11},{10,... | collective-permute-start | bytes 1720328 | tf_op jit(solution)/shard_map/ppermute | solution.py:168
  121.5 17.9 %collective-permute-start.21 = (bf16[2,128,1280]{2,1,0:T(8,128)(2,1)}, bf16[2,128,1280]{2,1,0:T(8,128)(2,1)}, u32[]{:S(2)}, u32[]{:S(2)}) collective-permute-start(bf16[2,128,1280]{2,1,0:T(8,128)(2,1)} %broadcast_select_fusion.2.up_ref), channel_id=1, source_target_pairs={{0,1},{1,0},{2,3},{3,2},{4,5},{5,4},{6,7},{7,6},{8,9},{9,8},{10,11... | collective-permute-start | bytes 1966088 | tf_op jit(solution)/shard_map/ppermute | solution.py:168
  122.3 10.4 %copy-start.14 = (bf16[112,512]{1,0:T(8,128)(2,1)S(1)}, bf16[112,512]{1,0:T(8,128)(2,1)}, u32[]{:S(2)}) copy-start(bf16[112,512]{1,0:T(8,128)(2,1)} %copy-done.13) | copy-start | bytes 344068
  122.3 10.4 %copy-start.16 = (bf16[112,512]{1,0:T(8,128)(2,1)S(1)}, bf16[112,512]{1,0:T(8,128)(2,1)}, u32[]{:S(2)}) copy-start(bf16[112,512]{1,0:T(8,128)(2,1)} %copy-done.15) | copy-start | bytes 344068
  128.7 2.7 %collective-permute-start.20 = (bf16[4,112,512]{2,1,0:T(8,128)(2,1)S(1)}, bf16[4,112,512]{2,1,0:T(8,128)(2,1)S(1)}, u32[]{:S(2)}, u32[]{:S(2)}) collective-permute-start(bf16[4,112,512]{2,1,0:T(8,128)(2,1)S(1)} %broadcast_select_fusion.3), channel_id=1, source_target_pairs={{0,8},{16,24},{1,9},{17,25},{10,2},{26,18},{11,3},{27,19},{20,28},... | collective-permute-start | bytes 1376264 | tf_op jit(solution)/shard_map/ppermute | solution.py:168
  131.5 17.4 %collective-permute-start.33 = (bf16[1,128,1280]{2,1,0:T(8,128)(2,1)}, bf16[1,128,1280]{2,1,0:T(8,128)(2,1)}, u32[]{:S(2)}, u32[]{:S(2)}) collective-permute-start(bf16[1,128,1280]{2,1,0:T(8,128)(2,1)} %get-tuple-element.66), channel_id=1, source_target_pairs={{0,1},{1,0},{2,3},{3,2},{4,5},{5,4},{6,7},{7,6},{8,9},{9,8},{10,11... | collective-permute-start | bytes 983048 | tf_op jit(solution)/shard_map/ppermute | solution.py:168
  136.7 2.7 %copy-start.17 = (bf16[1,128,1280]{2,1,0:T(8,128)(2,1)S(1)}, bf16[1,128,1280]{2,1,0:T(8,128)(2,1)}, u32[]{:S(2)}) copy-start(bf16[1,128,1280]{2,1,0:T(8,128)(2,1)} %get-tuple-element.67) | copy-start | bytes 983044
  139.4 13.1 %collective-permute-start.23 = (bf16[1,128,1280]{2,1,0:T(8,128)(2,1)S(1)}, bf16[1,128,1280]{2,1,0:T(8,128)(2,1)S(1)}, u32[]{:S(2)}, u32[]{:S(2)}) collective-permute-start(bf16[1,128,1280]{2,1,0:T(8,128)(2,1)S(1)} %copy-done.17), channel_id=1, source_target_pairs={{0,1},{1,0},{2,3},{3,2},{4,5},{5,4},{6,7},{7,6},{8,9},{9,8},{10,11... | collective-permute-start | bytes 983048 | tf_op jit(solution)/shard_map/ppermute | solution.py:168
  143.1 0.9 copy-start.3
  145.8 1.1 copy-start.5
  147.1 5.6 %copy-start.7 = (bf16[112,2560]{1,0:T(8,128)(2,1)}, bf16[112,2560]{1,0:T(8,128)(2,1)S(1)}, u32[]{:S(2)}) copy-start(bf16[112,2560]{1,0:T(8,128)(2,1)S(1)} %shard_map.107.refs_3_) | copy-start | bytes 1720324
  148.8 4.6 %copy-start.8 = (bf16[112,2560]{1,0:T(8,128)(2,1)}, bf16[112,2560]{1,0:T(8,128)(2,1)S(1)}, u32[]{:S(2)}) copy-start(bf16[112,2560]{1,0:T(8,128)(2,1)S(1)} %shard_map.109.refs_5_) | copy-start | bytes 1720324
  (5 other events, 3.9 us)
